TPU v7x, 256 devices: a whole 4x4x8 slice. The times are simulated.
256 devices in a mesh: dp: 32 (over z_hi, x, core), mp: 8 (over y, z_lo).
Axes of the slice: x: 4, y: 4, z: 8 (z_hi: 4, z_lo: 2; z = z_hi * 2 + z_lo), core: 2. Of those that a mesh axis runs over, the one named last changes fastest.
Arguments:
- tokens: bfloat16 [4096, 8192], P('dp'), may hold values from -6 to 6
- cotangent: bfloat16 [4096, 8192], P('dp'), may hold values from -1.1953125 to 1.1953125
- gate_weight: bfloat16 [112, 5, 128, 128], P('mp', None, 'dp'), may hold values from -0.3125 to 0.3125
- up_weight: bfloat16 [112, 5, 128, 128], P('mp', None, 'dp'), may hold values from -0.3125 to 0.3125
- down_weight: bfloat16 [112, 5, 128, 128], P('mp', None, 'dp'), may hold values from -0.25 to 0.25
- low_in: bfloat16 [8192, 64], P('dp'), may hold values from -0.0625 to 0.0625
- low_mid: bfloat16 [128, 14336], P('dp', 'mp'), may hold values from -0.75 to 0.75
- down_low_in: bfloat16 [64, 14336], P('dp', 'mp'), may hold values from -0.046875 to 0.046875
- down_low_out: bfloat16 [64, 8192], P('dp', 'mp'), may hold values from -0.75 to 0.75
- up_order: int32 [112], replicated, may hold values from 0 to 111, as said below
- down_order: int32 [112], replicated, may hold values from 0 to 111, as said below
- up_rows: int32 [112, 5], replicated, may hold values from 0 to 63, as said below
- down_cols: int32 [112, 5], replicated, may hold values from 0 to 63, as said below
- up_count: int32 [112], replicated, may hold values from 1 to 5, as said below
- down_count: int32 [112], replicated, may hold values from 1 to 5, as said below
Outputs:
- layer_out: bfloat16 [4096, 8192], P('dp', 'mp')
- token_grad: bfloat16 [4096, 8192], P('dp', 'mp')
- gate_weight_grad: bfloat16 [112, 5, 128, 128], P('mp', None, 'dp')
- up_weight_grad: bfloat16 [112, 5, 128, 128], P('mp', None, 'dp')
- down_weight_grad: bfloat16 [112, 5, 128, 128], P('mp', None, 'dp')
- low_in_grad: bfloat16 [8192, 64], P('dp')
- low_mid_grad: bfloat16 [128, 14336], P('dp', 'mp')
- down_low_in_grad: bfloat16 [64, 14336], P('dp', 'mp')
- down_low_out_grad: bfloat16 [64, 8192], P('dp', 'mp')
Inputs may be any that keep to these rules, and one draw needn't show every extreme that they name: up_order is a permutation of the hidden blocks. Slots g * 14 to (g + 1) * 14 - 1 form slot group g. down_order is a permutation of the hidden blocks. For any slot group a of up_order and slot group b of down_order, at most 2 hidden blocks lie in both, and some pair of groups shares exactly 2. `up_rows`: the 5 entries of a slot are distinct; only the first up_count[s] are used. `down_cols`: the 5 entries of a slot are distinct; only the first down_count[t] are used. `up_count`: the counts of every slot group of 14 consecutive slots add up to exactly 42. `down_count`: the counts of every slot group of 14 consecutive slots add up to exactly 42.
All inputs are finite; a program needn't handle non-finite values.
Results may differ from a plain program's by a relative error of at most 0.035.
Values may be sent and summed in bfloat16 or wider, within the bound.
No kernel may reach another device: no remote copies, remote signals or barrier semaphores. Data moves between devices by JAX's collectives and lax.ppermute only.
A program may use at most 128 MiB of HBM per device.

v0:
```python
import jax
import jax.numpy as jnp
from jax import lax
from jax.sharding import PartitionSpec as P


def lookup(table_ids, positions):
    span_ids = jnp.arange(table_ids.shape[0], dtype=jnp.int32)
    matches = positions[..., None] == span_ids
    return jnp.sum(jnp.where(matches, table_ids, 0), axis=-1)


def own_rows(table_ids, my_index, slot_count):
    return lax.dynamic_slice_in_dim(table_ids, my_index * slot_count, slot_count, 0)


def live_mask(count_rows, block_depth):
    return jnp.arange(block_depth, dtype=jnp.int32)[None, :] < count_rows[:, None]


def flat_blocks(weight):
    return weight.reshape(weight.shape[0] * weight.shape[1], weight.shape[2], weight.shape[3])


def keep_blocks(store, keep):
    return jnp.where(keep[:, None, None] > 0.5, store, jnp.zeros((), store.dtype))


def place_blocks(gradient, chosen, slot_count, block_depth):
    zeros_buffer = jnp.zeros((slot_count * block_depth,) + gradient.shape[1:], gradient.dtype)
    return (
        zeros_buffer.at[chosen]
        .set(gradient)
        .reshape((slot_count, block_depth) + gradient.shape[1:])
    )


def inverse_of(order_ids):
    span_ids = jnp.arange(order_ids.shape[0], dtype=jnp.int32)
    return jnp.sum(jnp.where(order_ids[None, :] == span_ids[:, None], span_ids[None, :], 0), axis=1)


def send_table(owner_dev, peer_dev, lane_rank, local_slot, my_index, lane_count, capacity):
    lane_ids = jnp.arange(lane_count, dtype=jnp.int32)
    target = peer_dev * capacity + lane_rank
    matched = (owner_dev[None, :] == my_index) & (target[None, :] == lane_ids[:, None])
    chosen = jnp.sum(jnp.where(matched, local_slot[None, :], 0), axis=1)
    return (chosen, jnp.any(matched, axis=1))


def relayout(blocks, chosen, present, arrival, groups, capacity):
    flags = present.reshape((-1,) + (1,) * (blocks.ndim - 1))
    parcel = jnp.where(flags, blocks[chosen], jnp.zeros((), blocks.dtype))
    parcel = parcel.reshape((groups, capacity) + blocks.shape[1:])
    arrived = lax.all_to_all(parcel, "mp", split_axis=0, concat_axis=0, tiled=True)
    return arrived.reshape((groups * capacity,) + blocks.shape[1:])[arrival]


def column_total(partial_value):
    return lax.psum_scatter(
        partial_value.astype(jnp.bfloat16), "mp", scatter_dimension=0, tiled=True
    ).astype(jnp.float32)


def rank_total(partial_value):
    return lax.psum(partial_value.astype(jnp.bfloat16), "mp").astype(jnp.float32)


def segment_total(products, segment_ids, segment_count):
    return jax.ops.segment_sum(products, segment_ids, num_segments=segment_count)


def slot_total(products, slot_count):
    return jnp.sum(products.reshape((slot_count, -1) + products.shape[1:]), axis=1)


def slot_pick(values, block_depth):
    spread = jnp.broadcast_to(values[:, None], (values.shape[0], block_depth) + values.shape[1:])
    return spread.reshape((values.shape[0] * block_depth,) + values.shape[1:])


def local(
    tokens,
    cotangent,
    gate_weight,
    up_weight,
    down_weight,
    low_in,
    low_mid,
    down_low_in,
    down_low_out,
    up_order,
    down_order,
    up_rows,
    down_cols,
    up_count,
    down_count,
):
    groups = lax.axis_size("mp")
    my_index = lax.axis_index("mp")
    slot_count, block_depth, shard_rows, block_width = gate_weight.shape
    tok_rows, model_width = tokens.shape
    block_count = model_width // block_width
    column_share = model_width // groups
    rank_width = low_in.shape[1]
    capacity = (slot_count + groups - 1) // groups
    lane_count = groups * capacity
    full_depth = slot_count * block_depth
    slot_ids = jnp.arange(up_order.shape[0], dtype=jnp.int32)
    up_where = inverse_of(up_order)
    down_where = inverse_of(down_order)
    source = lookup(up_where, down_order)
    from_device = source // slot_count
    to_device = slot_ids // slot_count
    earlier = (
        (from_device[None, :] == from_device[:, None])
        & (to_device[None, :] == to_device[:, None])
        & (slot_ids[None, :] < slot_ids[:, None])
    )
    lane_rank = jnp.sum(earlier.astype(jnp.int32), axis=1)
    ahead_chosen, ahead_present = send_table(
        from_device, to_device, lane_rank, source % slot_count, my_index, lane_count, capacity
    )
    ahead_arrival = own_rows(from_device * capacity + lane_rank, my_index, slot_count)
    back_chosen, back_present = send_table(
        to_device, from_device, lane_rank, slot_ids % slot_count, my_index, lane_count, capacity
    )
    my_blocks_down = lookup(down_where, own_rows(up_order, my_index, slot_count))
    back_arrival = lookup(to_device * capacity + lane_rank, my_blocks_down)
    up_rows_mine = own_rows(up_rows, my_index, slot_count)
    up_count_mine = own_rows(up_count, my_index, slot_count)
    down_cols_mine = own_rows(down_cols, my_index, slot_count)
    down_count_mine = own_rows(down_count, my_index, slot_count)
    down_chosen = jnp.arange(full_depth, dtype=jnp.int32)
    down_keep = live_mask(down_count_mine, block_depth).reshape(-1).astype(jnp.float32)
    down_store = keep_blocks(flat_blocks(down_weight), down_keep)
    up_chosen = jnp.arange(full_depth, dtype=jnp.int32)
    up_keep = live_mask(up_count_mine, block_depth).reshape(-1).astype(jnp.float32)
    gate_store = keep_blocks(flat_blocks(gate_weight), up_keep)
    up_store = keep_blocks(flat_blocks(up_weight), up_keep)
    gate_all, up_all, down_all, in_all, mid_all, back_in_all, back_out_all = (
        lax.all_gather(gate_store, "dp", axis=1, tiled=True),
        lax.all_gather(up_store, "dp", axis=1, tiled=True),
        lax.all_gather(down_store, "dp", axis=1, tiled=True),
        lax.all_gather(low_in, "dp", axis=0, tiled=True),
        lax.all_gather(low_mid, "dp", axis=0, tiled=True),
        lax.all_gather(down_low_in, "dp", axis=0, tiled=True),
        lax.all_gather(down_low_out, "dp", axis=0, tiled=True),
    )
    up_block = lookup(up_rows_mine.reshape(-1), up_chosen)
    down_block = lookup(down_cols_mine.reshape(-1), down_chosen)
    token_picked = tokens.reshape(tok_rows, block_count, block_width)[:, up_block, :]
    latent = jnp.dot(tokens, in_all, preferred_element_type=jnp.float32).astype(jnp.bfloat16)
    mid_gate = mid_all[:rank_width].reshape(rank_width, slot_count, block_width)
    mid_up = mid_all[rank_width:].reshape(rank_width, slot_count, block_width)
    gate_pre = slot_total(
        jnp.einsum("tlr,lrc->ltc", token_picked, gate_all, preferred_element_type=jnp.float32),
        slot_count,
    )
    gate_pre = gate_pre + jnp.einsum(
        "tr,rsc->stc", latent, mid_gate, preferred_element_type=jnp.float32
    )
    up_pre = slot_total(
        jnp.einsum("tlr,lrc->ltc", token_picked, up_all, preferred_element_type=jnp.float32),
        slot_count,
    )
    up_pre = up_pre + jnp.einsum("tr,rsc->stc", latent, mid_up, preferred_element_type=jnp.float32)
    sigmoid_gate = jax.nn.sigmoid(gate_pre)
    active = gate_pre * sigmoid_gate
    hidden = (active * up_pre).astype(jnp.bfloat16)
    hidden_down = relayout(hidden, ahead_chosen, ahead_present, ahead_arrival, groups, capacity)
    back_in_slots = back_in_all.reshape(rank_width, slot_count, block_width)
    latent_down = rank_total(
        jnp.einsum("sth,rsh->tr", hidden_down, back_in_slots, preferred_element_type=jnp.float32)
    ).astype(jnp.bfloat16)
    hidden_picked = slot_pick(hidden_down, block_depth)
    out_partial = segment_total(
        jnp.einsum("lth,lhc->ltc", hidden_picked, down_all, preferred_element_type=jnp.float32),
        down_block,
        block_count,
    )
    out_share = column_total(out_partial)
    layer_out = out_share.transpose(1, 0, 2).reshape(tok_rows, column_share)
    layer_out = (
        layer_out + jnp.dot(latent_down, back_out_all, preferred_element_type=jnp.float32)
    ).astype(jnp.bfloat16)
    grad_cols = lax.dynamic_slice_in_dim(cotangent, my_index * column_share, column_share, 1)
    back_latent = rank_total(
        jnp.einsum("td,rd->tr", grad_cols, back_out_all, preferred_element_type=jnp.float32)
    ).astype(jnp.bfloat16)
    grad_picked = cotangent.reshape(tok_rows, block_count, block_width)[:, down_block, :]
    hidden_grad = slot_total(
        jnp.einsum("tlc,lhc->lth", grad_picked, down_all, preferred_element_type=jnp.float32),
        slot_count,
    )
    hidden_grad = (
        hidden_grad
        + jnp.einsum("tr,rsh->sth", back_latent, back_in_slots, preferred_element_type=jnp.float32)
    ).astype(jnp.bfloat16)
    hidden_grad_up = relayout(
        hidden_grad, back_chosen, back_present, back_arrival, groups, capacity
    )
    flowing = hidden_grad_up.astype(jnp.float32)
    gate_grad = (flowing * up_pre * sigmoid_gate * (1.0 + gate_pre * (1.0 - sigmoid_gate))).astype(
        jnp.bfloat16
    )
    up_grad = (flowing * active).astype(jnp.bfloat16)
    latent_sum = jnp.einsum(
        "stc,rsc->tr", gate_grad, mid_gate, preferred_element_type=jnp.float32
    ) + jnp.einsum("stc,rsc->tr", up_grad, mid_up, preferred_element_type=jnp.float32)
    latent_grad = rank_total(latent_sum).astype(jnp.bfloat16)
    gate_picked = slot_pick(gate_grad, block_depth)
    up_picked = slot_pick(up_grad, block_depth)
    input_terms = jnp.einsum(
        "ltc,lrc->ltr", gate_picked, gate_all, preferred_element_type=jnp.float32
    ) + jnp.einsum("ltc,lrc->ltr", up_picked, up_all, preferred_element_type=jnp.float32)
    input_partial = segment_total(input_terms, up_block, block_count)
    input_share = column_total(input_partial)
    in_cols = lax.dynamic_slice_in_dim(in_all, my_index * column_share, column_share, 0)
    token_grad = input_share.transpose(1, 0, 2).reshape(tok_rows, column_share)
    token_grad = (
        token_grad
        + jnp.einsum("tr,dr->td", latent_grad, in_cols, preferred_element_type=jnp.float32)
    ).astype(jnp.bfloat16)
    gate_wgrad = jnp.einsum(
        "tlr,ltc->lrc", token_picked, gate_picked, preferred_element_type=jnp.float32
    )
    up_wgrad = jnp.einsum(
        "tlr,ltc->lrc", token_picked, up_picked, preferred_element_type=jnp.float32
    )
    down_wgrad = jnp.einsum(
        "lth,tlc->lhc", hidden_picked, grad_picked, preferred_element_type=jnp.float32
    )
    in_grad = jnp.einsum("td,tr->dr", tokens, latent_grad, preferred_element_type=jnp.float32)
    mid_grad = jnp.concatenate(
        [
            jnp.einsum("tr,stc->rsc", latent, gate_grad, preferred_element_type=jnp.float32),
            jnp.einsum("tr,stc->rsc", latent, up_grad, preferred_element_type=jnp.float32),
        ],
        axis=0,
    ).reshape(2 * rank_width, slot_count * block_width)
    back_in_grad = jnp.einsum(
        "tr,sth->rsh", back_latent, hidden_down, preferred_element_type=jnp.float32
    ).reshape(rank_width, slot_count * block_width)
    back_out_grad = jnp.einsum(
        "tr,td->rd", latent_down, grad_cols, preferred_element_type=jnp.float32
    )
    summed = (
        lax.psum_scatter(
            gate_wgrad.astype(jnp.bfloat16), "dp", scatter_dimension=1, tiled=True
        ).astype(jnp.float32),
        lax.psum_scatter(
            up_wgrad.astype(jnp.bfloat16), "dp", scatter_dimension=1, tiled=True
        ).astype(jnp.float32),
        lax.psum_scatter(
            down_wgrad.astype(jnp.bfloat16), "dp", scatter_dimension=1, tiled=True
        ).astype(jnp.float32),
        lax.psum_scatter(
            in_grad.astype(jnp.bfloat16), "dp", scatter_dimension=0, tiled=True
        ).astype(jnp.float32),
        lax.psum_scatter(
            mid_grad.astype(jnp.bfloat16), "dp", scatter_dimension=0, tiled=True
        ).astype(jnp.float32),
        lax.psum_scatter(
            back_in_grad.astype(jnp.bfloat16), "dp", scatter_dimension=0, tiled=True
        ).astype(jnp.float32),
        lax.psum_scatter(
            back_out_grad.astype(jnp.bfloat16), "dp", scatter_dimension=0, tiled=True
        ).astype(jnp.float32),
    )
    up_mask = up_keep[:, None, None]
    down_mask = down_keep[:, None, None]
    gate_out = place_blocks(
        (summed[0] * up_mask).astype(jnp.bfloat16), up_chosen, slot_count, block_depth
    )
    up_out = place_blocks(
        (summed[1] * up_mask).astype(jnp.bfloat16), up_chosen, slot_count, block_depth
    )
    down_flat = place_blocks(
        (summed[2] * down_mask).astype(jnp.bfloat16), down_chosen, slot_count, block_depth
    )
    back_in_out = summed[5].astype(jnp.bfloat16)
    return (
        layer_out,
        token_grad,
        gate_out,
        up_out,
        down_flat,
        summed[3].astype(jnp.bfloat16),
        summed[4].astype(jnp.bfloat16),
        back_in_out,
        summed[6].astype(jnp.bfloat16),
    )


def solution(mesh):
    in_specs = (
        P("dp", None),
        P("dp", None),
        P("mp", None, "dp", None),
        P("mp", None, "dp", None),
        P("mp", None, "dp", None),
        P("dp", None),
        P("dp", "mp"),
        P("dp", "mp"),
        P("dp", "mp"),
        P(),
        P(),
        P(),
        P(),
        P(),
        P(),
    )
    out_specs = (
        P("dp", "mp"),
        P("dp", "mp"),
        P("mp", None, "dp", None),
        P("mp", None, "dp", None),
        P("mp", None, "dp", None),
        P("dp", None),
        P("dp", "mp"),
        P("dp", "mp"),
        P("dp", "mp"),
    )
    return jax.shard_map(local, mesh=mesh, in_specs=in_specs, out_specs=out_specs, check_vma=False)
```

profile of v0, /device:TPU:64, one launch (start us, length us, event | category | flops | bytes accessed | tf_op | source)
XLA Modules:
  0.0 818.6 jit_solution(8887892417835541382)
XLA Ops:
  15.5 4.1 copy.150
  19.6 4.3 copy.151
  24.4 39.3 %all-gather.1 = bf16[32,2,1792]{2,1,0:T(2,128)(2,1)S(1)} all-gather(bf16[1,2,1792]{2,1,0:T(2,128)(2,1)S(1)} %bitcast.170), channel_id=1, replica_groups=mesh['dp'=32,'mp'=8] {'dp'}, dimensions={0}, use_global_device_ids=true | all-gather | bytes 236544 | tf_op jit(solution)/shard_map/all_gather | solution.py:147
  63.9 39.4 %all-gather.2 = bf16[32,2,1024]{2,1,0:T(2,128)(2,1)S(1)} all-gather(bf16[1,2,1024]{2,1,0:T(2,128)(2,1)S(1)} %bitcast.171), channel_id=1, replica_groups=mesh['dp'=32,'mp'=8] {'dp'}, dimensions={0}, use_global_device_ids=true | all-gather | bytes 135168 | tf_op jit(solution)/shard_map/all_gather | solution.py:148
  106.4 4.2 copy.137
  110.7 42.9 %all-gather = bf16[32,4,1792]{2,1,0:T(4,128)(2,1)S(1)} all-gather(bf16[1,4,1792]{2,1,0:T(4,128)(2,1)S(1)} %bitcast.169), channel_id=1, replica_groups=mesh['dp'=32,'mp'=8] {'dp'}, dimensions={0}, use_global_device_ids=true | all-gather | bytes 473088 | tf_op jit(solution)/shard_map/all_gather | solution.py:146
  161.9 34.1 %psum.22 = bf16[128,64]{0,1:T(8,128)(2,1)S(1)} all-reduce(bf16[128,64]{0,1:T(8,128)(2,1)S(1)} %convolution_convert_fusion.6), channel_id=1, replica_groups=mesh['dp'=32,'mp'=8] {'mp'}, use_global_device_ids=true, to_apply=%region_14.15 | all-reduce | flops 8192 | bytes 32768 | tf_op jit(solution)/shard_map/psum | solution.py:66
  199.3 6.1 fusion.1
  212.0 4.1 all-to-all-start.1
  216.4 4.5 fusion.9
  223.8 5.3 all-gather.12.cloned.1.call-done
  229.1 4.5 fusion.7
  251.4 3.8 convolution_add_fusion
  257.7 16.5 %scatter_fusion.1 = f32[64,128,128]{2,1,0:T(8,128)} fusion(f32[64,128,128]{2,1,0:T(8,128)} %broadcast.326.clone.1, s32[70]{0:T(128)S(1)} %select_reduce_fusion.3, f32[70,128,128]{2,1,0:T(8,128)} %convolution_add_fusion), kind=kCustom, calls=%fused_computation.7 | custom fusion | flops 1146880 | bytes 13762840 | tf_op jit(solution)/shard_map/scatter-add | solution.py:70
  274.1 4.0 convert_element_type.145
  282.4 4.7 all-to-all-start
  287.3 15.3 %all-to-all-done = bf16[8,2,128,128]{3,2,1,0:T(8,128)(2,1)} async-done(((bf16[8,2,128,128]{3,2,1,0:T(8,128)(2,1)}), bf16[8,2,128,128]{3,2,1,0:T(8,128)(2,1)}, u32[]{:S(2)}, u32[]{:S(2)}) %all-to-all-start) | async-done | bytes 524320 | tf_op jit(solution)/shard_map/all_to_all | solution.py:55
  312.5 16.7 %scatter_fusion = f32[64,128,128]{2,1,0:T(8,128)} fusion(f32[64,128,128]{2,1,0:T(8,128)} %broadcast.326.clone, s32[70]{0:T(128)S(1)} %select_reduce_fusion.4, f32[70,128,128]{2,1,0:T(8,128)} %fusion.14), kind=kCustom, calls=%fused_computation.6 | custom fusion | flops 1146880 | bytes 13762840 | tf_op jit(solution)/shard_map/scatter-add | solution.py:70
  329.2 3.9 convert_element_type.137
  340.3 4.1 fusion.24
  347.9 32.9 %all-reduce.7 = (bf16[128,64]{0,1:T(8,128)(2,1)S(1)}, bf16[128,64]{0,1:T(8,128)(2,1)S(1)}) all-reduce(bf16[128,64]{0,1:T(8,128)(2,1)S(1)} %fusion.38, bf16[128,64]{0,1:T(8,128)(2,1)S(1)} %fusion.39), channel_id=1, replica_groups=mesh['dp'=32,'mp'=8] {'mp'}, use_global_device_ids=true, to_apply=%region_11.12 | all-reduce | flops 16384 | bytes 65536 | tf_op jit(solution)/shard_map/psum | solution.py:66
  382.6 3.9 fusion.27
  396.2 312.3 %all-reduce.10.cloned.1.call-done = (bf16[70,128,128]{2,1,0:T(8,128)(2,1)}, bf16[70,128,128]{2,1,0:T(8,128)(2,1)}, bf16[70,128,128]{2,1,0:T(8,128)(2,1)}, bf16[1...) async-done(((bf16[70,128,128]{2,1,0:T(8,128)(2,1)}, bf16[70,128,128]{2,1,0:T(8,128)(2,1)}, bf16[70,128,128]{2,1,0:T(8,128)(2,1)}, ...) | async-done | bytes 7700496
  724.5 87.3 %reduce-scatter.12.cloned.1.call-done = bf16[256,64]{0,1:T(8,128)(2,1)} async-done(((bf16[8192,64]{0,1:T(8,128)(2,1)}), bf16[256,64]{0,1:T(8,128)(2,1)}) %reduce-scatter.12.cloned.1.call-update) | async-done | bytes 32784 | tf_op jit(solution)/shard_map/reduce_scatter | solution.py:258
  (182 shorter events, 104.5 us)
Async XLA Ops:
  7.2 16.7 %copy-start = (s32[112,5]{0,1:T(8,128)S(1)}, s32[112,5]{0,1:T(8,128)}, u32[]{:S(2)}) copy-start(s32[112,5]{0,1:T(8,128)} %param.26) | copy-start | bytes 6724
  7.2 189.4 %all-gather.10.cloned.1.call-start = ((), (), s32[]{:S(2)}) async-start(), calls=%async_computation.6 | async-start | bytes 1081344 | tf_op jit(solution)/shard_map/all_gather | solution.py:145
  7.9 191.4 %all-gather.14.cloned.1.call-start = ((), (), s32[]{:S(2)}) async-start(), calls=%async_computation.8 | async-start | bytes 2433024 | tf_op jit(solution)/shard_map/all_gather | solution.py:144
  10.6 205.8 %all-gather.8.cloned.1.call-start = ((), (), s32[]{:S(2)}) async-start(), calls=%async_computation.5 | async-start | bytes 2433024 | tf_op jit(solution)/shard_map/all_gather | solution.py:142
  13.3 215.8 %all-gather.12.cloned.1.call-start = ((), (), s32[]{:S(2)}) async-start(), calls=%async_computation.7 | async-start | bytes 2433024 | tf_op jit(solution)/shard_map/all_gather | solution.py:143
  19.6 4.8 copy-start.21
  19.6 44.3 %copy-start.22 = (bf16[2,1024]{1,0:T(2,128)(2,1)S(1)}, bf16[2,1024]{1,0:T(2,128)(2,1)}, u32[]{:S(2)}) copy-start(bf16[2,1024]{1,0:T(2,128)(2,1)} %param.23) | copy-start | bytes 12292
  19.6 83.8 %copy-start.24 = (s32[112]{0:T(128)S(1)}, s32[112]{0:T(128)}, u32[]{:S(2)}) copy-start(s32[112]{0:T(128)} %param.25) | copy-start | bytes 1348
  19.6 84.4 %copy-start.7 = (bf16[128,8192]{1,0:T(8,128)(2,1)S(1)}, bf16[128,8192]{1,0:T(8,128)(2,1)}, u32[]{:S(2)}) copy-start(bf16[128,8192]{1,0:T(8,128)(2,1)} %param.15) | copy-start | bytes 6291460
  103.4 57.4 %copy-start.14 = (bf16[64,1024]{1,0:T(8,128)(2,1)}, bf16[64,1024]{1,0:T(8,128)(2,1)S(1)}, u32[]{:S(2)}) copy-start(bf16[64,1024]{1,0:T(8,128)(2,1)S(1)} %reshape.439) | copy-start | bytes 393220
  106.4 49.3 %copy-start.9 = (bf16[128,64,128]{2,0,1:T(8,128)(2,1)S(1)}, bf16[128,64,128]{2,0,1:T(8,128)(2,1)}, u32[]{:S(2)}) copy-start(bf16[128,64,128]{2,0,1:T(8,128)(2,1)} %copy.151) | copy-start | bytes 6291460
  212.0 27.5 %all-to-all-start.1 = ((bf16[8,2,128,128]{3,2,1,0:T(8,128)(2,1)}), bf16[8,2,128,128]{3,2,1,0:T(8,128)(2,1)}, u32[]{:S(2)}, u32[]{:S(2)}) async-start(bf16[8,2,128,128]{3,2,1,0:T(8,128)(2,1)} %broadcast_select_fusion), calls=%async_computation.2 | async-start | bytes 1048576 | tf_op jit(solution)/shard_map/all_to_all | solution.py:55
  216.1 175.4 %reduce-scatter.10.cloned.1.call-start = ((), (), s32[]{:S(2)}) async-start(), calls=%async_computation.10 | async-start | bytes 2359296 | tf_op jit(solution)/shard_map/reduce_scatter | solution.py:60
  249.9 5.2 copy-start.4
  282.4 20.1 %all-to-all-start = ((bf16[8,2,128,128]{3,2,1,0:T(8,128)(2,1)}), bf16[8,2,128,128]{3,2,1,0:T(8,128)(2,1)}, u32[]{:S(2)}, u32[]{:S(2)}) async-start(bf16[8,2,128,128]{3,2,1,0:T(8,128)(2,1)} %broadcast_select_fusion.1), calls=%async_computation | async-start | bytes 1048576 | tf_op jit(solution)/shard_map/all_to_all | solution.py:55
  287.1 107.2 %reduce-scatter.8.cloned.1.call-start = ((), (), s32[]{:S(2)}) async-start(), calls=%async_computation.9 | async-start | bytes 2359296 | tf_op jit(solution)/shard_map/reduce_scatter | solution.py:60
  333.1 375.4 %all-reduce.10.cloned.1.call-start = ((), (), s32[]{:S(2)}) async-start(), calls=%async_computation.12 | async-start | bytes 15400960
  346.7 35.9 %copy-start.2 = (bf16[70,128,128]{2,1,0:T(8,128)(2,1)S(1)}, bf16[70,128,128]{2,1,0:T(8,128)(2,1)}, u32[]{:S(2)}) copy-start(bf16[70,128,128]{2,1,0:T(8,128)(2,1)} %gather_fusion.3) | copy-start | bytes 6881284
  386.5 425.3 %reduce-scatter.12.cloned.1.call-start = ((), (), s32[]{:S(2)}) async-start(), calls=%async_computation.11 | async-start | bytes 1081344 | tf_op jit(solution)/shard_map/reduce_scatter | solution.py:258
  388.1 6.2 copy-start.15
  389.5 422.3 %copy-start.1 = (s32[112,5]{0,1:T(8,128)S(1)}, s32[112,5]{0,1:T(8,128)}, u32[]{:S(2)}) copy-start(s32[112,5]{0,1:T(8,128)} %param.26) | copy-start | bytes 6724
  714.7 97.1 %copy-start.18 = (bf16[70,4,128]{2,1,0:T(4,128)(2,1)}, bf16[70,4,128]{2,1,0:T(4,128)(2,1)S(1)}, u32[]{:S(2)}) copy-start(bf16[70,4,128]{2,1,0:T(4,128)(2,1)S(1)} %scatter_fusion.2) | copy-start | bytes 215044
  717.7 94.1 %copy-start.19 = (bf16[70,4,128]{2,1,0:T(4,128)(2,1)}, bf16[70,4,128]{2,1,0:T(4,128)(2,1)S(1)}, u32[]{:S(2)}) copy-start(bf16[70,4,128]{2,1,0:T(4,128)(2,1)S(1)} %scatter_fusion.3) | copy-start | bytes 215044
  721.8 90.0 %copy-start.17 = (bf16[70,4,128]{2,1,0:T(4,128)(2,1)}, bf16[70,4,128]{2,1,0:T(4,128)(2,1)S(1)}, u32[]{:S(2)}) copy-start(bf16[70,4,128]{2,1,0:T(4,128)(2,1)S(1)} %scatter_fusion.4) | copy-start | bytes 215044
  (12 other events, 36.1 us)
Sparse Core Ops, SparseCore 0:
  10.5 52.9 all-gather.9
  66.0 52.4 all-gather.13
  121.0 52.7 all-gather.7
  176.2 52.8 all-gather.11
  278.2 58.9 reduce-scatter.9
  339.6 54.6 reduce-scatter.7
  397.5 311.0 all-reduce.9
  713.4 98.3 reduce-scatter.11
where the time goes:
time: 823 us; the launch traced here: 819 us
  waiting for transfers between devices  422 us (51%)
  blocking collectives  189 us (23%)
  local copies, waits for them, and re-layouts  65.8 us (8%)
  other arithmetic  60.8 us (7%)
  matrix products  55.9 us (7%)
  between operations  16 us (2%)
  starting transfers between devices  9.54 us (1%)
    unnamed x9, waiting for transfers between devices  313 us
    reduce_scatter x1, waiting for transfers between devices, local(): lax.psum_scatter(in_grad.astype(jnp.bfloat16), 'dp', scatter_dimension=0,...  87.3 us
    psum x2, blocking collectives, rank_total(): lax.psum(partial_value.astype(jnp.bfloat16), 'mp').astype(jnp.float32)  67 us
    all_gather x1, blocking collectives, local(): lax.all_gather(low_mid, 'dp', axis=0, tiled=True)  42.9 us
    all_gather x1, blocking collectives, local(): lax.all_gather(down_low_out, 'dp', axis=0, tiled=True)  39.4 us
    all_gather x1, blocking collectives, local(): lax.all_gather(down_low_in, 'dp', axis=0, tiled=True)  39.3 us
    scatter-add x2, other arithmetic, segment_total(): jax.ops.segment_sum(products, segment_ids, num_segments=segment_count)  33.1 us
    unnamed x60, local copies, waits for them, and re-layouts  17.6 us
  transfers between devices with their start and end apart: 10, of which 5 were waited for; matrix products, arithmetic and copies ran while one was open for 17% of the time, Pallas kernels for 0%

commit v1 on v0

v1 whole, which is shorter than its diff:
```python
import jax
import jax.numpy as jnp
from jax import lax
from jax.experimental import pallas as pl
from jax.experimental.pallas import tpu as pltpu
from jax.sharding import Mesh, PartitionSpec as P

F32 = jnp.float32
BF16 = jnp.bfloat16
I32 = jnp.int32
DP = ("zh", "x", "core")
MP = ("y", "zl")
NDP, NMP = 32, 8
SLOTS, DEPTH, BLK = 14, 5, 128
LIVE = 42
RANK = 64
COLS = 64
SHARE = COLS // NMP
CAP = 2
VMEM_LIMIT = 58 * 2**20

GATE, MID, UP, DOWN, DLIN, LOWIN, PACK = 0, 42, 56, 100, 144, 152, 184
GRAD = 152

U_ROW, U_SLOT, D_COL, D_SLOT = 0, 48, 96, 144
U_KEY, D_KEY, U_POS, D_POS = 192, 264, 336, 408
SEND_A, SEND_B, GOT_A, GOT_B, WHO, META = 480, 496, 512, 528, 544, 560


def dot(a, b):
    return lax.dot_general(a, b, (((1,), (0,)), ((), ())), preferred_element_type=F32)


def dot_t(a, b):
    return lax.dot_general(a, b, (((1,), (1,)), ((), ())), preferred_element_type=F32)


def turned(a):
    return a.astype(F32).T.astype(BF16)


def span(start):
    return pl.ds(pl.multiple_of(start * BLK, BLK), BLK)


def call(body, out_shapes, operands, scalars, scratch=()):
    vmem = pl.BlockSpec(memory_space=pltpu.VMEM)
    smem = pl.BlockSpec(memory_space=pltpu.SMEM)
    return pl.pallas_call(
        body,
        out_shape=out_shapes,
        in_specs=[smem] * len(scalars) + [vmem] * len(operands),
        out_specs=jax.tree.map(lambda _: vmem, out_shapes),
        scratch_shapes=list(scratch),
        compiler_params=pltpu.CompilerParams(vmem_limit_bytes=VMEM_LIMIT),
    )(*scalars, *operands)


def shape(*dims, dtype=BF16):
    return jax.ShapeDtypeStruct(dims, dtype)


def pack_body(up_count, down_count, who, gate_w, up_w, down_w, extra, out):
    mine = who[0] * SLOTS
    for pad in (UP + 42, UP + 43, DOWN + 42, DOWN + 43):
        out[pad] = jnp.zeros((4, BLK), BF16)

    def put(weight, counts, base):
        at = jnp.int32(base)
        for s in range(SLOTS):
            count = counts[mine + s]
            for k in range(DEPTH):
                out[at] = weight[s, k]
                at = at + (k < count).astype(I32)

    put(gate_w, up_count, GATE)
    put(up_w, up_count, UP)
    put(down_w, down_count, DOWN)
    for s in range(SLOTS):
        out[MID + s] = extra[s]
    for e in range(PACK - DLIN):
        out[DLIN + e] = extra[SLOTS + e]


def back_latent_body(meta, got, cot, perm2, out):
    mine = meta[WHO] * SHARE
    rows = dot(perm2[...], got[...].reshape(512, BLK)).astype(BF16)
    acc = jnp.zeros((BLK, RANK), F32)
    for e in range(SHARE):
        acc = acc + dot_t(cot[:, span(mine + e)], rows[e * RANK : (e + 1) * RANK])
    out[...] = jnp.concatenate([acc, jnp.zeros_like(acc)], axis=1).astype(BF16)


def forward_body(
    meta, got, tok, cot, back, perm, perm2,
    send, act, w_gu, w_d, mid, dlin, lat, low_share, hid, hgrad,
):
    def rows(block):
        return got[:, 4 * block : 4 * block + 16, :].reshape(512, BLK)

    def pair(first, second):
        joined = jnp.concatenate([rows(first), rows(second)], axis=1)
        return dot(perm[...], joined).astype(BF16)

    for g in range(11):
        both = pair(GATE + 4 * g, UP + 4 * g)
        for jj in range(4):
            piece = both[jj * BLK : (jj + 1) * BLK]
            if 4 * g + jj < LIVE:
                w_gu[4 * g + jj] = piece
            else:
                mid[4 * g + jj - LIVE] = piece[:, :BLK]
    w_gu[LIVE] = jnp.zeros((BLK, 2 * BLK), BF16)
    tiles = [("m", i) for i in range(2, 14, 4)] + [("d", i) for i in range(0, 44, 4)]
    for a, b in zip(tiles[0::2], tiles[1::2]):
        at = [(MID if t == "m" else DOWN) + i for t, i in (a, b)]
        both = pair(*at)
        for jj in range(4):
            for half, (t, i) in enumerate((a, b)):
                piece = both[jj * BLK : (jj + 1) * BLK, half * BLK : (half + 1) * BLK]
                if t == "m":
                    mid[i + jj] = piece
                elif i + jj < LIVE:
                    w_d[i + jj] = piece
    w_d[LIVE] = jnp.zeros((BLK, BLK), BF16)
    joined = jnp.concatenate([rows(DLIN), rows(DLIN + 4)], axis=1)
    both = dot(perm2[...], joined).astype(BF16)
    for t in range(SLOTS):
        dlin[t] = both[(t % 8) * RANK : (t % 8 + 1) * RANK, (t // 8) * BLK : (t // 8 + 1) * BLK]

    acc0 = jnp.zeros((BLK, BLK), F32)
    acc1 = jnp.zeros((BLK, BLK), F32)
    for d in range(NDP):
        low = got[d, 4 * LOWIN : 4 * PACK, :]
        acc0 = acc0 + dot(tok[:, 2 * d * BLK : (2 * d + 1) * BLK], low)
        acc1 = acc1 + dot(tok[:, (2 * d + 1) * BLK : (2 * d + 2) * BLK], low)
    latent = (acc0[:, :RANK] + acc1[:, RANK:]).astype(BF16)
    total = back[0].astype(F32)
    for i in range(1, NMP):
        total = total + back[i].astype(F32)
    back_latent = total[:, :RANK].astype(BF16)
    lat[0] = latent
    lat[1] = back_latent
    for i in range(4):
        low_share[i] = got[4 * meta[WHO] + i, 4 * LOWIN : 4 * PACK, :]

    for t in range(SLOTS):
        acc = dot(back_latent, dlin[t])
        for k in range(DEPTH):
            p = DEPTH * t + k
            acc = acc + dot_t(cot[:, span(meta[D_KEY + p])], w_d[meta[D_POS + p]])
        hgrad[t] = acc.astype(BF16)
    for s in range(SLOTS):
        acc = jnp.concatenate([dot(latent, mid[s, :RANK]), dot(latent, mid[s, RANK:])], axis=1)
        for k in range(DEPTH):
            p = DEPTH * s + k
            acc = acc + dot(tok[:, span(meta[U_KEY + p])], w_gu[meta[U_POS + p]])
        gate, up = acc[:, :BLK], acc[:, BLK:]
        sig = jax.nn.sigmoid(gate)
        active = gate * sig
        hid[s] = (active * up).astype(BF16)
        act[s, :, :BLK] = up * sig * (1.0 + gate * (1.0 - sig))
        act[s, :, BLK:] = active
    for lane in range(NMP * CAP):
        send[lane // CAP, lane % CAP] = hid[meta[SEND_A + lane]]
        send[lane // CAP, CAP + lane % CAP] = hgrad[meta[SEND_B + lane]]


def grads_body(
    meta, got, act, mid, dlin, lat, tok_t, cot, perm, perm2,
    grad, gu, hd, part, hd_t, midg, ding,
):
    latent_t = turned(jnp.concatenate([lat[0], lat[1]], axis=1))
    lat_sum = jnp.zeros((BLK, RANK), F32)
    down_sum = jnp.zeros((BLK, RANK), F32)
    for s in range(SLOTS):
        lane = meta[GOT_B + s]
        flow = got[lane // CAP, CAP + lane % CAP].astype(F32)
        gg = (flow * act[s, :, :BLK]).astype(BF16)
        ug = (flow * act[s, :, BLK:]).astype(BF16)
        both = jnp.concatenate([gg, ug], axis=1)
        gu[s] = both
        lat_sum = lat_sum + dot_t(gg, mid[s, :RANK]) + dot_t(ug, mid[s, RANK:])
        two = dot(latent_t[:RANK], both).astype(BF16)
        midg[s] = jnp.concatenate([two[:, :BLK], two[:, BLK:]], axis=0)
        lane = meta[GOT_A + s]
        h = got[lane // CAP, lane % CAP]
        hd[s] = h
        hd_t[s] = turned(h)
        down_sum = down_sum + dot_t(h, dlin[s])
        ding[s] = dot(latent_t[RANK:], h).astype(BF16)
    part[...] = jnp.concatenate([lat_sum, down_sum], axis=1).astype(BF16)

    def store(tile, rows):
        grad[:, 4 * tile : 4 * tile + 16, :] = rows.reshape(NDP, 16, BLK)

    def pair(first, second, left, right):
        both = dot(perm[...], jnp.concatenate([left, right], axis=1)).astype(BF16)
        store(first, both[:, :BLK])
        store(second, both[:, BLK:])

    zero = jnp.zeros((BLK, BLK), BF16)
    for g in range(11):
        pieces = []
        for j in range(4 * g, 4 * g + 4):
            if j < LIVE:
                piece = dot(tok_t[meta[U_ROW + j]], gu[meta[U_SLOT + j]]).astype(BF16)
            else:
                piece = jnp.concatenate([midg[j - LIVE], zero], axis=1)
            pieces.append(piece)
        both = dot(perm[...], jnp.concatenate(pieces, axis=0)).astype(BF16)
        store(GATE + 4 * g, both[:, :BLK])
        store(UP + 4 * g, both[:, BLK:])

    def tile_of(kind, i):
        pieces = []
        for j in range(i, i + 4):
            if kind == "m":
                pieces.append(midg[j])
            elif j < LIVE:
                cols = cot[:, span(meta[D_COL + j])]
                pieces.append(dot(hd_t[meta[D_SLOT + j]], cols).astype(BF16))
            else:
                pieces.append(zero)
        return jnp.concatenate(pieces, axis=0)

    tiles = [("m", i) for i in range(2, 14, 4)] + [("d", i) for i in range(0, 44, 4)]
    for a, b in zip(tiles[0::2], tiles[1::2]):
        at = [(MID if t == "m" else DOWN) + i for t, i in (a, b)]
        pair(*at, tile_of(*a), tile_of(*b))
    none = jnp.zeros((RANK, BLK), BF16)
    left = jnp.concatenate([ding[t] for t in range(8)], axis=0)
    right = jnp.concatenate([ding[t] for t in range(8, SLOTS)] + [none, none], axis=0)
    both = dot(perm2[...], jnp.concatenate([left, right], axis=1)).astype(BF16)
    store(DLIN, both[:, :BLK])
    store(DLIN + 4, both[:, BLK:])


def token_part_body(meta, gu, w_gu, out, acc):
    acc[...] = jnp.zeros_like(acc)
    for j in range(LIVE):
        r = meta[U_ROW + j]
        acc[r] = acc[r] + dot_t(gu[meta[U_SLOT + j]], w_gu[j])
    for b in range(COLS):
        out[b // SHARE, b % SHARE] = acc[b].astype(BF16)


def out_part_body(meta, hd, w_d, out, acc):
    acc[...] = jnp.zeros_like(acc)
    for j in range(LIVE):
        c = meta[D_COL + j]
        acc[c] = acc[c] + dot(hd[meta[D_SLOT + j]], w_d[j])
    for b in range(COLS):
        out[b // SHARE, b % SHARE] = acc[b].astype(BF16)


def small_grads_body(meta, parts, tok_t, cot, perm2, latents, grad):
    total = parts[0].astype(F32)
    for i in range(1, NMP):
        total = total + parts[i].astype(F32)
    total = total.astype(BF16)
    latents[0] = total[:, :RANK]
    latents[1] = total[:, RANK:]
    who = meta[WHO]
    rows = pl.ds(pl.multiple_of((who % 4) * 32, 32), 32)
    pieces = [tok_t[2 * d + who // 4, rows, :] for d in range(NDP)]
    low = dot(jnp.concatenate(pieces, axis=0), total[:, :RANK]).reshape(NDP, 32, RANK)
    low = jnp.concatenate([low[:, :16], low[:, 16:]], axis=2)
    grad[:, :16, :] = low.astype(BF16)
    down_t = turned(total)[RANK:]
    pieces = [dot(down_t, cot[:, span(who * SHARE + e)]).astype(BF16) for e in range(SHARE)]
    rows = dot(perm2[...], jnp.concatenate(pieces, axis=0)).astype(BF16)
    grad[:, 16:, :] = rows.reshape(NDP, 16, BLK)


def token_out_body(got, latents, low_share, out):
    latent = latents[0]
    for e in range(SHARE):
        total = got[0, e].astype(F32)
        for i in range(1, NMP):
            total = total + got[i, e].astype(F32)
        low = low_share[e // 2]
        low = low[:, :RANK] if e % 2 == 0 else low[:, RANK:]
        out[:, e * BLK : (e + 1) * BLK] = (total + dot_t(latent, low)).astype(BF16)


def layer_out_body(got, latents, dlout, perm2, out):
    latent = latents[1]
    rows = dot(perm2[...], dlout[...].reshape(512, BLK)).astype(BF16)
    for e in range(SHARE):
        total = got[0, e].astype(F32)
        for i in range(1, NMP):
            total = total + got[i, e].astype(F32)
        low = dot(latent, rows[e * RANK : (e + 1) * RANK])
        out[:, e * BLK : (e + 1) * BLK] = (total + low).astype(BF16)


def final_body(up_count, down_count, who, got, gate_o, up_o, down_o, mid_o, tail, red):
    total = got[0].astype(F32)
    for i in range(1, 4):
        total = total + got[i].astype(F32)
    red[...] = total.astype(BF16)
    mine = who[0] * SLOTS
    zero = jnp.zeros((4, BLK), BF16)

    def put(out, counts, base):
        at = jnp.int32(base)
        for s in range(SLOTS):
            count = counts[mine + s]
            for k in range(DEPTH):
                out[s, k] = jnp.where(k < count, red[at], zero)
                at = at + (k < count).astype(I32)

    put(gate_o, up_count, GATE)
    put(up_o, up_count, UP)
    put(down_o, down_count, DOWN)
    for s in range(SLOTS):
        mid_o[:, s * BLK : (s + 1) * BLK] = red[MID + s]
    for e in range(8):
        tail[e] = red[DLIN + e]


def lookup(table_ids, positions):
    span_ids = jnp.arange(table_ids.shape[0], dtype=I32)
    return jnp.sum(jnp.where(positions[..., None] == span_ids, table_ids, 0), axis=-1)


def own_rows(table_ids, mine):
    return lax.dynamic_slice_in_dim(table_ids, mine * SLOTS, SLOTS, 0)


def inverse_of(order_ids):
    ids = jnp.arange(order_ids.shape[0], dtype=I32)
    return jnp.sum(jnp.where(order_ids[None, :] == ids[:, None], ids[None, :], 0), axis=1)


def send_table(owner, peer, rank, local_slot, mine):
    lanes = jnp.arange(NMP * CAP, dtype=I32)
    target = peer * CAP + rank
    matched = (owner[None, :] == mine) & (target[None, :] == lanes[:, None])
    return jnp.sum(jnp.where(matched, local_slot[None, :], 0), axis=1)


def live_table(count, keys):
    live = (jnp.arange(DEPTH, dtype=I32)[None, :] < count[:, None]).reshape(-1)
    ids = jnp.arange(SLOTS * DEPTH, dtype=I32)
    place = jnp.sum(jnp.where((ids[None, :] < ids[:, None]) & live[None, :], 1, 0), axis=1)
    hit = (jnp.arange(LIVE, dtype=I32)[:, None] == place[None, :]) & live[None, :]
    flat = keys.reshape(-1)
    of_key = jnp.sum(jnp.where(hit, flat[None, :], 0), axis=1)
    of_slot = jnp.sum(jnp.where(hit, (ids // DEPTH)[None, :], 0), axis=1)
    return of_key, of_slot, flat, jnp.where(live, place, LIVE)


def tables(mine, up_order, down_order, up_rows, down_cols, up_count, down_count):
    slot_ids = jnp.arange(up_order.shape[0], dtype=I32)
    source = lookup(inverse_of(up_order), down_order)
    from_device, to_device = source // SLOTS, slot_ids // SLOTS
    earlier = (
        (from_device[None, :] == from_device[:, None])
        & (to_device[None, :] == to_device[:, None])
        & (slot_ids[None, :] < slot_ids[:, None])
    )
    rank = jnp.sum(earlier.astype(I32), axis=1)
    send_a = send_table(from_device, to_device, rank, source % SLOTS, mine)
    got_a = own_rows(from_device * CAP + rank, mine)
    send_b = send_table(to_device, from_device, rank, slot_ids % SLOTS, mine)
    blocks_down = lookup(inverse_of(down_order), own_rows(up_order, mine))
    got_b = lookup(to_device * CAP + rank, blocks_down)
    u = live_table(own_rows(up_count, mine), own_rows(up_rows, mine))
    d = live_table(own_rows(down_count, mine), own_rows(down_cols, mine))
    fields = [
        (U_ROW, u[0]), (U_SLOT, u[1]), (D_COL, d[0]), (D_SLOT, d[1]), (U_KEY, u[2]), (D_KEY, d[2]),
        (U_POS, u[3]), (D_POS, d[3]), (SEND_A, send_a), (SEND_B, send_b), (GOT_A, got_a),
        (GOT_B, got_b), (WHO, mine.reshape(1)),
    ]
    ends = [start for start, _ in fields[1:]] + [META]
    padded = [jnp.pad(v, (0, end - start - v.shape[0])) for (start, v), end in zip(fields, ends)]
    return jnp.concatenate(padded)


def permutations():
    r = jnp.arange(512, dtype=I32)
    q_device, q_rest = r // 16, r % 16
    device = (q_device % 4) * 8 + q_device // 4
    row4 = lambda d, rest: (rest // 4) * BLK + 4 * d + rest % 4
    row2 = lambda d, rest: (rest // 2) * RANK + 2 * d + rest % 2
    mat = lambda src: (src[:, None] == r[None, :]).astype(BF16)
    take = mat(row4(q_device, q_rest)).T
    take2 = mat(row2(q_device, q_rest)).T
    give = mat(row4(device, q_rest))
    give2 = mat(row2(device, q_rest))
    give2_plain = mat(row2(q_device, q_rest))
    return take, take2, give, give2, give2_plain


def spread(x, axis, n):
    return lax.all_to_all(jnp.broadcast_to(x[None], (n,) + x.shape), axis, 0, 0, tiled=True)


def local(
    tokens, cotangent, gate_weight, up_weight, down_weight, low_in, low_mid, down_low_in,
    down_low_out, up_order, down_order, up_rows, down_cols, up_count, down_count,
):
    mine = lax.axis_index(MP).astype(I32)
    who = mine.reshape(1)
    mid_rows = low_mid.reshape(4, SLOTS, BLK).transpose(1, 0, 2)
    dlin_rows = jnp.pad(
        down_low_in.reshape(2, SLOTS, BLK).transpose(1, 0, 2).reshape(2 * SLOTS, BLK), ((0, 4), (0, 0))
    ).reshape(8, 4, BLK)
    low_rows = jnp.concatenate([low_in[:BLK], low_in[BLK:]], axis=1).reshape(32, 4, BLK)
    extra = jnp.concatenate([mid_rows, dlin_rows, low_rows], axis=0)
    packed = call(
        pack_body, shape(PACK, 4, BLK), (gate_weight, up_weight, down_weight, extra),
        (up_count, down_count, who),
    )
    gathered = lax.all_gather(packed.reshape(4 * PACK, BLK), DP)

    meta = tables(mine, up_order, down_order, up_rows, down_cols, up_count, down_count)
    take, take2, give, give2, give2_plain = permutations()
    tok_t = tokens.reshape(BLK, COLS, BLK).transpose(1, 2, 0)
    dlout = down_low_out.reshape(2, SHARE, BLK).transpose(1, 0, 2).reshape(16, BLK)
    dlout = spread(dlout, DP, NDP)
    back = call(back_latent_body, shape(BLK, BLK), (dlout, cotangent, take2), (meta,))
    back = spread(back, MP, NMP)

    send, act, w_gu, w_d, mid, dlin, lat, low_share = call(
        forward_body,
        (
            shape(NMP, 2 * CAP, BLK, BLK), shape(SLOTS, BLK, 2 * BLK, dtype=F32),
            shape(LIVE + 1, BLK, 2 * BLK), shape(LIVE + 1, BLK, BLK), shape(SLOTS, BLK, BLK),
            shape(SLOTS, RANK, BLK), shape(2, BLK, RANK), shape(4, BLK, BLK),
        ),
        (gathered, tokens, cotangent, back, take, take2),
        (meta,),
        (pltpu.VMEM((SLOTS, BLK, BLK), BF16), pltpu.VMEM((SLOTS, BLK, BLK), BF16)),
    )
    got = lax.all_to_all(send, MP, 0, 0, tiled=True)

    grad, gu, hd, part = call(
        grads_body,
        (
            shape(NDP, 4 * GRAD, BLK), shape(SLOTS, BLK, 2 * BLK), shape(SLOTS, BLK, BLK),
            shape(BLK, BLK),
        ),
        (got, act, mid, dlin, lat, tok_t, cotangent, give, give2),
        (meta,),
        (
            pltpu.VMEM((SLOTS, BLK, BLK), BF16), pltpu.VMEM((SLOTS, BLK, BLK), BF16),
            pltpu.VMEM((SLOTS, RANK, BLK), BF16),
        ),
    )
    grad = lax.psum_scatter(
        grad.reshape(NDP * 4 * GRAD, BLK), ("x", "core"), scatter_dimension=0, tiled=True
    )
    parts = spread(part, MP, NMP)
    latents, small = call(
        small_grads_body, (shape(2, BLK, RANK), shape(NDP, 32, BLK)),
        (parts, tok_t, cotangent, give2_plain), (meta,),
    )

    acc = pltpu.VMEM((COLS, BLK, BLK), F32)
    columns = shape(NMP, SHARE, BLK, BLK)
    token_part = call(token_part_body, columns, (gu, w_gu), (meta,), (acc,))
    token_got = lax.all_to_all(token_part, MP, 0, 0, tiled=True)
    out_part = call(out_part_body, columns, (hd, w_d), (meta,), (acc,))
    out_got = lax.all_to_all(out_part, MP, 0, 0, tiled=True)
    token_grad = call(
        token_out_body, shape(BLK, SHARE * BLK), (token_got, latents, low_share), ()
    )
    layer_out = call(
        layer_out_body, shape(BLK, SHARE * BLK), (out_got, latents, dlout, take2), ()
    )

    small = lax.all_to_all(small, DP, 0, 0, tiled=True)
    small = jnp.sum(small.astype(F32), axis=0).astype(BF16)
    low_g = spread(small[:16], MP, NMP)
    low_g = jnp.concatenate([low_g[:, :, :RANK], low_g[:, :, RANK:]], axis=1)
    low_in_grad = low_g.reshape(2 * BLK, RANK)
    dlout_g = small[16:].reshape(SHARE, 2, BLK).transpose(1, 0, 2).reshape(2, SHARE * BLK)
    grad = lax.all_to_all(grad.reshape(4, 4 * GRAD, BLK), "zh", 0, 0, tiled=True)
    wide = shape(SLOTS, DEPTH, 4, BLK)
    gate_g, up_g, down_g, mid_g, tail = call(
        final_body, (wide, wide, wide, shape(4, SLOTS * BLK), shape(8, 4, BLK)),
        (grad.reshape(4, GRAD, 4, BLK),), (up_count, down_count, who),
        (pltpu.VMEM((GRAD, 4, BLK), BF16),),
    )
    dlin_g = tail.reshape(16, 2, BLK)[:SLOTS].transpose(1, 0, 2).reshape(2, SLOTS * BLK)
    return layer_out, token_grad, gate_g, up_g, down_g, low_in_grad, mid_g, dlin_g, dlout_g


def solution(mesh):
    fine = Mesh(mesh.devices.reshape(4, 4, 2, 4, 2), DP + MP)
    rows, both, blocks = P(DP, None), P(DP, MP), P(MP, None, DP, None)
    in_specs = (rows, rows, blocks, blocks, blocks, rows, both, both, both) + (P(),) * 6
    out_specs = (both, both, blocks, blocks, blocks, rows, both, both, both)
    return jax.shard_map(local, mesh=fine, in_specs=in_specs, out_specs=out_specs, check_vma=False)
```

time: 823 us -> 270 us (0.33)
  waiting for transfers between devices: 422 us -> 84 us
  blocking collectives: 189 us -> 60.7 us
  matrix products: 55.9 us -> 0 us
  other arithmetic: 60.8 us -> 7.87 us
  Pallas kernels: 0 us -> 50.4 us
  local copies, waits for them, and re-layouts: 65.8 us -> 17.9 us
  starting transfers between devices: 9.54 us -> 33.3 us
    unnamed x9 -> x2, waiting for transfers between devices: 313 us -> 0.03 us
    all_gather x3 -> x0, blocking collectives: 122 us -> none  [the longest x1 42.9 us: local(): lax.all_gather(low_mid, 'dp', axis=0, tiled=True)]
    reduce_scatter x3 -> x1, waiting for transfers between devices: 88.1 us -> 0.01 us  [local(): lax.psum_scatter(grad.reshape(NDP * 4 * GRAD, BLK), ('x', 'core'), scatte...]
    psum x2 -> x0, blocking collectives: 67 us -> none  [rank_total(): lax.psum(partial_value.astype(jnp.bfloat16), 'mp').astype(jnp.float32)]
    all_to_all x0 -> x3, blocking collectives: none -> 60.7 us  [the longest x1 30.2 us: local(): out_got = lax.all_to_all(out_part, MP, 0, 0, tiled=True)]
    dot_general x24 -> x0, matrix products: 55.9 us -> none  [the longest x1 6.13 us: local(): jnp.einsum('tlc,lhc->lth', grad_picked, down_all, preferred_element_type=...]
    pallas_call x0 -> x10, Pallas kernels: none -> 50.4 us  [call(): pl.pallas_call(body, out_shape=out_shapes, in_specs=[smem] * len(scalars)...]
    all_to_all x2 -> x6, waiting for transfers between devices: 15.3 us -> 52.9 us  [the longest x1 22.9 us: local(): token_got = lax.all_to_all(token_part, MP, 0, 0, tiled=True)]
  transfers between devices with their start and end apart: 10 -> 8, of which waited for: 5 -> 7; matrix products, arithmetic and copies ran while one was open for 17% -> 7% of each run, Pallas kernels for 0% -> 8%
where the time goes in v1:
time: 270 us; the launch traced here: 269 us
  waiting for transfers between devices  84 us (31%)
  blocking collectives  60.7 us (22%)
  Pallas kernels  50.4 us (19%)
  starting transfers between devices  33.3 us (12%)
  local copies, waits for them, and re-layouts  17.9 us (7%)
  between operations  14.3 us (5%)
  other arithmetic  7.87 us (3%)
    pallas_call x10, Pallas kernels, call(): pl.pallas_call(body, out_shape=out_shapes, in_specs=[smem] * len(scalars)...  50.4 us
    all_gather x1, waiting for transfers between devices, local(): gathered = lax.all_gather(packed.reshape(4 * PACK, BLK), DP)  31.1 us
    all_to_all x1, blocking collectives, local(): out_got = lax.all_to_all(out_part, MP, 0, 0, tiled=True)  30.2 us
    all_to_all x1, waiting for transfers between devices, local(): token_got = lax.all_to_all(token_part, MP, 0, 0, tiled=True)  22.9 us
    all_to_all x1, blocking collectives, local(): small = lax.all_to_all(small, DP, 0, 0, tiled=True)  20.1 us
    all_to_all x3, starting transfers between devices, spread(): lax.all_to_all(jnp.broadcast_to(x[None], (n,) + x.shape), axis, 0, 0, til...  19 us
    all_to_all x1, waiting for transfers between devices, local(): got = lax.all_to_all(send, MP, 0, 0, tiled=True)  12.1 us
    all_to_all x1, blocking collectives, spread(): lax.all_to_all(jnp.broadcast_to(x[None], (n,) + x.shape), axis, 0, 0, til...  10.3 us
  transfers between devices with their start and end apart: 8, of which 7 were waited for; matrix products, arithmetic and copies ran while one was open for 7% of the time, Pallas kernels for 8%

profile of v1, /device:TPU:64, one launch (start us, length us, event | category | flops | bytes accessed | tf_op | source)
XLA Modules:
  0.0 268.5 jit_solution(2075398237722106830)
XLA Ops:
  13.7 10.7 %all-to-all-start = ((bf16[32,16,128]{2,1,0:T(8,128)(2,1)}), bf16[32,16,128]{2,1,0:T(8,128)(2,1)S(1)}, u32[]{:S(2)}, u32[]{:S(2)}) async-start(bf16[32,16,128]{2,1,0:T(8,128)(2,1)} %broadcast_in_dim.192), calls=%async_computation | async-start | bytes 262144 | tf_op jit(solution)/shard_map/all_to_all | solution.py:398
  34.2 2.9 %shard_map.215 = bf16[128,128]{1,0:T(8,128)(2,1)} custom-call(s32[560]{0:T(1024)} %concatenate.12.meta, bf16[32,16,128]{2,1,0:T(8,128)(2,1)} %copy-done.4, bf16[128,8192]{1,0:T(8,128)(2,1)} %cot.7, bf16[512,512]{1,0:T(8,128)(2,1)} %get-tuple-element.100.perm2), custom_call_target="tpu_custom_call" | custom-call | tf_op jit(solution)/shard_map/pallas_call | solution.py:49
  38.6 4.9 %all-to-all-start.1 = ((bf16[8,128,128]{2,1,0:T(8,128)(2,1)}), bf16[8,128,128]{2,1,0:T(8,128)(2,1)S(1)}, u32[]{:S(2)}, u32[]{:S(2)}) async-start(bf16[8,128,128]{2,1,0:T(8,128)(2,1)} %broadcast_in_dim.193), calls=%async_computation.1 | async-start | bytes 524288 | tf_op jit(solution)/shard_map/all_to_all | solution.py:398
  44.5 6.7 %all-to-all-done.1.back = bf16[8,128,128]{2,1,0:T(8,128)(2,1)S(1)} async-done(((bf16[8,128,128]{2,1,0:T(8,128)(2,1)}), bf16[8,128,128]{2,1,0:T(8,128)(2,1)S(1)}, u32[]{:S(2)}, u32[]{:S(2)}) %all-to-all-start.1) | async-done | bytes 262176 | tf_op jit(solution)/shard_map/all_to_all | solution.py:398
  51.2 31.1 %all-gather.2.cloned.1.call-done.got = bf16[32,736,128]{2,1,0:T(8,128)(2,1)} async-done(((bf16[1,736,128]{2,1,0:T(8,128)(2,1)}), bf16[32,736,128]{2,1,0:T(8,128)(2,1)}) %all-gather.2.cloned.1.call-update) | async-done | bytes 6029328 | tf_op jit(solution)/shard_map/all_gather | solution.py:417
  82.3 13.6 %shard_map.216 = (bf16[8,4,128,128]{3,2,1,0:T(8,128)(2,1)}, f32[14,128,256]{2,1,0:T(8,128)}, bf16[43,128,256]{2,1,0:T(8,128)(2,1)}, bf16[43,128,128]{2,1,0:T(8,1...) custom-call(s32[560]{0:T(1024)} %concatenate.12.meta, ...), custom_call_target="tpu_custom_call" | custom-call | tf_op jit(solution)/shard_map/pallas_call | solution.py:49
  95.9 4.4 %all-to-all-start.2 = ((bf16[8,4,128,128]{3,2,1,0:T(8,128)(2,1)}), bf16[8,4,128,128]{3,2,1,0:T(8,128)(2,1)S(1)}, u32[]{:S(2)}, u32[]{:S(2)}) async-start(bf16[8,4,128,128]{3,2,1,0:T(8,128)(2,1)} %get-tuple-element.28), calls=%async_computation.2 | async-start | bytes 2097152 | tf_op jit(solution)/shard_map/all_to_all | solution.py:438
  100.6 2.5 copy.59
  104.4 12.1 %all-to-all-done.2.got = bf16[8,4,128,128]{3,2,1,0:T(8,128)(2,1)S(1)} async-done(((bf16[8,4,128,128]{3,2,1,0:T(8,128)(2,1)}), bf16[8,4,128,128]{3,2,1,0:T(8,128)(2,1)S(1)}, u32[]{:S(2)}, u32[]{:S(2)}) %all-to-all-start.2) | async-done | bytes 1048608 | tf_op jit(solution)/shard_map/all_to_all | solution.py:438
  117.5 11.1 %shard_map.217 = (bf16[32,608,128]{2,1,0:T(8,128)(2,1)}, bf16[14,128,256]{2,1,0:T(8,128)(2,1)}, bf16[14,128,128]{2,1,0:T(8,128)(2,1)}, bf16[128,128]{1,0:T(8,128)(2,1)}) custom-call(s32[560]{0:T(1024)} %concatenate.12.meta, bf16[8,4,128,128]{3,2,1,0:T(8,128)(2,1)} %copy-done.2, f32[14,128,256]{2,1,0:T(8,128)} %get-tuple-element.29.act, ...), custom_call_target="tpu_custom_call" | custom-call | tf_op jit(solution)/shard_map/pallas_call | solution.py:49
  129.4 10.3 %all_to_all.45.parts = bf16[8,128,128]{2,1,0:T(8,128)(2,1)} all-to-all(bf16[8,128,128]{2,1,0:T(8,128)(2,1)S(1)} %broadcast_in_dim.194), channel_id=1, replica_groups=mesh['zh'=4,'x'=4,'core'=2,'y'=4,'zl'=2] {'y','zl'}, dimensions={0} | all-to-all | bytes 524288 | tf_op jit(solution)/shard_map/all_to_all | solution.py:398
  139.8 3.8 %shard_map.219 = (bf16[2,128,64]{2,1,0:T(8,128)(2,1)}, bf16[32,32,128]{2,1,0:T(8,128)(2,1)}) custom-call(s32[560]{0:T(1024)} %concatenate.12.meta, bf16[8,128,128]{2,1,0:T(8,128)(2,1)} %all_to_all.45.parts, bf16[64,128,128]{2,1,0:T(8,128)(2,1)} %bitcast.37, bf16[128,8192]{1,0:T(8,128)(2,1)} %cot.7, bf16[512,512]{1,0:T(8,128)(2,1)} %get-tuple-element.99.perm2), custom_call_target="tpu_custom_call" | custom-call | tf_op jit(solution)/shard_map/pallas_call | solution.py:49
  143.5 20.1 %all_to_all.46 = bf16[32,32,128]{2,1,0:T(8,128)(2,1)S(1)} all-to-all(bf16[32,32,128]{2,1,0:T(8,128)(2,1)} %get-tuple-element.44), channel_id=1, replica_groups=mesh['zh'=4,'x'=4,'core'=2,'y'=4,'zl'=2] {'zh','x','core'}, dimensions={0} | all-to-all | bytes 524288 | tf_op jit(solution)/shard_map/all_to_all | solution.py:475
  164.9 3.3 %all-to-all-start.8 = ((bf16[8,16,128]{2,1,0:T(8,128)(2,1)}), bf16[8,16,128]{2,1,0:T(8,128)(2,1)S(1)}, u32[]{:S(2)}, u32[]{:S(2)}) async-start(bf16[8,16,128]{2,1,0:T(8,128)(2,1)} %broadcast_in_dim.195), calls=%async_computation.9 | async-start | bytes 65536 | tf_op jit(solution)/shard_map/all_to_all | solution.py:398
  168.3 4.8 %shard_map.221 = bf16[8,8,128,128]{3,2,1,0:T(8,128)(2,1)} custom-call(s32[560]{0:T(1024)} %concatenate.12.meta, bf16[14,128,256]{2,1,0:T(8,128)(2,1)} %get-tuple-element.37.gu, bf16[43,128,256]{2,1,0:T(8,128)(2,1)} %get-tuple-element.38.w_gu), custom_call_target="tpu_custom_call" | custom-call | tf_op jit(solution)/shard_map/pallas_call | solution.py:49
  174.5 4.2 %all-to-all-start.5 = ((bf16[8,8,128,128]{3,2,1,0:T(8,128)(2,1)}), bf16[8,8,128,128]{3,2,1,0:T(8,128)(2,1)S(1)}, u32[]{:S(2)}, u32[]{:S(2)}) async-start(bf16[8,8,128,128]{3,2,1,0:T(8,128)(2,1)} %shard_map.221), calls=%async_computation.5 | async-start | bytes 4194304 | tf_op jit(solution)/shard_map/all_to_all | solution.py:465
  178.7 3.9 %shard_map.218 = bf16[8,8,128,128]{3,2,1,0:T(8,128)(2,1)} custom-call(s32[560]{0:T(1024)} %concatenate.12.meta, bf16[14,128,128]{2,1,0:T(8,128)(2,1)} %get-tuple-element.33.hd, bf16[43,128,128]{2,1,0:T(8,128)(2,1)} %get-tuple-element.34.w_d), custom_call_target="tpu_custom_call" | custom-call | tf_op jit(solution)/shard_map/pallas_call | solution.py:49
  182.6 22.9 %all-to-all-done.5.got = bf16[8,8,128,128]{3,2,1,0:T(8,128)(2,1)S(1)} async-done(((bf16[8,8,128,128]{3,2,1,0:T(8,128)(2,1)}), bf16[8,8,128,128]{3,2,1,0:T(8,128)(2,1)S(1)}, u32[]{:S(2)}, u32[]{:S(2)}) %all-to-all-start.5) | async-done | bytes 2097184 | tf_op jit(solution)/shard_map/all_to_all | solution.py:465
  205.5 30.2 %all_to_all.47.got = bf16[8,8,128,128]{3,2,1,0:T(8,128)(2,1)} all-to-all(bf16[8,8,128,128]{3,2,1,0:T(8,128)(2,1)} %shard_map.218), channel_id=1, replica_groups=mesh['zh'=4,'x'=4,'core'=2,'y'=4,'zl'=2] {'y','zl'}, dimensions={0} | all-to-all | bytes 4194304 | tf_op jit(solution)/shard_map/all_to_all | solution.py:467
  235.7 5.5 %all-to-all-start.6 = ((bf16[4,608,128]{2,1,0:T(8,128)(2,1)}), bf16[4,608,128]{2,1,0:T(8,128)(2,1)S(1)}, u32[]{:S(2)}, u32[]{:S(2)}) async-start(bf16[4,608,128]{2,1,0:T(8,128)(2,1)} %bitcast.41), calls=%async_computation.7 | async-start | bytes 1245184 | tf_op jit(solution)/shard_map/all_to_all | solution.py:481
  242.1 3.0 %shard_map.220 = bf16[128,1024]{1,0:T(8,128)(2,1)} custom-call(bf16[8,8,128,128]{3,2,1,0:T(8,128)(2,1)} %all_to_all.47.got, bf16[2,128,64]{2,1,0:T(8,128)(2,1)} %get-tuple-element.36.latents, bf16[32,16,128]{2,1,0:T(8,128)(2,1)} %copy-done.4, bf16[512,512]{1,0:T(8,128)(2,1)} %get-tuple-element.100.perm2), custom_call_target="tpu_custom_call" | custom-call | tf_op jit(solution)/shard_map/pallas_call | solution.py:49
  245.1 2.8 %shard_map.222 = bf16[128,1024]{1,0:T(8,128)(2,1)} custom-call(bf16[8,8,128,128]{3,2,1,0:T(8,128)(2,1)} %copy-done, bf16[2,128,64]{2,1,0:T(8,128)(2,1)} %get-tuple-element.36.latents, bf16[4,128,128]{2,1,0:T(8,128)(2,1)} %get-tuple-element.39.low_share), custom_call_target="tpu_custom_call" | custom-call | tf_op jit(solution)/shard_map/pallas_call | solution.py:49
  247.9 9.3 %all-to-all-done.6 = bf16[4,608,128]{2,1,0:T(8,128)(2,1)S(1)} async-done(((bf16[4,608,128]{2,1,0:T(8,128)(2,1)}), bf16[4,608,128]{2,1,0:T(8,128)(2,1)S(1)}, u32[]{:S(2)}, u32[]{:S(2)}) %all-to-all-start.6) | async-done | bytes 622624 | tf_op jit(solution)/shard_map/all_to_all | solution.py:481
  258.0 2.4 shard_map.223
  (92 shorter events, 27.4 us)
Async XLA Ops:
  7.2 75.1 %all-gather.2.cloned.1.call-start = ((), (), s32[]{:S(2)}) async-start(), calls=%async_computation.10 | async-start | bytes 6217728 | tf_op jit(solution)/shard_map/all_gather | solution.py:417
  13.7 19.9 %all-to-all-start = ((bf16[32,16,128]{2,1,0:T(8,128)(2,1)}), bf16[32,16,128]{2,1,0:T(8,128)(2,1)S(1)}, u32[]{:S(2)}, u32[]{:S(2)}) async-start(bf16[32,16,128]{2,1,0:T(8,128)(2,1)} %broadcast_in_dim.192), calls=%async_computation | async-start | bytes 262144 | tf_op jit(solution)/shard_map/all_to_all | solution.py:398
  33.6 0.6 copy-start.4
  38.6 12.6 %all-to-all-start.1 = ((bf16[8,128,128]{2,1,0:T(8,128)(2,1)}), bf16[8,128,128]{2,1,0:T(8,128)(2,1)S(1)}, u32[]{:S(2)}, u32[]{:S(2)}) async-start(bf16[8,128,128]{2,1,0:T(8,128)(2,1)} %broadcast_in_dim.193), calls=%async_computation.1 | async-start | bytes 524288 | tf_op jit(solution)/shard_map/all_to_all | solution.py:398
  51.2 31.1 %copy-start.5 = (bf16[8,128,128]{2,1,0:T(8,128)(2,1)}, bf16[8,128,128]{2,1,0:T(8,128)(2,1)S(1)}, u32[]{:S(2)}) copy-start(bf16[8,128,128]{2,1,0:T(8,128)(2,1)S(1)} %all-to-all-done.1.back) | copy-start | bytes 786436
  95.9 4.7 %copy-start.1 = (bf16[128,8192]{1,0:T(8,128)(2,1)S(1)}, bf16[128,8192]{1,0:T(8,128)(2,1)}, u32[]{:S(2)}) copy-start(bf16[128,8192]{1,0:T(8,128)(2,1)} %tok.1) | copy-start | bytes 6291460
  95.9 20.6 %all-to-all-start.2 = ((bf16[8,4,128,128]{3,2,1,0:T(8,128)(2,1)}), bf16[8,4,128,128]{3,2,1,0:T(8,128)(2,1)S(1)}, u32[]{:S(2)}, u32[]{:S(2)}) async-start(bf16[8,4,128,128]{3,2,1,0:T(8,128)(2,1)} %get-tuple-element.28), calls=%async_computation.2 | async-start | bytes 2097152 | tf_op jit(solution)/shard_map/all_to_all | solution.py:438
  100.3 135.4 %reduce-scatter.2.cloned.1.call-start = ((), (), s32[]{:S(2)}) async-start(), calls=%async_computation.11 | async-start | bytes 5603328 | tf_op jit(solution)/shard_map/reduce_scatter | solution.py:453
  116.5 1.0 copy-start.2
  128.6 0.8 copy-start.6
  164.9 9.5 %all-to-all-start.8 = ((bf16[8,16,128]{2,1,0:T(8,128)(2,1)}), bf16[8,16,128]{2,1,0:T(8,128)(2,1)S(1)}, u32[]{:S(2)}, u32[]{:S(2)}) async-start(bf16[8,16,128]{2,1,0:T(8,128)(2,1)} %broadcast_in_dim.195), calls=%async_computation.9 | async-start | bytes 65536 | tf_op jit(solution)/shard_map/all_to_all | solution.py:398
  174.5 31.0 %all-to-all-start.5 = ((bf16[8,8,128,128]{3,2,1,0:T(8,128)(2,1)}), bf16[8,8,128,128]{3,2,1,0:T(8,128)(2,1)S(1)}, u32[]{:S(2)}, u32[]{:S(2)}) async-start(bf16[8,8,128,128]{3,2,1,0:T(8,128)(2,1)} %shard_map.221), calls=%async_computation.5 | async-start | bytes 4194304 | tf_op jit(solution)/shard_map/all_to_all | solution.py:465
  205.5 30.2 %copy-start = (bf16[8,8,128,128]{3,2,1,0:T(8,128)(2,1)}, bf16[8,8,128,128]{3,2,1,0:T(8,128)(2,1)S(1)}, u32[]{:S(2)}) copy-start(bf16[8,8,128,128]{3,2,1,0:T(8,128)(2,1)S(1)} %all-to-all-done.5.got) | copy-start | bytes 6291460
  235.7 21.4 %all-to-all-start.6 = ((bf16[4,608,128]{2,1,0:T(8,128)(2,1)}), bf16[4,608,128]{2,1,0:T(8,128)(2,1)S(1)}, u32[]{:S(2)}, u32[]{:S(2)}) async-start(bf16[4,608,128]{2,1,0:T(8,128)(2,1)} %bitcast.41), calls=%async_computation.7 | async-start | bytes 1245184 | tf_op jit(solution)/shard_map/all_to_all | solution.py:481
  257.1 0.8 copy-start.3
Sparse Core Ops, SparseCore 0:
  12.4 69.8 all-gather.1
  128.8 40.6 reduce-scatter.1

commit v2 on v1

v2 whole, which is shorter than its diff:
```python
import jax
import jax.numpy as jnp
from jax import lax
from jax.experimental import pallas as pl
from jax.experimental.pallas import tpu as pltpu
from jax.sharding import Mesh, PartitionSpec as P

F32 = jnp.float32
BF16 = jnp.bfloat16
I32 = jnp.int32
DP = ("zh", "x", "core")
MP = ("y", "zl")
NDP, NMP = 32, 8
SLOTS, DEPTH, BLK = 14, 5, 128
LIVE = 42
RANK = 64
COLS = 64
SHARE = COLS // NMP
CAP = 2
NY = 4
BACK_LOW = CAP * BLK
BACK_SUM = BACK_LOW + CAP * RANK
BACK_ROWS = BACK_SUM + BLK
VMEM_LIMIT = 58 * 2**20

GATE, MID, UP, LOWIN, PACK_A = 0, 42, 56, 100, 132
DOWN, DLIN, DLOUT, PACK_B = 0, 44, 52, 56
GRAD_A, GRAD = 100, 152

U_ROW, U_SLOT, D_COL, D_SLOT = 0, 48, 96, 144
U_KEY, D_KEY, U_POS, D_POS = 192, 264, 336, 408
SEND_A, SEND_B, GOT_A, GOT_B, WHO, META = 480, 496, 512, 528, 544, 560


def dot(a, b):
    return lax.dot_general(a, b, (((1,), (0,)), ((), ())), preferred_element_type=F32)


def dot_t(a, b):
    return lax.dot_general(a, b, (((1,), (1,)), ((), ())), preferred_element_type=F32)


def turned(a):
    return a.astype(F32).T.astype(BF16)


def span(start):
    return pl.ds(pl.multiple_of(start * BLK, BLK), BLK)


def call(body, out_shapes, operands, scalars, scratch=()):
    vmem = pl.BlockSpec(memory_space=pltpu.VMEM)
    smem = pl.BlockSpec(memory_space=pltpu.SMEM)
    return pl.pallas_call(
        body,
        out_shape=out_shapes,
        in_specs=[smem] * len(scalars) + [vmem] * len(operands),
        out_specs=jax.tree.map(lambda _: vmem, out_shapes),
        scratch_shapes=list(scratch),
        compiler_params=pltpu.CompilerParams(vmem_limit_bytes=VMEM_LIMIT),
    )(*scalars, *operands)


def shape(*dims, dtype=BF16):
    return jax.ShapeDtypeStruct(dims, dtype)


def pack_body(up_count, down_count, who, gate_w, up_w, down_w, mid, low, dlin, dlout, first, second):
    mine = who[0] * SLOTS
    for pad in (UP + 42, UP + 43):
        first[pad] = jnp.zeros((4, BLK), BF16)
    for pad in (DOWN + 42, DOWN + 43):
        second[pad] = jnp.zeros((4, BLK), BF16)

    def put(out, weight, counts, base):
        at = jnp.int32(base)
        for s in range(SLOTS):
            count = counts[mine + s]
            for k in range(DEPTH):
                out[at] = weight[s, k]
                at = at + (k < count).astype(I32)

    put(second, down_w, down_count, DOWN)
    put(first, gate_w, up_count, GATE)
    put(first, up_w, up_count, UP)
    for s in range(SLOTS):
        first[MID + s] = mid[s]
    for e in range(32):
        first[LOWIN + e] = low[e]
    for e in range(8):
        second[DLIN + e] = dlin[e]
    for e in range(4):
        second[DLOUT + e] = dlout[e]


def hidden_grad_body(meta, got, cot, perm, perm2, send, w_d, dlin, dlout, hgrad):
    def rows(block):
        return got[:, 4 * block : 4 * block + 16, :].reshape(512, BLK)

    for g in range(0, 11, 2):
        blocks = [DOWN + 4 * i for i in (g, g + 1) if i < 11]
        both = dot(perm[...], jnp.concatenate([rows(b) for b in blocks], axis=1)).astype(BF16)
        for half in range(len(blocks)):
            for jj in range(4):
                j = 4 * (g + half) + jj
                if j < LIVE:
                    w_d[j] = both[jj * BLK : (jj + 1) * BLK, half * BLK : (half + 1) * BLK]
    w_d[LIVE] = jnp.zeros((BLK, BLK), BF16)
    joined = jnp.concatenate([rows(DLIN), rows(DLIN + 4)], axis=1)
    both = dot(perm2[...], joined).astype(BF16)
    for t in range(SLOTS):
        dlin[t] = both[(t % 8) * RANK : (t % 8 + 1) * RANK, (t // 8) * BLK : (t // 8 + 1) * BLK]
    who = meta[WHO] * SHARE
    low = dot(perm2[...], rows(DLOUT)).astype(BF16)
    dlout[...] = low
    total = jnp.zeros((BLK, RANK), F32)
    for e in range(SHARE):
        total = total + dot_t(cot[:, span(who + e)], low[e * RANK : (e + 1) * RANK])
    total = jnp.concatenate([total, jnp.zeros_like(total)], axis=1).astype(BF16)
    for t in range(SLOTS):
        acc = jnp.zeros((BLK, BLK), F32)
        for k in range(DEPTH):
            p = DEPTH * t + k
            acc = acc + dot_t(cot[:, span(meta[D_KEY + p])], w_d[meta[D_POS + p]])
        hgrad[t] = acc.astype(BF16)
    for lane in range(NMP * CAP):
        peer, c = lane // CAP, lane % CAP
        t = meta[SEND_B + lane]
        send[peer, c * BLK : (c + 1) * BLK] = hgrad[t]
        send[peer, BACK_LOW + c * RANK : BACK_LOW + (c + 1) * RANK] = dlin[t]
    for peer in range(NMP):
        send[peer, BACK_SUM:] = total


def forward_body(meta, got, tok, perm, send, act, w_gu, mid, lat, low_share, hid):
    def rows(block):
        return got[:, 4 * block : 4 * block + 16, :].reshape(512, BLK)

    def pair(first, second):
        joined = jnp.concatenate([rows(first), rows(second)], axis=1)
        return dot(perm[...], joined).astype(BF16)

    for g in range(11):
        both = pair(GATE + 4 * g, UP + 4 * g)
        for jj in range(4):
            piece = both[jj * BLK : (jj + 1) * BLK]
            if 4 * g + jj < LIVE:
                w_gu[4 * g + jj] = piece
            else:
                mid[4 * g + jj - LIVE] = piece[:, :BLK]
    w_gu[LIVE] = jnp.zeros((BLK, 2 * BLK), BF16)
    for a, b in ((2, 6), (10, 10)):
        both = pair(MID + a, MID + b)
        for half, i in enumerate((a, b)[: 1 + (a != b)]):
            for jj in range(4):
                mid[i + jj] = both[jj * BLK : (jj + 1) * BLK, half * BLK : (half + 1) * BLK]

    acc0 = jnp.zeros((BLK, BLK), F32)
    acc1 = jnp.zeros((BLK, BLK), F32)
    for d in range(NDP):
        low = got[d, 4 * LOWIN : 4 * PACK_A, :]
        acc0 = acc0 + dot(tok[:, 2 * d * BLK : (2 * d + 1) * BLK], low)
        acc1 = acc1 + dot(tok[:, (2 * d + 1) * BLK : (2 * d + 2) * BLK], low)
    latent = (acc0[:, :RANK] + acc1[:, RANK:]).astype(BF16)
    lat[...] = latent
    for i in range(4):
        low_share[i] = got[4 * meta[WHO] + i, 4 * LOWIN : 4 * PACK_A, :]

    for s in range(SLOTS):
        acc = jnp.concatenate([dot(latent, mid[s, :RANK]), dot(latent, mid[s, RANK:])], axis=1)
        for k in range(DEPTH):
            p = DEPTH * s + k
            acc = acc + dot(tok[:, span(meta[U_KEY + p])], w_gu[meta[U_POS + p]])
        gate, up = acc[:, :BLK], acc[:, BLK:]
        sig = jax.nn.sigmoid(gate)
        active = gate * sig
        hid[s] = (active * up).astype(BF16)
        act[s, :, :BLK] = up * sig * (1.0 + gate * (1.0 - sig))
        act[s, :, BLK:] = active
    for lane in range(NMP * CAP):
        send[lane // CAP, lane % CAP] = hid[meta[SEND_A + lane]]


def up_grads_body(
    meta, got, act, mid, lat, tok_t, perm, grad, gu, part, back_latent, midg, full, sem
):
    latent = lat[...]
    total = got[0, BACK_SUM:].astype(F32)
    for i in range(1, NMP):
        total = total + got[i, BACK_SUM:].astype(F32)
    back = total[:, :RANK].astype(BF16)
    back_latent[...] = back
    latent_t = turned(jnp.concatenate([latent, latent], axis=1))[:RANK]
    lat_sum = jnp.zeros((BLK, RANK), F32)
    for s in range(SLOTS):
        lane = meta[GOT_B + s]
        peer, c = lane // CAP, lane % CAP
        block = got[peer, span(c), :].astype(F32)
        at = pl.multiple_of(BACK_LOW + c * RANK, RANK)
        flow = (block + dot(back, got[peer, pl.ds(at, RANK), :])).astype(BF16).astype(F32)
        gg = (flow * act[s, :, :BLK]).astype(BF16)
        ug = (flow * act[s, :, BLK:]).astype(BF16)
        both = jnp.concatenate([gg, ug], axis=1)
        gu[s] = both
        lat_sum = lat_sum + dot_t(gg, mid[s, :RANK]) + dot_t(ug, mid[s, RANK:])
        two = dot(latent_t, both).astype(BF16)
        midg[s] = jnp.concatenate([two[:, :BLK], two[:, BLK:]], axis=0)
    part[...] = lat_sum

    def store(block, rows):
        full[:, 4 * block : 4 * block + 16, :] = rows.reshape(NDP, 16, BLK)

    zero = jnp.zeros((BLK, BLK), BF16)
    for g in range(11):
        pieces = []
        for j in range(4 * g, 4 * g + 4):
            if j < LIVE:
                piece = dot(tok_t[meta[U_ROW + j]], gu[meta[U_SLOT + j]]).astype(BF16)
            else:
                piece = jnp.concatenate([midg[j - LIVE], zero], axis=1)
            pieces.append(piece)
        both = dot(perm[...], jnp.concatenate(pieces, axis=0)).astype(BF16)
        store(GATE + 4 * g, both[:, :BLK])
        store(UP + 4 * g, both[:, BLK:])
    for i in (2, 6, 10):
        rows = jnp.concatenate([midg[i + jj] for jj in range(4)], axis=0)
        store(MID + i, dot(perm[...], rows).astype(BF16))
    copy = pltpu.make_async_copy(full, grad.at[:, : 4 * GRAD_A, :], sem)
    copy.start()
    copy.wait()


def down_grads_body(
    meta, got, dlin, back_latent, cot, perm, perm2, start, grad, hd, part, hd_t, ding, full, sem
):
    back = back_latent[...]
    back_t = turned(jnp.concatenate([back, back], axis=1))[:RANK]
    down_sum = jnp.zeros((BLK, RANK), F32)
    for t in range(SLOTS):
        lane = meta[GOT_A + t]
        h = got[lane // CAP, lane % CAP]
        hd[t] = h
        hd_t[t] = turned(h)
        down_sum = down_sum + dot_t(h, dlin[t])
        ding[t] = dot(back_t, h).astype(BF16)
    part[...] = down_sum

    def store(block, rows):
        full[:, 4 * block : 4 * block + 16, :] = rows.reshape(NDP, 16, BLK)

    zero = jnp.zeros((BLK, BLK), BF16)

    def tile_of(g):
        pieces = []
        for j in range(4 * g, 4 * g + 4):
            if j < LIVE:
                cols = cot[:, span(meta[D_COL + j])]
                pieces.append(dot(hd_t[meta[D_SLOT + j]], cols).astype(BF16))
            else:
                pieces.append(zero)
        return jnp.concatenate(pieces, axis=0)

    for g in range(0, 11, 2):
        tiles = [i for i in (g, g + 1) if i < 11]
        both = dot(perm[...], jnp.concatenate([tile_of(i) for i in tiles], axis=1)).astype(BF16)
        for half, i in enumerate(tiles):
            store(DOWN + 4 * i, both[:, half * BLK : (half + 1) * BLK])
    none = jnp.zeros((RANK, BLK), BF16)
    left = jnp.concatenate([ding[t] for t in range(8)], axis=0)
    right = jnp.concatenate([ding[t] for t in range(8, SLOTS)] + [none, none], axis=0)
    both = dot(perm2[...], jnp.concatenate([left, right], axis=1)).astype(BF16)
    store(DLIN, both[:, :BLK])
    store(DLIN + 4, both[:, BLK:])
    copy = pltpu.make_async_copy(full, grad.at[:, 4 * GRAD_A :, :], sem)
    copy.start()
    copy.wait()


def token_part_body(meta, gu, w_gu, keep, pass_on, acc):
    acc[...] = jnp.zeros_like(acc)
    for j in range(LIVE):
        r = meta[U_ROW + j]
        acc[r] = acc[r] + dot_t(gu[meta[U_SLOT + j]], w_gu[j])
    y, z = meta[WHO] // 2, lax.rem(meta[WHO], 2)
    for k in range(NY):
        owner = 2 * lax.rem(y + k, NY)
        for e in range(SHARE):
            keep[k, e] = acc[(owner + z) * SHARE + e].astype(BF16)
            pass_on[k, e] = acc[(owner + 1 - z) * SHARE + e].astype(BF16)


def out_part_body(meta, hd, w_d, *rest):
    outs, acc = rest[:NY], rest[NY]
    acc[...] = jnp.zeros_like(acc)
    for j in range(LIVE):
        c = meta[D_COL + j]
        acc[c] = acc[c] + dot(hd[meta[D_SLOT + j]], w_d[j])
    for k in range(NY):
        owner = 2 * lax.rem(meta[WHO] // 2 + k, NY)
        for i in range(2):
            for e in range(SHARE):
                outs[k][i, e] = acc[(owner + i) * SHARE + e].astype(BF16)


def token_pair_body(keep, came, *outs):
    for k in range(NY):
        outs[k][...] = (keep[k].astype(F32) + came[k].astype(F32)).astype(BF16)


def out_y_body(meta, *refs):
    got, (keep, pass_on) = refs[:NY], refs[NY:]
    z = lax.rem(meta[WHO], 2)
    for out, i in ((pass_on, 1 - z), (keep, z)):
        for e in range(SHARE):
            total = got[0][i, e].astype(F32)
            for ref in got[1:]:
                total = total + ref[i, e].astype(F32)
            out[e] = total.astype(BF16)


def small_grads_body(meta, parts, tok_t, cot, perm2, latents, grad):
    total = parts[0].astype(F32)
    for i in range(1, NMP):
        total = total + parts[i].astype(F32)
    total = total.astype(BF16)
    latents[0] = total[:, :RANK]
    latents[1] = total[:, RANK:]
    who = meta[WHO]
    rows = pl.ds(pl.multiple_of((who % 4) * 32, 32), 32)
    pieces = [tok_t[2 * d + who // 4, rows, :] for d in range(NDP)]
    low = dot(jnp.concatenate(pieces, axis=0), total[:, :RANK]).reshape(NDP, 32, RANK)
    low = jnp.concatenate([low[:, :16], low[:, 16:]], axis=2)
    grad[:, :16, :] = low.astype(BF16)
    down_t = turned(total)[RANK:]
    pieces = [dot(down_t, cot[:, span(who * SHARE + e)]).astype(BF16) for e in range(SHARE)]
    rows = dot(perm2[...], jnp.concatenate(pieces, axis=0)).astype(BF16)
    grad[:, 16:, :] = rows.reshape(NDP, 16, BLK)


def share_sum(refs, e):
    total = refs[0][e].astype(F32)
    for ref in refs[1:]:
        total = total + ref[e].astype(F32)
    return total


def token_out_body(*refs):
    got, (latents, low_share, out) = refs[:NY], refs[NY:]
    latent = latents[0]
    for e in range(SHARE):
        low = low_share[e // 2]
        low = low[:, :RANK] if e % 2 == 0 else low[:, RANK:]
        out[:, e * BLK : (e + 1) * BLK] = (share_sum(got, e) + dot_t(latent, low)).astype(BF16)


def layer_out_body(keep, came, latents, dlout, out):
    latent = latents[1]
    for e in range(SHARE):
        low = dot(latent, dlout[e * RANK : (e + 1) * RANK])
        out[:, e * BLK : (e + 1) * BLK] = (share_sum((keep, came), e) + low).astype(BF16)


def final_body(up_count, down_count, who, got, gate_o, up_o, down_o, mid_o, tail, red):
    total = got[0].astype(F32)
    for i in range(1, 4):
        total = total + got[i].astype(F32)
    red[...] = total.astype(BF16)
    mine = who[0] * SLOTS
    zero = jnp.zeros((4, BLK), BF16)

    def put(out, counts, base):
        at = jnp.int32(base)
        for s in range(SLOTS):
            count = counts[mine + s]
            for k in range(DEPTH):
                out[s, k] = jnp.where(k < count, red[at], zero)
                at = at + (k < count).astype(I32)

    put(gate_o, up_count, GATE)
    put(up_o, up_count, UP)
    put(down_o, down_count, GRAD_A + DOWN)
    for s in range(SLOTS):
        mid_o[:, s * BLK : (s + 1) * BLK] = red[MID + s]
    for e in range(8):
        tail[e] = red[GRAD_A + DLIN + e]


def lookup(table_ids, positions):
    span_ids = jnp.arange(table_ids.shape[0], dtype=I32)
    return jnp.sum(jnp.where(positions[..., None] == span_ids, table_ids, 0), axis=-1)


def own_rows(table_ids, mine):
    return lax.dynamic_slice_in_dim(table_ids, mine * SLOTS, SLOTS, 0)


def inverse_of(order_ids):
    ids = jnp.arange(order_ids.shape[0], dtype=I32)
    return jnp.sum(jnp.where(order_ids[None, :] == ids[:, None], ids[None, :], 0), axis=1)


def send_table(owner, peer, rank, local_slot, mine):
    lanes = jnp.arange(NMP * CAP, dtype=I32)
    target = peer * CAP + rank
    matched = (owner[None, :] == mine) & (target[None, :] == lanes[:, None])
    return jnp.sum(jnp.where(matched, local_slot[None, :], 0), axis=1)


def live_table(count, keys):
    live = (jnp.arange(DEPTH, dtype=I32)[None, :] < count[:, None]).reshape(-1)
    ids = jnp.arange(SLOTS * DEPTH, dtype=I32)
    place = jnp.sum(jnp.where((ids[None, :] < ids[:, None]) & live[None, :], 1, 0), axis=1)
    hit = (jnp.arange(LIVE, dtype=I32)[:, None] == place[None, :]) & live[None, :]
    flat = keys.reshape(-1)
    of_key = jnp.sum(jnp.where(hit, flat[None, :], 0), axis=1)
    of_slot = jnp.sum(jnp.where(hit, (ids // DEPTH)[None, :], 0), axis=1)
    return of_key, of_slot, flat, jnp.where(live, place, LIVE)


def tables(mine, up_order, down_order, up_rows, down_cols, up_count, down_count):
    slot_ids = jnp.arange(up_order.shape[0], dtype=I32)
    source = lookup(inverse_of(up_order), down_order)
    from_device, to_device = source // SLOTS, slot_ids // SLOTS
    earlier = (
        (from_device[None, :] == from_device[:, None])
        & (to_device[None, :] == to_device[:, None])
        & (slot_ids[None, :] < slot_ids[:, None])
    )
    rank = jnp.sum(earlier.astype(I32), axis=1)
    send_a = send_table(from_device, to_device, rank, source % SLOTS, mine)
    got_a = own_rows(from_device * CAP + rank, mine)
    send_b = send_table(to_device, from_device, rank, slot_ids % SLOTS, mine)
    blocks_down = lookup(inverse_of(down_order), own_rows(up_order, mine))
    got_b = lookup(to_device * CAP + rank, blocks_down)
    u = live_table(own_rows(up_count, mine), own_rows(up_rows, mine))
    d = live_table(own_rows(down_count, mine), own_rows(down_cols, mine))
    fields = [
        (U_ROW, u[0]), (U_SLOT, u[1]), (D_COL, d[0]), (D_SLOT, d[1]), (U_KEY, u[2]), (D_KEY, d[2]),
        (U_POS, u[3]), (D_POS, d[3]), (SEND_A, send_a), (SEND_B, send_b), (GOT_A, got_a),
        (GOT_B, got_b), (WHO, mine.reshape(1)),
    ]
    ends = [start for start, _ in fields[1:]] + [META]
    padded = [jnp.pad(v, (0, end - start - v.shape[0])) for (start, v), end in zip(fields, ends)]
    return jnp.concatenate(padded)


def permutations():
    r = jnp.arange(512, dtype=I32)
    q, rest = r // 16, r % 16
    plain = q
    chain = (q % 4) * 8 + (q // 4 % 4) * 2 + q // 16
    give = (q % 4) * 8 + q // 4
    row4 = lambda d: (rest // 4) * BLK + 4 * d + rest % 4
    row2 = lambda d: (rest // 2) * RANK + 2 * d + rest % 2
    out = lambda src: (src[:, None] == r[None, :]).astype(BF16)
    into = lambda src: (src[None, :] == r[:, None]).astype(BF16)
    return (
        into(row4(plain)), into(row4(chain)), into(row2(chain)),
        out(row4(give)), out(row2(give)), out(row2(plain)),
    )


def spread(x, axis, n):
    return lax.all_to_all(jnp.broadcast_to(x[None], (n,) + x.shape), axis, 0, 0, tiled=True)


def gather_step(x, axis, n):
    x = spread(x, axis, n)
    return x.reshape((-1,) + x.shape[-2:])


def together(values):
    return lax.optimization_barrier(values)


def rotate(parts):
    moved = [
        lax.ppermute(parts[k], "y", [(i, (i + k) % NY) for i in range(NY)]) for k in range(1, NY)
    ]
    return [parts[0]] + moved


def double(x, axis, pairs, upper):
    came = lax.ppermute(x, axis, pairs)
    return jnp.concatenate([jnp.where(upper, came, x), jnp.where(upper, x, came)], axis=0)


def local(
    tokens, cotangent, gate_weight, up_weight, down_weight, low_in, low_mid, down_low_in,
    down_low_out, up_order, down_order, up_rows, down_cols, up_count, down_count,
):
    mine = lax.axis_index(MP).astype(I32)
    who = mine.reshape(1)
    mid_rows = low_mid.reshape(4, SLOTS, BLK).transpose(1, 0, 2)
    dlin_rows = jnp.pad(
        down_low_in.reshape(2, SLOTS, BLK).transpose(1, 0, 2).reshape(2 * SLOTS, BLK), ((0, 4), (0, 0))
    ).reshape(8, 4, BLK)
    low_rows = jnp.concatenate([low_in[:BLK], low_in[BLK:]], axis=1).reshape(32, 4, BLK)
    dlout_rows = down_low_out.reshape(2, SHARE, BLK).transpose(1, 0, 2).reshape(4, 4, BLK)
    first, second = call(
        pack_body, (shape(PACK_A, 4, BLK), shape(PACK_B, 4, BLK)),
        (gate_weight, up_weight, down_weight, mid_rows, low_rows, dlin_rows, dlout_rows),
        (up_count, down_count, who),
    )
    got_up = lax.all_gather(first.reshape(4 * PACK_A, BLK), DP)
    got_down = gather_step(second.reshape(1, 4 * PACK_B, BLK), "zh", 4)
    ids = (mine, up_order, down_order, up_rows, down_cols, up_count, down_count)
    got_down, ids = together((got_down, ids))
    got_down = gather_step(got_down, "x", 4)
    meta = tables(*ids)
    take, take_c, take2_c, give, give2, give2_plain = permutations()
    got_down, meta = together((got_down, meta))
    got_down = gather_step(got_down, "core", 2)
    tok_t = tokens.reshape(BLK, COLS, BLK).transpose(1, 2, 0)

    slots = shape(SLOTS, BLK, BLK)
    slots_scratch = pltpu.VMEM((SLOTS, BLK, BLK), BF16)
    parcel = shape(NMP, CAP, BLK, BLK)
    got_down, take, give, give2, give2_plain = together((got_down, take, give, give2, give2_plain))
    back_send, w_d, dlin, dlout = call(
        hidden_grad_body,
        (
            shape(NMP, BACK_ROWS, BLK), shape(LIVE + 1, BLK, BLK), shape(SLOTS, RANK, BLK),
            shape(512, BLK),
        ),
        (got_down, cotangent, take_c, take2_c), (meta,), (slots_scratch,),
    )
    back_send, tok_t = together((back_send, tok_t))
    back_got = lax.all_to_all(back_send, MP, 0, 0, tiled=True)

    send, act, w_gu, mid, lat, low_share = call(
        forward_body,
        (
            parcel, shape(SLOTS, BLK, 2 * BLK, dtype=F32), shape(LIVE + 1, BLK, 2 * BLK), slots,
            shape(BLK, RANK), shape(4, BLK, BLK),
        ),
        (got_up, tokens, take), (meta,), (slots_scratch,),
    )
    got = lax.all_to_all(send, MP, 0, 0, tiled=True)

    hbm = pl.BlockSpec(memory_space=pl.ANY)
    vmem = pl.BlockSpec(memory_space=pltpu.VMEM)
    smem = pl.BlockSpec(memory_space=pltpu.SMEM)
    grad_shape = shape(NDP, 4 * GRAD, BLK)
    grad, gu, part_up, back_latent = pl.pallas_call(
        up_grads_body,
        out_shape=(
            grad_shape, shape(SLOTS, BLK, 2 * BLK), shape(BLK, RANK, dtype=F32), shape(BLK, RANK),
        ),
        in_specs=[smem] + [vmem] * 6,
        out_specs=(hbm, vmem, vmem, vmem),
        scratch_shapes=[
            slots_scratch, pltpu.VMEM((NDP, 4 * GRAD_A, BLK), BF16), pltpu.SemaphoreType.DMA,
        ],
        compiler_params=pltpu.CompilerParams(vmem_limit_bytes=VMEM_LIMIT),
    )(meta, back_got, act, mid, lat, tok_t, give)
    grad, hd, part_down = pl.pallas_call(
        down_grads_body,
        out_shape=(grad_shape, slots, shape(BLK, RANK, dtype=F32)),
        in_specs=[smem] + [vmem] * 6 + [hbm],
        out_specs=(hbm, vmem, vmem),
        scratch_shapes=[
            slots_scratch, pltpu.VMEM((SLOTS, RANK, BLK), BF16),
            pltpu.VMEM((NDP, 4 * (GRAD - GRAD_A), BLK), BF16), pltpu.SemaphoreType.DMA,
        ],
        input_output_aliases={7: 0},
        compiler_params=pltpu.CompilerParams(vmem_limit_bytes=VMEM_LIMIT),
    )(meta, got, dlin, back_latent, cotangent, give, give2, grad)
    grad = lax.psum_scatter(
        grad.reshape(NDP * 4 * GRAD, BLK), ("x", "core"), scatter_dimension=0, tiled=True
    )
    part = jnp.concatenate([part_up, part_down], axis=1).astype(BF16)
    parts = spread(part, MP, NMP)
    acc = pltpu.VMEM((COLS, BLK, BLK), F32)
    token_part = call(
        token_part_body, (shape(NY, SHARE, BLK, BLK),) * 2, (gu, w_gu), (meta,), (acc,)
    )
    out_part = call(
        out_part_body, (shape(2, SHARE, BLK, BLK),) * NY, (hd, w_d), (meta,), (acc,)
    )
    parts, token_part, out_part = together((parts, token_part, out_part))
    latents, small = call(
        small_grads_body, (shape(2, BLK, RANK), shape(NDP, 32, BLK)),
        (parts, tok_t, cotangent, give2_plain), (meta,),
    )

    swap = [(0, 1), (1, 0)]
    token_came = lax.ppermute(token_part[1], "zl", swap)
    out_got = rotate(out_part)
    small = lax.all_to_all(small, DP, 0, 0, tiled=True)
    small = jnp.sum(small.astype(F32), axis=0).astype(BF16)
    small, grad, token_came, out_got = together((small, grad, token_came, out_got))
    grad = lax.all_to_all(grad.reshape(4, 4 * GRAD, BLK), "zh", 0, 0, tiled=True)
    half = shape(SHARE, BLK, BLK)
    token_got = rotate(call(token_pair_body, (half,) * NY, (token_part[0], token_came), ()))
    out_keep, out_give = call(out_y_body, (half,) * 2, out_got, (meta,))
    out_came = lax.ppermute(out_give, "zl", swap)
    low_g = small[:16]
    y, z = lax.axis_index("y"), lax.axis_index("zl")
    low_g = double(low_g, "zl", swap, z == 1)
    low_g = double(low_g, "y", [(0, 1), (1, 0), (2, 3), (3, 2)], y % 2 == 1)
    low_g = double(low_g, "y", [(0, 2), (2, 0), (1, 3), (3, 1)], y >= 2)
    low_g = low_g.reshape(NMP, 16, BLK)
    wide = shape(BLK, SHARE * BLK)
    token_grad = call(token_out_body, wide, (*token_got, latents, low_share), ())
    layer_out = call(layer_out_body, wide, (out_keep, out_came, latents, dlout), ())
    wide = shape(SLOTS, DEPTH, 4, BLK)
    gate_g, up_g, down_g, mid_g, tail = call(
        final_body, (wide, wide, wide, shape(4, SLOTS * BLK), shape(8, 4, BLK)),
        (grad.reshape(4, GRAD, 4, BLK),), (up_count, down_count, who),
        (pltpu.VMEM((GRAD, 4, BLK), BF16),),
    )
    dlin_g = tail.reshape(16, 2, BLK)[:SLOTS].transpose(1, 0, 2).reshape(2, SLOTS * BLK)
    low_g = jnp.concatenate([low_g[:, :, :RANK], low_g[:, :, RANK:]], axis=1)
    low_in_grad = low_g.reshape(2 * BLK, RANK)
    dlout_g = small[16:].reshape(SHARE, 2, BLK).transpose(1, 0, 2).reshape(2, SHARE * BLK)
    return layer_out, token_grad, gate_g, up_g, down_g, low_in_grad, mid_g, dlin_g, dlout_g


def solution(mesh):
    fine = Mesh(mesh.devices.reshape(4, 4, 2, 4, 2), DP + MP)
    rows, both, blocks = P(DP, None), P(DP, MP), P(MP, None, DP, None)
    in_specs = (rows, rows, blocks, blocks, blocks, rows, both, both, both) + (P(),) * 6
    out_specs = (both, both, blocks, blocks, blocks, rows, both, both, both)
    return jax.shard_map(local, mesh=fine, in_specs=in_specs, out_specs=out_specs, check_vma=False)
```

time: 270 us -> 210 us (0.78)
  waiting for transfers between devices: 84 us -> 29.3 us
  blocking collectives: 60.7 us -> 31 us
  starting transfers between devices: 33.3 us -> 48.9 us
  Pallas kernels: 50.4 us -> 60.3 us
    all_to_all x1 -> x0, blocking collectives: 30.2 us -> none  [local(): out_got = lax.all_to_all(out_part, MP, 0, 0, tiled=True)]
    all_gather x1, waiting for transfers between devices: 31.1 us -> 7.81 us  [local(): got_up = lax.all_gather(first.reshape(4 * PACK_A, BLK), DP)]
    all_to_all x1, waiting for transfers between devices: 22.9 us -> 0.01 us  [local(): back_got = lax.all_to_all(back_send, MP, 0, 0, tiled=True)]
    pallas_call x0 -> x2, Pallas kernels: none -> 17.3 us  [the longest x1 10.9 us: local(): pl.pallas_call(up_grads_body, out_shape=(grad_shape, shape(SLOTS, BLK, 2...]
    ppermute x0 -> x11, starting transfers between devices: none -> 16.6 us  [the longest x6 9.09 us: rotate(): lax.ppermute(parts[k], 'y', [(i, (i + k) % NY) for i in range(NY)])]
    all_to_all x1, waiting for transfers between devices: 12.1 us -> 0.01 us  [local(): got = lax.all_to_all(send, MP, 0, 0, tiled=True)]
    ppermute x0 -> x11, waiting for transfers between devices: none -> 10.7 us  [the longest x1 7.06 us: local(): out_came = lax.ppermute(out_give, 'zl', swap)]
    all_to_all x1, waiting for transfers between devices: 9.27 us -> 0.01 us  [local(): lax.all_to_all(grad.reshape(4, 4 * GRAD, BLK), 'zh', 0, 0, tiled=True)]
  transfers between devices with their start and end apart: 8 -> 19, of which waited for: 7 -> 5; matrix products, arithmetic and copies ran while one was open for 7% -> 7% of each run, Pallas kernels for 8% -> 24%
where the time goes in v2:
time: 210 us; the launch traced here: 208 us
  Pallas kernels  60.3 us (29%)
  starting transfers between devices  48.9 us (23%)
  blocking collectives  31 us (15%)
  waiting for transfers between devices  29.3 us (14%)
  local copies, waits for them, and re-layouts  18.3 us (9%)
  between operations  14.5 us (7%)
  other arithmetic  6.11 us (3%)
    pallas_call x11, Pallas kernels, call(): pl.pallas_call(body, out_shape=out_shapes, in_specs=[smem] * len(scalars)...  43 us
    all_to_all x1, blocking collectives, local(): small = lax.all_to_all(small, DP, 0, 0, tiled=True)  24.9 us
    all_to_all x3, starting transfers between devices, spread(): lax.all_to_all(jnp.broadcast_to(x[None], (n,) + x.shape), axis, 0, 0, til...  17.9 us
    pallas_call x1, Pallas kernels, local(): pl.pallas_call(up_grads_body, out_shape=(grad_shape, shape(SLOTS, BLK, 2...  10.9 us
    all_to_all x3, waiting for transfers between devices, spread(): lax.all_to_all(jnp.broadcast_to(x[None], (n,) + x.shape), axis, 0, 0, til...  10.7 us
    unnamed x43, local copies, waits for them, and re-layouts  9.47 us
    ppermute x6, starting transfers between devices, rotate(): lax.ppermute(parts[k], 'y', [(i, (i + k) % NY) for i in range(NY)])  9.09 us
    all_gather x1, waiting for transfers between devices, local(): got_up = lax.all_gather(first.reshape(4 * PACK_A, BLK), DP)  7.81 us
  transfers between devices with their start and end apart: 19, of which 5 were waited for; matrix products, arithmetic and copies ran while one was open for 7% of the time, Pallas kernels for 24%

profile of v2, /device:TPU:64, one launch (start us, length us, event | category | flops | bytes accessed | tf_op | source)
XLA Modules:
  0.0 208.4 jit_solution(9835673309261539066)
XLA Ops:
  13.7 8.1 %all-to-all-start = ((bf16[4,1,224,128]{3,2,1,0:T(8,128)(2,1)}), bf16[4,1,224,128]{3,2,1,0:T(8,128)(2,1)S(1)}, u32[]{:S(2)}, u32[]{:S(2)}) async-start(bf16[4,1,224,128]{3,2,1,0:T(8,128)(2,1)} %broadcast_in_dim.177), calls=%async_computation | async-start | bytes 458752 | tf_op jit(solution)/shard_map/all_to_all | solution.py:464
  21.8 4.1 %copy.60 = bf16[128,8192]{0,1:T(8,128)(2,1)} copy(bf16[128,8192]{1,0:T(8,128)(2,1)} %tok.1) | data formatting | bytes 4194304 | tf_op args[0]
  32.4 4.3 %all-to-all-start.1 = ((bf16[4,4,224,128]{3,2,1,0:T(8,128)(2,1)}), bf16[4,4,224,128]{3,2,1,0:T(8,128)(2,1)S(1)}, u32[]{:S(2)}, u32[]{:S(2)}) async-start(bf16[4,4,224,128]{3,2,1,0:T(8,128)(2,1)} %broadcast_in_dim.178), calls=%async_computation.1 | async-start | bytes 1835008 | tf_op jit(solution)/shard_map/all_to_all | solution.py:464
  39.4 9.7 %all-to-all-done.1 = bf16[4,4,224,128]{3,2,1,0:T(8,128)(2,1)S(1)} async-done(((bf16[4,4,224,128]{3,2,1,0:T(8,128)(2,1)}), bf16[4,4,224,128]{3,2,1,0:T(8,128)(2,1)S(1)}, u32[]{:S(2)}, u32[]{:S(2)}) %all-to-all-start.1) | async-done | bytes 917536 | tf_op jit(solution)/shard_map/all_to_all | solution.py:464
  49.4 6.1 %all_to_all.40 = bf16[2,16,224,128]{3,2,1,0:T(8,128)(2,1)} all-to-all(bf16[2,16,224,128]{3,2,1,0:T(8,128)(2,1)S(1)} %broadcast_in_dim.196), channel_id=1, replica_groups=mesh['zh'=4,'x'=4,'core'=2,'y'=4,'zl'=2] {'core'}, dimensions={0} | all-to-all | bytes 3670016 | tf_op jit(solution)/shard_map/all_to_all | solution.py:464
  55.5 6.6 %shard_map.215 = (bf16[8,512,128]{2,1,0:T(8,128)(2,1)}, bf16[43,128,128]{2,1,0:T(8,128)(2,1)}, bf16[14,64,128]{2,1,0:T(8,128)(2,1)}, bf16[512,128]{1,0:T(8,128)(2,1)}) custom-call(s32[560]{0:T(1024)} %concatenate.27.meta, bf16[32,224,128]{2,1,0:T(8,128)(2,1)} %bitcast.42, bf16[128,8192]{1,0:T(8,128)(2,1)} %cot.5, bf16[512,512]{1,0:T(8,128)(2,1)} %get-tuple-element.217.perm, ...), custom_call_target="tpu_custom_call" | custom-call | tf_op jit(solution)/shard_map/pallas_call | solution.py:54
  62.1 5.2 %all-to-all-start.3 = ((bf16[8,512,128]{2,1,0:T(8,128)(2,1)}), bf16[8,512,128]{2,1,0:T(8,128)(2,1)S(1)}, u32[]{:S(2)}, u32[]{:S(2)}) async-start(bf16[8,512,128]{2,1,0:T(8,128)(2,1)} %get-tuple-element.91), calls=%async_computation.3 | async-start | bytes 2097152 | tf_op jit(solution)/shard_map/all_to_all | solution.py:529
  67.3 7.8 %all-gather.2.cloned.1.call-done.got = bf16[32,528,128]{2,1,0:T(8,128)(2,1)} async-done(((bf16[1,528,128]{2,1,0:T(8,128)(2,1)}), bf16[32,528,128]{2,1,0:T(8,128)(2,1)}) %all-gather.2.cloned.1.call-update) | async-done | bytes 4325392 | tf_op jit(solution)/shard_map/all_gather | solution.py:505
  75.1 10.3 %shard_map.216 = (bf16[8,2,128,128]{3,2,1,0:T(8,128)(2,1)}, f32[14,128,256]{2,1,0:T(8,128)}, bf16[43,128,256]{2,1,0:T(8,128)(2,1)}, bf16[14,128,128]{2,1,0:T(8,1...) custom-call(s32[560]{0:T(1024)} %concatenate.27.meta, ...), custom_call_target="tpu_custom_call" | custom-call | tf_op jit(solution)/shard_map/pallas_call | solution.py:54
  85.4 4.5 %all-to-all-start.4 = ((bf16[8,2,128,128]{3,2,1,0:T(8,128)(2,1)}), bf16[8,2,128,128]{3,2,1,0:T(8,128)(2,1)S(1)}, u32[]{:S(2)}, u32[]{:S(2)}) async-start(bf16[8,2,128,128]{3,2,1,0:T(8,128)(2,1)} %get-tuple-element.100), calls=%async_computation.4 | async-start | bytes 1048576 | tf_op jit(solution)/shard_map/all_to_all | solution.py:539
  90.2 10.9 %shard_map.217 = (bf16[32,608,128]{2,1,0:T(8,128)(2,1)}, bf16[14,128,256]{2,1,0:T(8,128)(2,1)}, f32[128,64]{1,0:T(8,128)}, bf16[128,64]{1,0:T(8,128)(2,1)}) custom-call(s32[560]{0:T(1024)} %concatenate.27.meta, bf16[8,512,128]{2,1,0:T(8,128)(2,1)} %copy-done, f32[14,128,256]{2,1,0:T(8,128)} %get-tuple-element.94.act, ...), custom_call_target="tpu_custom_call" | custom-call | tf_op jit(solution)/shard_map/pallas_call | solution.py:545
  102.0 6.4 %shard_map.218 = (bf16[32,608,128]{2,1,0:T(8,128)(2,1)}, bf16[14,128,128]{2,1,0:T(8,128)(2,1)}, f32[128,64]{1,0:T(8,128)}) custom-call(s32[560]{0:T(1024)} %concatenate.27.meta, bf16[8,2,128,128]{3,2,1,0:T(8,128)(2,1)} %copy-done.2, bf16[14,64,128]{2,1,0:T(8,128)(2,1)} %get-tuple-element.101.dlin, ...), custom_call_target="tpu_custom_call", output_to_operand_aliasing={{0}: (7, {})} | custom-call | tf_op jit(solution)/shard_map/pallas_call | solution.py:557
  110.0 5.5 %all-to-all-start.5 = ((bf16[8,128,128]{2,1,0:T(8,128)(2,1)}), bf16[8,128,128]{2,1,0:T(8,128)(2,1)S(1)}, u32[]{:S(2)}, u32[]{:S(2)}) async-start(bf16[8,128,128]{2,1,0:T(8,128)(2,1)} %broadcast_in_dim.197), calls=%async_computation.5 | async-start | bytes 524288 | tf_op jit(solution)/shard_map/all_to_all | solution.py:464
  115.5 4.6 %shard_map.219 = (bf16[4,8,128,128]{3,2,1,0:T(8,128)(2,1)}, bf16[4,8,128,128]{3,2,1,0:T(8,128)(2,1)}) custom-call(s32[560]{0:T(1024)} %concatenate.27.meta, bf16[14,128,256]{2,1,0:T(8,128)(2,1)} %get-tuple-element.106.gu, bf16[43,128,256]{2,1,0:T(8,128)(2,1)} %get-tuple-element.107.w_gu), custom_call_target="tpu_custom_call" | custom-call | tf_op jit(solution)/shard_map/pallas_call | solution.py:54
  120.1 3.9 %shard_map.220 = (bf16[2,8,128,128]{3,2,1,0:T(8,128)(2,1)}, bf16[2,8,128,128]{3,2,1,0:T(8,128)(2,1)}, bf16[2,8,128,128]{3,2,1,0:T(8,128)(2,1)}, bf16[2,8,128,128]{3,2,1,0:T(8,128)(2,1)}) custom-call(s32[560]{0:T(1024)} %concatenate.27.meta, bf16[14,128,128]{2,1,0:T(8,128)(2,1)} %get-tuple-element.110.hd, bf16[43,128,128]{2,1,0:T(8,128)(2,1)} %get-tuple-element.111.w_d), custom_call_target="tpu_custom_call" | custom-call | tf_op jit(solution)/shard_map/pallas_call | solution.py:54
  127.4 2.7 %collective-permute-start.2 = (bf16[2,8,128,128]{3,2,1,0:T(8,128)(2,1)}, bf16[2,8,128,128]{3,2,1,0:T(8,128)(2,1)S(1)}, u32[]{:S(2)}, u32[]{:S(2)}) collective-permute-start(bf16[2,8,128,128]{3,2,1,0:T(8,128)(2,1)} %get-tuple-element.123), channel_id=1, source_target_pairs={{0,4},{2,6},{4,0},{6,2},{1,5},{3,7},{5,1},{7,3},{8,12},{10,14},{12... | collective-permute-start | bytes 1572872 | tf_op jit(solution)/shard_map/ppermute | solution.py:478
  131.6 3.7 %shard_map.221 = (bf16[2,128,64]{2,1,0:T(8,128)(2,1)}, bf16[32,32,128]{2,1,0:T(8,128)(2,1)}) custom-call(s32[560]{0:T(1024)} %concatenate.27.meta, bf16[8,128,128]{2,1,0:T(8,128)(2,1)} %copy-done.3, bf16[64,128,128]{2,1,0:T(8,128)(2,1)} %bitcast.41, bf16[128,8192]{1,0:T(8,128)(2,1)} %cot.5, bf16[512,512]{1,0:T(8,128)(2,1)} %get-tuple-element.117.perm2), custom_call_target="tpu_custom_call" | custom-call | tf_op jit(solution)/shard_map/pallas_call | solution.py:54
  135.3 24.9 %all_to_all.41 = bf16[32,32,128]{2,1,0:T(8,128)(2,1)S(1)} all-to-all(bf16[32,32,128]{2,1,0:T(8,128)(2,1)} %get-tuple-element.118), channel_id=1, replica_groups=mesh['zh'=4,'x'=4,'core'=2,'y'=4,'zl'=2] {'zh','x','core'}, dimensions={0} | all-to-all | bytes 524288 | tf_op jit(solution)/shard_map/all_to_all | solution.py:590
  160.7 3.6 %collective-permute-done.8 = bf16[16,128]{1,0:T(8,128)(2,1)S(1)} collective-permute-done((bf16[16,128]{1,0:T(8,128)(2,1)S(1)}, bf16[16,128]{1,0:T(8,128)(2,1)S(1)}, u32[]{:S(2)}, u32[]{:S(2)}) %collective-permute-start.8) | collective-permute-done | bytes 4128 | tf_op jit(solution)/shard_map/ppermute | solution.py:484
  166.4 4.5 %all-to-all-start.7 = ((bf16[4,608,128]{2,1,0:T(8,128)(2,1)}), bf16[4,608,128]{2,1,0:T(8,128)(2,1)S(1)}, u32[]{:S(2)}, u32[]{:S(2)}) async-start(bf16[4,608,128]{2,1,0:T(8,128)(2,1)} %bitcast.46), calls=%async_computation.8 | async-start | bytes 1245184 | tf_op jit(solution)/shard_map/all_to_all | solution.py:593
  170.8 2.8 %collective-permute-start.10 = (bf16[64,128]{1,0:T(8,128)(2,1)S(1)}, bf16[64,128]{1,0:T(8,128)(2,1)S(1)}, u32[]{:S(2)}, u32[]{:S(2)}) collective-permute-start(bf16[64,128]{1,0:T(8,128)(2,1)S(1)} %pad_maximum_fusion.4), channel_id=1, source_target_pairs={{0,4},{4,0},{2,6},{6,2},{1,5},{5,1},{3,7},{7,3},{8,12},{12,8},{10,... | collective-permute-start | bytes 49160 | tf_op jit(solution)/shard_map/ppermute | solution.py:484
  173.6 2.6 %shard_map.224 = (bf16[8,128,128]{2,1,0:T(8,128)(2,1)}, bf16[8,128,128]{2,1,0:T(8,128)(2,1)}, bf16[8,128,128]{2,1,0:T(8,128)(2,1)}, bf16[8,128,128]{2,1,0:T(8,128)(2,1)}) custom-call(bf16[4,8,128,128]{3,2,1,0:T(8,128)(2,1)} %get-tuple-element.133.keep, bf16[4,8,128,128]{3,2,1,0:T(8,128)(2,1)} %copy-done.4), custom_call_target="tpu_custom_call" | custom-call | tf_op jit(solution)/shard_map/pallas_call | solution.py:54
  179.7 2.5 %shard_map.222 = (bf16[8,128,128]{2,1,0:T(8,128)(2,1)}, bf16[8,128,128]{2,1,0:T(8,128)(2,1)}) custom-call(s32[560]{0:T(1024)} %concatenate.27.meta, bf16[2,8,128,128]{3,2,1,0:T(8,128)(2,1)} %get-tuple-element.125.refs_0_, bf16[2,8,128,128]{3,2,1,0:T(8,128)(2,1)} %copy-done.5, bf16[2,8,128,128]{3,2,1,0:T(8,128)(2,1)} %copy-done.6, ...), custom_call_target="tpu_custom_call" | custom-call | tf_op jit(solution)/shard_map/pallas_call | solution.py:54
  184.0 7.1 %collective-permute-done.4.came = bf16[8,128,128]{2,1,0:T(8,128)(2,1)S(1)} collective-permute-done((bf16[8,128,128]{2,1,0:T(8,128)(2,1)}, bf16[8,128,128]{2,1,0:T(8,128)(2,1)S(1)}, u32[]{:S(2)}, u32[]{:S(2)}) %collective-permute-start.4) | collective-permute-done | bytes 262176 | tf_op jit(solution)/shard_map/ppermute | solution.py:597
  (150 shorter events, 41.7 us)
Async XLA Ops:
  7.2 68.0 %all-gather.2.cloned.1.call-start = ((), (), s32[]{:S(2)}) async-start(), calls=%async_computation.9 | async-start | bytes 4460544 | tf_op jit(solution)/shard_map/all_gather | solution.py:505
  13.7 17.0 %all-to-all-start = ((bf16[4,1,224,128]{3,2,1,0:T(8,128)(2,1)}), bf16[4,1,224,128]{3,2,1,0:T(8,128)(2,1)S(1)}, u32[]{:S(2)}, u32[]{:S(2)}) async-start(bf16[4,1,224,128]{3,2,1,0:T(8,128)(2,1)} %broadcast_in_dim.177), calls=%async_computation | async-start | bytes 458752 | tf_op jit(solution)/shard_map/all_to_all | solution.py:464
  28.3 9.5 %copy-start.15 = (s32[112,5]{0,1:T(8,128)S(1)}, s32[112,5]{0,1:T(8,128)}, u32[]{:S(2)}) copy-start(s32[112,5]{0,1:T(8,128)} %param.26) | copy-start | bytes 6724
  32.4 16.7 %all-to-all-start.1 = ((bf16[4,4,224,128]{3,2,1,0:T(8,128)(2,1)}), bf16[4,4,224,128]{3,2,1,0:T(8,128)(2,1)S(1)}, u32[]{:S(2)}, u32[]{:S(2)}) async-start(bf16[4,4,224,128]{3,2,1,0:T(8,128)(2,1)} %broadcast_in_dim.178), calls=%async_computation.1 | async-start | bytes 1835008 | tf_op jit(solution)/shard_map/all_to_all | solution.py:464
  62.1 23.3 %all-to-all-start.3 = ((bf16[8,512,128]{2,1,0:T(8,128)(2,1)}), bf16[8,512,128]{2,1,0:T(8,128)(2,1)S(1)}, u32[]{:S(2)}, u32[]{:S(2)}) async-start(bf16[8,512,128]{2,1,0:T(8,128)(2,1)} %get-tuple-element.91), calls=%async_computation.3 | async-start | bytes 2097152 | tf_op jit(solution)/shard_map/all_to_all | solution.py:529
  85.4 15.7 %all-to-all-start.4 = ((bf16[8,2,128,128]{3,2,1,0:T(8,128)(2,1)}), bf16[8,2,128,128]{3,2,1,0:T(8,128)(2,1)S(1)}, u32[]{:S(2)}, u32[]{:S(2)}) async-start(bf16[8,2,128,128]{3,2,1,0:T(8,128)(2,1)} %get-tuple-element.100), calls=%async_computation.4 | async-start | bytes 1048576 | tf_op jit(solution)/shard_map/all_to_all | solution.py:539
  90.0 70.4 %reduce-scatter.2.cloned.1.call-start = ((), (), s32[]{:S(2)}) async-start(), calls=%async_computation.10 | async-start | bytes 5603328 | tf_op jit(solution)/shard_map/reduce_scatter | solution.py:569
  110.0 13.9 %all-to-all-start.5 = ((bf16[8,128,128]{2,1,0:T(8,128)(2,1)}), bf16[8,128,128]{2,1,0:T(8,128)(2,1)S(1)}, u32[]{:S(2)}, u32[]{:S(2)}) async-start(bf16[8,128,128]{2,1,0:T(8,128)(2,1)} %broadcast_in_dim.197), calls=%async_computation.5 | async-start | bytes 524288 | tf_op jit(solution)/shard_map/all_to_all | solution.py:464
  124.0 36.4 %collective-permute-start = (bf16[4,8,128,128]{3,2,1,0:T(8,128)(2,1)}, bf16[4,8,128,128]{3,2,1,0:T(8,128)(2,1)S(1)}, u32[]{:S(2)}, u32[]{:S(2)}) collective-permute-start(bf16[4,8,128,128]{3,2,1,0:T(8,128)(2,1)} %get-tuple-element.120), channel_id=1, source_target_pairs={{0,1},{1,0},{2,3},{3,2},{4,5},{5,4},{6,7},{7,6},{8,9},{9,8},{10,11... | collective-permute-start | bytes 3145736 | tf_op jit(solution)/shard_map/ppermute | solution.py:588
  126.0 34.3 %collective-permute-start.1 = (bf16[2,8,128,128]{3,2,1,0:T(8,128)(2,1)}, bf16[2,8,128,128]{3,2,1,0:T(8,128)(2,1)S(1)}, u32[]{:S(2)}, u32[]{:S(2)}) collective-permute-start(bf16[2,8,128,128]{3,2,1,0:T(8,128)(2,1)} %get-tuple-element.122), channel_id=1, source_target_pairs={{0,2},{2,4},{4,6},{6,0},{1,3},{3,5},{5,7},{7,1},{8,10},{10,12},{12... | collective-permute-start | bytes 1572872 | tf_op jit(solution)/shard_map/ppermute | solution.py:478
  127.4 32.8 %collective-permute-start.2 = (bf16[2,8,128,128]{3,2,1,0:T(8,128)(2,1)}, bf16[2,8,128,128]{3,2,1,0:T(8,128)(2,1)S(1)}, u32[]{:S(2)}, u32[]{:S(2)}) collective-permute-start(bf16[2,8,128,128]{3,2,1,0:T(8,128)(2,1)} %get-tuple-element.123), channel_id=1, source_target_pairs={{0,4},{2,6},{4,0},{6,2},{1,5},{3,7},{5,1},{7,3},{8,12},{10,14},{12... | collective-permute-start | bytes 1572872 | tf_op jit(solution)/shard_map/ppermute | solution.py:478
  130.1 30.2 %collective-permute-start.3 = (bf16[2,8,128,128]{3,2,1,0:T(8,128)(2,1)}, bf16[2,8,128,128]{3,2,1,0:T(8,128)(2,1)S(1)}, u32[]{:S(2)}, u32[]{:S(2)}) collective-permute-start(bf16[2,8,128,128]{3,2,1,0:T(8,128)(2,1)} %get-tuple-element.124), channel_id=1, source_target_pairs={{0,6},{2,0},{4,2},{6,4},{1,7},{3,1},{5,3},{7,5},{8,14},{10,8},{12,... | collective-permute-start | bytes 1572872 | tf_op jit(solution)/shard_map/ppermute | solution.py:478
  160.3 19.4 %copy-start.5 = (bf16[2,8,128,128]{3,2,1,0:T(8,128)(2,1)}, bf16[2,8,128,128]{3,2,1,0:T(8,128)(2,1)S(1)}, u32[]{:S(2)}) copy-start(bf16[2,8,128,128]{3,2,1,0:T(8,128)(2,1)S(1)} %collective-permute-done.1.refs_1_) | copy-start | bytes 1572868
  160.3 19.4 %copy-start.6 = (bf16[2,8,128,128]{3,2,1,0:T(8,128)(2,1)}, bf16[2,8,128,128]{3,2,1,0:T(8,128)(2,1)S(1)}, u32[]{:S(2)}) copy-start(bf16[2,8,128,128]{3,2,1,0:T(8,128)(2,1)S(1)} %collective-permute-done.2.refs_2_) | copy-start | bytes 1572868
  160.3 19.4 %copy-start.7 = (bf16[2,8,128,128]{3,2,1,0:T(8,128)(2,1)}, bf16[2,8,128,128]{3,2,1,0:T(8,128)(2,1)S(1)}, u32[]{:S(2)}) copy-start(bf16[2,8,128,128]{3,2,1,0:T(8,128)(2,1)S(1)} %collective-permute-done.3.refs_3_) | copy-start | bytes 1572868
  160.3 13.3 %copy-start.4 = (bf16[4,8,128,128]{3,2,1,0:T(8,128)(2,1)}, bf16[4,8,128,128]{3,2,1,0:T(8,128)(2,1)S(1)}, u32[]{:S(2)}) copy-start(bf16[4,8,128,128]{3,2,1,0:T(8,128)(2,1)S(1)} %collective-permute-done.came) | copy-start | bytes 3145732
  160.4 3.9 %collective-permute-start.8 = (bf16[16,128]{1,0:T(8,128)(2,1)S(1)}, bf16[16,128]{1,0:T(8,128)(2,1)S(1)}, u32[]{:S(2)}, u32[]{:S(2)}) collective-permute-start(bf16[16,128]{1,0:T(8,128)(2,1)S(1)} %slice.26), channel_id=1, source_target_pairs={{0,1},{1,0},{2,3},{3,2},{4,5},{5,4},{6,7},{7,6},{8,9},{9,8},{10,11... | collective-permute-start | bytes 12296 | tf_op jit(solution)/shard_map/ppermute | solution.py:484
  164.9 5.9 %collective-permute-start.9 = (bf16[32,128]{1,0:T(8,128)(2,1)S(1)}, bf16[32,128]{1,0:T(8,128)(2,1)S(1)}, u32[]{:S(2)}, u32[]{:S(2)}) collective-permute-start(bf16[32,128]{1,0:T(8,128)(2,1)S(1)} %pad_maximum_fusion.5), channel_id=1, source_target_pairs={{0,2},{2,0},{4,6},{6,4},{1,3},{3,1},{5,7},{7,5},{8,10},{10,8},{12,... | collective-permute-start | bytes 24584 | tf_op jit(solution)/shard_map/ppermute | solution.py:484
  166.4 30.6 %all-to-all-start.7 = ((bf16[4,608,128]{2,1,0:T(8,128)(2,1)}), bf16[4,608,128]{2,1,0:T(8,128)(2,1)S(1)}, u32[]{:S(2)}, u32[]{:S(2)}) async-start(bf16[4,608,128]{2,1,0:T(8,128)(2,1)} %bitcast.46), calls=%async_computation.8 | async-start | bytes 1245184 | tf_op jit(solution)/shard_map/all_to_all | solution.py:593
  170.8 12.3 %collective-permute-start.10 = (bf16[64,128]{1,0:T(8,128)(2,1)S(1)}, bf16[64,128]{1,0:T(8,128)(2,1)S(1)}, u32[]{:S(2)}, u32[]{:S(2)}) collective-permute-start(bf16[64,128]{1,0:T(8,128)(2,1)S(1)} %pad_maximum_fusion.4), channel_id=1, source_target_pairs={{0,4},{4,0},{2,6},{6,2},{1,5},{5,1},{3,7},{7,3},{8,12},{12,8},{10,... | collective-permute-start | bytes 49160 | tf_op jit(solution)/shard_map/ppermute | solution.py:484
  176.2 17.6 %collective-permute-start.5 = (bf16[8,128,128]{2,1,0:T(8,128)(2,1)}, bf16[8,128,128]{2,1,0:T(8,128)(2,1)S(1)}, u32[]{:S(2)}, u32[]{:S(2)}) collective-permute-start(bf16[8,128,128]{2,1,0:T(8,128)(2,1)} %get-tuple-element.136), channel_id=1, source_target_pairs={{0,2},{2,4},{4,6},{6,0},{1,3},{3,5},{5,7},{7,1},{8,10},{10,12},{12... | collective-permute-start | bytes 786440 | tf_op jit(solution)/shard_map/ppermute | solution.py:478
  176.4 17.3 %collective-permute-start.6 = (bf16[8,128,128]{2,1,0:T(8,128)(2,1)}, bf16[8,128,128]{2,1,0:T(8,128)(2,1)S(1)}, u32[]{:S(2)}, u32[]{:S(2)}) collective-permute-start(bf16[8,128,128]{2,1,0:T(8,128)(2,1)} %get-tuple-element.137), channel_id=1, source_target_pairs={{0,4},{2,6},{4,0},{6,2},{1,5},{3,7},{5,1},{7,3},{8,12},{10,14},{12... | collective-permute-start | bytes 786440 | tf_op jit(solution)/shard_map/ppermute | solution.py:478
  178.2 15.6 %collective-permute-start.7 = (bf16[8,128,128]{2,1,0:T(8,128)(2,1)}, bf16[8,128,128]{2,1,0:T(8,128)(2,1)S(1)}, u32[]{:S(2)}, u32[]{:S(2)}) collective-permute-start(bf16[8,128,128]{2,1,0:T(8,128)(2,1)} %get-tuple-element.138), channel_id=1, source_target_pairs={{0,6},{2,0},{4,2},{6,4},{1,7},{3,1},{5,3},{7,5},{8,14},{10,8},{12,... | collective-permute-start | bytes 786440 | tf_op jit(solution)/shard_map/ppermute | solution.py:478
  182.2 8.9 %collective-permute-start.4 = (bf16[8,128,128]{2,1,0:T(8,128)(2,1)}, bf16[8,128,128]{2,1,0:T(8,128)(2,1)S(1)}, u32[]{:S(2)}, u32[]{:S(2)}) collective-permute-start(bf16[8,128,128]{2,1,0:T(8,128)(2,1)} %get-tuple-element.130), channel_id=1, source_target_pairs={{0,1},{1,0},{2,3},{3,2},{4,5},{5,4},{6,7},{7,6},{8,9},{9,8},{10,11... | collective-permute-start | bytes 786440 | tf_op jit(solution)/shard_map/ppermute | solution.py:597
  (15 other events, 51.5 us)
Sparse Core Ops, SparseCore 0:
  12.3 62.8 all-gather.1
  108.5 43.6 reduce-scatter.1

commit v3 on v2

--- a/solution.py
+++ b/solution.py
@@ -327,7 +327,8 @@
     latents[1] = total[:, RANK:]
     who = meta[WHO]
     rows = pl.ds(pl.multiple_of((who % 4) * 32, 32), 32)
-    pieces = [tok_t[2 * d + who // 4, rows, :] for d in range(NDP)]
+    order = [(q % 4) * 8 + q // 4 for q in range(NDP)]
+    pieces = [tok_t[2 * d + who // 4, rows, :] for d in order]
     low = dot(jnp.concatenate(pieces, axis=0), total[:, :RANK]).reshape(NDP, 32, RANK)
     low = jnp.concatenate([low[:, :16], low[:, 16:]], axis=2)
     grad[:, :16, :] = low.astype(BF16)
@@ -361,9 +362,9 @@
 
 
 def final_body(up_count, down_count, who, got, gate_o, up_o, down_o, mid_o, tail, red):
-    total = got[0].astype(F32)
+    total = got[0, :GRAD].astype(F32)
     for i in range(1, 4):
-        total = total + got[i].astype(F32)
+        total = total + got[i, :GRAD].astype(F32)
     red[...] = total.astype(BF16)
     mine = who[0] * SLOTS
     zero = jnp.zeros((4, BLK), BF16)
@@ -456,7 +457,7 @@
     into = lambda src: (src[None, :] == r[:, None]).astype(BF16)
     return (
         into(row4(plain)), into(row4(chain)), into(row2(chain)),
-        out(row4(give)), out(row2(give)), out(row2(plain)),
+        out(row4(give)), out(row2(give)),
     )
 
 
@@ -478,11 +479,6 @@
         lax.ppermute(parts[k], "y", [(i, (i + k) % NY) for i in range(NY)]) for k in range(1, NY)
     ]
     return [parts[0]] + moved
-
-
-def double(x, axis, pairs, upper):
-    came = lax.ppermute(x, axis, pairs)
-    return jnp.concatenate([jnp.where(upper, came, x), jnp.where(upper, x, came)], axis=0)
 
 
 def local(
@@ -508,7 +504,7 @@
     got_down, ids = together((got_down, ids))
     got_down = gather_step(got_down, "x", 4)
     meta = tables(*ids)
-    take, take_c, take2_c, give, give2, give2_plain = permutations()
+    take, take_c, take2_c, give, give2 = permutations()
     got_down, meta = together((got_down, meta))
     got_down = gather_step(got_down, "core", 2)
     tok_t = tokens.reshape(BLK, COLS, BLK).transpose(1, 2, 0)
@@ -516,7 +512,7 @@
     slots = shape(SLOTS, BLK, BLK)
     slots_scratch = pltpu.VMEM((SLOTS, BLK, BLK), BF16)
     parcel = shape(NMP, CAP, BLK, BLK)
-    got_down, take, give, give2, give2_plain = together((got_down, take, give, give2, give2_plain))
+    got_down, take, give, give2 = together((got_down, take, give, give2))
     back_send, w_d, dlin, dlout = call(
         hidden_grad_body,
         (
@@ -581,33 +577,30 @@
     parts, token_part, out_part = together((parts, token_part, out_part))
     latents, small = call(
         small_grads_body, (shape(2, BLK, RANK), shape(NDP, 32, BLK)),
-        (parts, tok_t, cotangent, give2_plain), (meta,),
+        (parts, tok_t, cotangent, give2), (meta,),
     )
 
     swap = [(0, 1), (1, 0)]
     token_came = lax.ppermute(token_part[1], "zl", swap)
     out_got = rotate(out_part)
-    small = lax.all_to_all(small, DP, 0, 0, tiled=True)
-    small = jnp.sum(small.astype(F32), axis=0).astype(BF16)
+    small = lax.all_to_all(small.reshape(8, BLK, BLK), ("x", "core"), 0, 0, tiled=True)
+    small = jnp.sum(small.astype(F32), axis=0).astype(BF16).reshape(4, 32, BLK)
     small, grad, token_came, out_got = together((small, grad, token_came, out_got))
-    grad = lax.all_to_all(grad.reshape(4, 4 * GRAD, BLK), "zh", 0, 0, tiled=True)
+    grad = jnp.concatenate([grad.reshape(4, 4 * GRAD, BLK), small], axis=1)
+    grad = lax.all_to_all(grad, "zh", 0, 0, tiled=True)
+    small = jnp.sum(grad[:, 4 * GRAD :].astype(F32), axis=0).astype(BF16)
     half = shape(SHARE, BLK, BLK)
     token_got = rotate(call(token_pair_body, (half,) * NY, (token_part[0], token_came), ()))
     out_keep, out_give = call(out_y_body, (half,) * 2, out_got, (meta,))
     out_came = lax.ppermute(out_give, "zl", swap)
-    low_g = small[:16]
-    y, z = lax.axis_index("y"), lax.axis_index("zl")
-    low_g = double(low_g, "zl", swap, z == 1)
-    low_g = double(low_g, "y", [(0, 1), (1, 0), (2, 3), (3, 2)], y % 2 == 1)
-    low_g = double(low_g, "y", [(0, 2), (2, 0), (1, 3), (3, 1)], y >= 2)
-    low_g = low_g.reshape(NMP, 16, BLK)
+    low_g = spread(small[:16], MP, NMP)
     wide = shape(BLK, SHARE * BLK)
     token_grad = call(token_out_body, wide, (*token_got, latents, low_share), ())
     layer_out = call(layer_out_body, wide, (out_keep, out_came, latents, dlout), ())
     wide = shape(SLOTS, DEPTH, 4, BLK)
     gate_g, up_g, down_g, mid_g, tail = call(
         final_body, (wide, wide, wide, shape(4, SLOTS * BLK), shape(8, 4, BLK)),
-        (grad.reshape(4, GRAD, 4, BLK),), (up_count, down_count, who),
+        (grad.reshape(4, GRAD + 8, 4, BLK),), (up_count, down_count, who),
         (pltpu.VMEM((GRAD, 4, BLK), BF16),),
     )
     dlin_g = tail.reshape(16, 2, BLK)[:SLOTS].transpose(1, 0, 2).reshape(2, SLOTS * BLK)

time: 210 us -> 207 us (0.986)
  blocking collectives: 31 us -> 20.2 us
  starting transfers between devices: 48.9 us -> 53.8 us
    all_to_all x1, blocking collectives: 24.9 us -> 14.1 us  [local(): lax.all_to_all(small.reshape(8, BLK, BLK), ('x', 'core'), 0, 0, tiled=True)]
    ppermute x1, waiting for transfers between devices: 7.06 us -> 0.01 us  [local(): out_came = lax.ppermute(out_give, 'zl', swap)]
    all_to_all x1, waiting for transfers between devices: 0.01 us -> 5.85 us  [local(): grad = lax.all_to_all(grad, 'zh', 0, 0, tiled=True)]
    all_to_all x3 -> x4, starting transfers between devices: 17.9 us -> 22.4 us  [spread(): lax.all_to_all(jnp.broadcast_to(x[None], (n,) + x.shape), axis, 0, 0, til...]
    ppermute x3 -> x0, starting transfers between devices: 4.53 us -> none  [double(): came = lax.ppermute(x, axis, pairs)]
    ppermute x3 -> x0, waiting for transfers between devices: 3.6 us -> none  [double(): came = lax.ppermute(x, axis, pairs)]
    ppermute x6, waiting for transfers between devices: 0.02 us -> 3.01 us  [rotate(): lax.ppermute(parts[k], 'y', [(i, (i + k) % NY) for i in range(NY)])]
    ppermute x6, starting transfers between devices: 9.09 us -> 12 us  [rotate(): lax.ppermute(parts[k], 'y', [(i, (i + k) % NY) for i in range(NY)])]
  transfers between devices with their start and end apart: 19 -> 17, of which waited for: 5 -> 6; matrix products, arithmetic and copies ran while one was open for 7% -> 8% of each run, Pallas kernels for 24% -> 25%
where the time goes in v3:
time: 207 us; the launch traced here: 204 us
  Pallas kernels  60.3 us (29%)
  starting transfers between devices  53.8 us (26%)
  waiting for transfers between devices  29.3 us (14%)
  blocking collectives  20.2 us (10%)
  local copies, waits for them, and re-layouts  18.7 us (9%)
  between operations  14.4 us (7%)
  other arithmetic  7.18 us (3%)
    pallas_call x11, Pallas kernels, call(): pl.pallas_call(body, out_shape=out_shapes, in_specs=[smem] * len(scalars)...  43 us
    all_to_all x4, starting transfers between devices, spread(): lax.all_to_all(jnp.broadcast_to(x[None], (n,) + x.shape), axis, 0, 0, til...  22.4 us
    all_to_all x1, blocking collectives, local(): lax.all_to_all(small.reshape(8, BLK, BLK), ('x', 'core'), 0, 0, tiled=True)  14.1 us
    ppermute x6, starting transfers between devices, rotate(): lax.ppermute(parts[k], 'y', [(i, (i + k) % NY) for i in range(NY)])  12 us
    pallas_call x1, Pallas kernels, local(): pl.pallas_call(up_grads_body, out_shape=(grad_shape, shape(SLOTS, BLK, 2...  11 us
    all_to_all x4, waiting for transfers between devices, spread(): lax.all_to_all(jnp.broadcast_to(x[None], (n,) + x.shape), axis, 0, 0, til...  10.9 us
    unnamed x43, local copies, waits for them, and re-layouts  8.61 us
    all_gather x1, waiting for transfers between devices, local(): got_up = lax.all_gather(first.reshape(4 * PACK_A, BLK), DP)  8.1 us
  transfers between devices with their start and end apart: 17, of which 6 were waited for; matrix products, arithmetic and copies ran while one was open for 8% of the time, Pallas kernels for 25%

profile of v3, /device:TPU:64, one launch (start us, length us, event | category | flops | bytes accessed | tf_op | source)
XLA Modules:
  0.0 204.0 jit_solution(3685982785915917971)
XLA Ops:
  13.7 8.1 %all-to-all-start = ((bf16[4,1,224,128]{3,2,1,0:T(8,128)(2,1)}), bf16[4,1,224,128]{3,2,1,0:T(8,128)(2,1)S(1)}, u32[]{:S(2)}, u32[]{:S(2)}) async-start(bf16[4,1,224,128]{3,2,1,0:T(8,128)(2,1)} %broadcast_in_dim.181), calls=%async_computation | async-start | bytes 458752 | tf_op jit(solution)/shard_map/all_to_all | solution.py:465
  21.8 4.1 %copy.60 = bf16[128,8192]{0,1:T(8,128)(2,1)} copy(bf16[128,8192]{1,0:T(8,128)(2,1)} %tok.1) | data formatting | bytes 4194304 | tf_op args[0]
  32.4 4.3 %all-to-all-start.1 = ((bf16[4,4,224,128]{3,2,1,0:T(8,128)(2,1)}), bf16[4,4,224,128]{3,2,1,0:T(8,128)(2,1)S(1)}, u32[]{:S(2)}, u32[]{:S(2)}) async-start(bf16[4,4,224,128]{3,2,1,0:T(8,128)(2,1)} %broadcast_in_dim.182), calls=%async_computation.1 | async-start | bytes 1835008 | tf_op jit(solution)/shard_map/all_to_all | solution.py:465
  39.4 9.6 %all-to-all-done.1 = bf16[4,4,224,128]{3,2,1,0:T(8,128)(2,1)S(1)} async-done(((bf16[4,4,224,128]{3,2,1,0:T(8,128)(2,1)}), bf16[4,4,224,128]{3,2,1,0:T(8,128)(2,1)S(1)}, u32[]{:S(2)}, u32[]{:S(2)}) %all-to-all-start.1) | async-done | bytes 917536 | tf_op jit(solution)/shard_map/all_to_all | solution.py:465
  49.3 6.1 %all_to_all.45 = bf16[2,16,224,128]{3,2,1,0:T(8,128)(2,1)} all-to-all(bf16[2,16,224,128]{3,2,1,0:T(8,128)(2,1)S(1)} %broadcast_in_dim.200), channel_id=1, replica_groups=mesh['zh'=4,'x'=4,'core'=2,'y'=4,'zl'=2] {'core'}, dimensions={0} | all-to-all | bytes 3670016 | tf_op jit(solution)/shard_map/all_to_all | solution.py:465
  55.4 6.6 %shard_map.215 = (bf16[8,512,128]{2,1,0:T(8,128)(2,1)}, bf16[43,128,128]{2,1,0:T(8,128)(2,1)}, bf16[14,64,128]{2,1,0:T(8,128)(2,1)}, bf16[512,128]{1,0:T(8,128)(2,1)}) custom-call(s32[560]{0:T(1024)} %concatenate.21.meta, bf16[32,224,128]{2,1,0:T(8,128)(2,1)} %bitcast.43, bf16[128,8192]{1,0:T(8,128)(2,1)} %cot.5, bf16[512,512]{1,0:T(8,128)(2,1)} %get-tuple-element.208.perm, ...), custom_call_target="tpu_custom_call" | custom-call | tf_op jit(solution)/shard_map/pallas_call | solution.py:54
  62.0 5.1 %all-to-all-start.3 = ((bf16[8,512,128]{2,1,0:T(8,128)(2,1)}), bf16[8,512,128]{2,1,0:T(8,128)(2,1)S(1)}, u32[]{:S(2)}, u32[]{:S(2)}) async-start(bf16[8,512,128]{2,1,0:T(8,128)(2,1)} %get-tuple-element.90), calls=%async_computation.3 | async-start | bytes 2097152 | tf_op jit(solution)/shard_map/all_to_all | solution.py:525
  67.1 8.1 %all-gather.2.cloned.1.call-done.got = bf16[32,528,128]{2,1,0:T(8,128)(2,1)} async-done(((bf16[1,528,128]{2,1,0:T(8,128)(2,1)}), bf16[32,528,128]{2,1,0:T(8,128)(2,1)}) %all-gather.2.cloned.1.call-update) | async-done | bytes 4325392 | tf_op jit(solution)/shard_map/all_gather | solution.py:501
  75.2 10.3 %shard_map.216 = (bf16[8,2,128,128]{3,2,1,0:T(8,128)(2,1)}, f32[14,128,256]{2,1,0:T(8,128)}, bf16[43,128,256]{2,1,0:T(8,128)(2,1)}, bf16[14,128,128]{2,1,0:T(8,1...) custom-call(s32[560]{0:T(1024)} %concatenate.21.meta, ...), custom_call_target="tpu_custom_call" | custom-call | tf_op jit(solution)/shard_map/pallas_call | solution.py:54
  85.5 4.5 %all-to-all-start.4 = ((bf16[8,2,128,128]{3,2,1,0:T(8,128)(2,1)}), bf16[8,2,128,128]{3,2,1,0:T(8,128)(2,1)S(1)}, u32[]{:S(2)}, u32[]{:S(2)}) async-start(bf16[8,2,128,128]{3,2,1,0:T(8,128)(2,1)} %get-tuple-element.99), calls=%async_computation.4 | async-start | bytes 1048576 | tf_op jit(solution)/shard_map/all_to_all | solution.py:535
  90.2 11.0 %shard_map.217 = (bf16[32,608,128]{2,1,0:T(8,128)(2,1)}, bf16[14,128,256]{2,1,0:T(8,128)(2,1)}, f32[128,64]{1,0:T(8,128)}, bf16[128,64]{1,0:T(8,128)(2,1)}) custom-call(s32[560]{0:T(1024)} %concatenate.21.meta, bf16[8,512,128]{2,1,0:T(8,128)(2,1)} %copy-done, f32[14,128,256]{2,1,0:T(8,128)} %get-tuple-element.93.act, ...), custom_call_target="tpu_custom_call" | custom-call | tf_op jit(solution)/shard_map/pallas_call | solution.py:541
  102.1 6.3 %shard_map.218 = (bf16[32,608,128]{2,1,0:T(8,128)(2,1)}, bf16[14,128,128]{2,1,0:T(8,128)(2,1)}, f32[128,64]{1,0:T(8,128)}) custom-call(s32[560]{0:T(1024)} %concatenate.21.meta, bf16[8,2,128,128]{3,2,1,0:T(8,128)(2,1)} %copy-done.2, bf16[14,64,128]{2,1,0:T(8,128)(2,1)} %get-tuple-element.100.dlin, ...), custom_call_target="tpu_custom_call", output_to_operand_aliasing={{0}: (7, {})} | custom-call | tf_op jit(solution)/shard_map/pallas_call | solution.py:553
  110.1 5.5 %all-to-all-start.5 = ((bf16[8,128,128]{2,1,0:T(8,128)(2,1)}), bf16[8,128,128]{2,1,0:T(8,128)(2,1)S(1)}, u32[]{:S(2)}, u32[]{:S(2)}) async-start(bf16[8,128,128]{2,1,0:T(8,128)(2,1)} %broadcast_in_dim.201), calls=%async_computation.5 | async-start | bytes 524288 | tf_op jit(solution)/shard_map/all_to_all | solution.py:465
  115.6 4.6 %shard_map.219 = (bf16[4,8,128,128]{3,2,1,0:T(8,128)(2,1)}, bf16[4,8,128,128]{3,2,1,0:T(8,128)(2,1)}) custom-call(s32[560]{0:T(1024)} %concatenate.21.meta, bf16[14,128,256]{2,1,0:T(8,128)(2,1)} %get-tuple-element.105.gu, bf16[43,128,256]{2,1,0:T(8,128)(2,1)} %get-tuple-element.106.w_gu), custom_call_target="tpu_custom_call" | custom-call | tf_op jit(solution)/shard_map/pallas_call | solution.py:54
  120.2 3.9 %shard_map.220 = (bf16[2,8,128,128]{3,2,1,0:T(8,128)(2,1)}, bf16[2,8,128,128]{3,2,1,0:T(8,128)(2,1)}, bf16[2,8,128,128]{3,2,1,0:T(8,128)(2,1)}, bf16[2,8,128,128]{3,2,1,0:T(8,128)(2,1)}) custom-call(s32[560]{0:T(1024)} %concatenate.21.meta, bf16[14,128,128]{2,1,0:T(8,128)(2,1)} %get-tuple-element.109.hd, bf16[43,128,128]{2,1,0:T(8,128)(2,1)} %get-tuple-element.110.w_d), custom_call_target="tpu_custom_call" | custom-call | tf_op jit(solution)/shard_map/pallas_call | solution.py:54
  127.5 2.7 %collective-permute-start.2 = (bf16[2,8,128,128]{3,2,1,0:T(8,128)(2,1)}, bf16[2,8,128,128]{3,2,1,0:T(8,128)(2,1)S(1)}, u32[]{:S(2)}, u32[]{:S(2)}) collective-permute-start(bf16[2,8,128,128]{3,2,1,0:T(8,128)(2,1)} %get-tuple-element.121), channel_id=1, source_target_pairs={{0,4},{2,6},{4,0},{6,2},{1,5},{3,7},{5,1},{7,3},{8,12},{10,14},{12... | collective-permute-start | bytes 1572872 | tf_op jit(solution)/shard_map/ppermute | solution.py:479
  131.7 3.7 %shard_map.221 = (bf16[2,128,64]{2,1,0:T(8,128)(2,1)}, bf16[32,32,128]{2,1,0:T(8,128)(2,1)}) custom-call(s32[560]{0:T(1024)} %concatenate.21.meta, bf16[8,128,128]{2,1,0:T(8,128)(2,1)} %copy-done.3, bf16[64,128,128]{2,1,0:T(8,128)(2,1)} %bitcast.42, bf16[128,8192]{1,0:T(8,128)(2,1)} %cot.5, bf16[512,512]{1,0:T(8,128)(2,1)} %fusion.2.perm2), custom_call_target="tpu_custom_call" | custom-call | tf_op jit(solution)/shard_map/pallas_call | solution.py:54
  135.4 14.1 %all_to_all.46 = bf16[8,128,128]{2,1,0:T(8,128)(2,1)S(1)} all-to-all(bf16[8,128,128]{2,1,0:T(8,128)(2,1)} %bitcast.48), channel_id=1, replica_groups=mesh['zh'=4,'x'=4,'core'=2,'y'=4,'zl'=2] {'x','core'}, dimensions={0} | all-to-all | bytes 524288 | tf_op jit(solution)/shard_map/all_to_all | solution.py:586
  149.6 3.0 %collective-permute-done.2.refs_2_ = bf16[2,8,128,128]{3,2,1,0:T(8,128)(2,1)S(1)} collective-permute-done((bf16[2,8,128,128]{3,2,1,0:T(8,128)(2,1)}, bf16[2,8,128,128]{3,2,1,0:T(8,128)(2,1)S(1)}, u32[]{:S(2)}, u32[]{:S(2)}) %collective-permute-start.2) | collective-permute-done | bytes 524320 | tf_op jit(solution)/shard_map/ppermute | solution.py:479
  156.0 6.7 %all-to-all-start.7 = ((bf16[4,640,128]{2,1,0:T(8,128)(2,1)}), bf16[4,640,128]{2,1,0:T(8,128)(2,1)S(1)}, u32[]{:S(2)}, u32[]{:S(2)}) async-start(bf16[4,640,128]{2,1,0:T(8,128)(2,1)} %pad_maximum_fusion), calls=%async_computation.8 | async-start | bytes 1310720 | tf_op jit(solution)/shard_map/all_to_all | solution.py:590
  162.7 2.6 %shard_map.224 = (bf16[8,128,128]{2,1,0:T(8,128)(2,1)}, bf16[8,128,128]{2,1,0:T(8,128)(2,1)}, bf16[8,128,128]{2,1,0:T(8,128)(2,1)}, bf16[8,128,128]{2,1,0:T(8,128)(2,1)}) custom-call(bf16[4,8,128,128]{3,2,1,0:T(8,128)(2,1)} %get-tuple-element.131.keep, bf16[4,8,128,128]{3,2,1,0:T(8,128)(2,1)} %copy-done.4), custom_call_target="tpu_custom_call" | custom-call | tf_op jit(solution)/shard_map/pallas_call | solution.py:54
  166.7 4.0 %collective-permute-start.6 = (bf16[8,128,128]{2,1,0:T(8,128)(2,1)}, bf16[8,128,128]{2,1,0:T(8,128)(2,1)S(1)}, u32[]{:S(2)}, u32[]{:S(2)}) collective-permute-start(bf16[8,128,128]{2,1,0:T(8,128)(2,1)} %get-tuple-element.135), channel_id=1, source_target_pairs={{0,4},{2,6},{4,0},{6,2},{1,5},{3,7},{5,1},{7,3},{8,12},{10,14},{12... | collective-permute-start | bytes 786440 | tf_op jit(solution)/shard_map/ppermute | solution.py:479
  175.0 5.9 %all-to-all-done.7 = bf16[4,640,128]{2,1,0:T(8,128)(2,1)S(1)} async-done(((bf16[4,640,128]{2,1,0:T(8,128)(2,1)}), bf16[4,640,128]{2,1,0:T(8,128)(2,1)S(1)}, u32[]{:S(2)}, u32[]{:S(2)}) %all-to-all-start.7) | async-done | bytes 655392 | tf_op jit(solution)/shard_map/all_to_all | solution.py:590
  182.1 4.5 %all-to-all-start.8 = ((bf16[8,16,128]{2,1,0:T(8,128)(2,1)}), bf16[8,16,128]{2,1,0:T(8,128)(2,1)S(1)}, u32[]{:S(2)}, u32[]{:S(2)}) async-start(bf16[8,16,128]{2,1,0:T(8,128)(2,1)} %broadcast_in_dim.202), calls=%async_computation.9 | async-start | bytes 65536 | tf_op jit(solution)/shard_map/all_to_all | solution.py:465
  (142 shorter events, 44.2 us)
Async XLA Ops:
  7.2 68.0 %all-gather.2.cloned.1.call-start = ((), (), s32[]{:S(2)}) async-start(), calls=%async_computation.10 | async-start | bytes 4460544 | tf_op jit(solution)/shard_map/all_gather | solution.py:501
  13.7 17.0 %all-to-all-start = ((bf16[4,1,224,128]{3,2,1,0:T(8,128)(2,1)}), bf16[4,1,224,128]{3,2,1,0:T(8,128)(2,1)S(1)}, u32[]{:S(2)}, u32[]{:S(2)}) async-start(bf16[4,1,224,128]{3,2,1,0:T(8,128)(2,1)} %broadcast_in_dim.181), calls=%async_computation | async-start | bytes 458752 | tf_op jit(solution)/shard_map/all_to_all | solution.py:465
  28.1 9.7 %copy-start.14 = (s32[112,5]{0,1:T(8,128)S(1)}, s32[112,5]{0,1:T(8,128)}, u32[]{:S(2)}) copy-start(s32[112,5]{0,1:T(8,128)} %param.27) | copy-start | bytes 6724
  28.1 9.7 %copy-start.15 = (s32[112,5]{0,1:T(8,128)S(1)}, s32[112,5]{0,1:T(8,128)}, u32[]{:S(2)}) copy-start(s32[112,5]{0,1:T(8,128)} %param.26) | copy-start | bytes 6724
  32.4 16.7 %all-to-all-start.1 = ((bf16[4,4,224,128]{3,2,1,0:T(8,128)(2,1)}), bf16[4,4,224,128]{3,2,1,0:T(8,128)(2,1)S(1)}, u32[]{:S(2)}, u32[]{:S(2)}) async-start(bf16[4,4,224,128]{3,2,1,0:T(8,128)(2,1)} %broadcast_in_dim.182), calls=%async_computation.1 | async-start | bytes 1835008 | tf_op jit(solution)/shard_map/all_to_all | solution.py:465
  62.0 23.5 %all-to-all-start.3 = ((bf16[8,512,128]{2,1,0:T(8,128)(2,1)}), bf16[8,512,128]{2,1,0:T(8,128)(2,1)S(1)}, u32[]{:S(2)}, u32[]{:S(2)}) async-start(bf16[8,512,128]{2,1,0:T(8,128)(2,1)} %get-tuple-element.90), calls=%async_computation.3 | async-start | bytes 2097152 | tf_op jit(solution)/shard_map/all_to_all | solution.py:525
  85.5 15.8 %all-to-all-start.4 = ((bf16[8,2,128,128]{3,2,1,0:T(8,128)(2,1)}), bf16[8,2,128,128]{3,2,1,0:T(8,128)(2,1)S(1)}, u32[]{:S(2)}, u32[]{:S(2)}) async-start(bf16[8,2,128,128]{3,2,1,0:T(8,128)(2,1)} %get-tuple-element.99), calls=%async_computation.4 | async-start | bytes 1048576 | tf_op jit(solution)/shard_map/all_to_all | solution.py:535
  90.0 64.0 %reduce-scatter.2.cloned.1.call-start = ((), (), s32[]{:S(2)}) async-start(), calls=%async_computation.11 | async-start | bytes 5603328 | tf_op jit(solution)/shard_map/reduce_scatter | solution.py:565
  110.1 13.9 %all-to-all-start.5 = ((bf16[8,128,128]{2,1,0:T(8,128)(2,1)}), bf16[8,128,128]{2,1,0:T(8,128)(2,1)S(1)}, u32[]{:S(2)}, u32[]{:S(2)}) async-start(bf16[8,128,128]{2,1,0:T(8,128)(2,1)} %broadcast_in_dim.201), calls=%async_computation.5 | async-start | bytes 524288 | tf_op jit(solution)/shard_map/all_to_all | solution.py:465
  124.0 28.6 %collective-permute-start = (bf16[4,8,128,128]{3,2,1,0:T(8,128)(2,1)}, bf16[4,8,128,128]{3,2,1,0:T(8,128)(2,1)S(1)}, u32[]{:S(2)}, u32[]{:S(2)}) collective-permute-start(bf16[4,8,128,128]{3,2,1,0:T(8,128)(2,1)} %get-tuple-element.118), channel_id=1, source_target_pairs={{0,1},{1,0},{2,3},{3,2},{4,5},{5,4},{6,7},{7,6},{8,9},{9,8},{10,11... | collective-permute-start | bytes 3145736 | tf_op jit(solution)/shard_map/ppermute | solution.py:584
  126.0 23.5 %collective-permute-start.1 = (bf16[2,8,128,128]{3,2,1,0:T(8,128)(2,1)}, bf16[2,8,128,128]{3,2,1,0:T(8,128)(2,1)S(1)}, u32[]{:S(2)}, u32[]{:S(2)}) collective-permute-start(bf16[2,8,128,128]{3,2,1,0:T(8,128)(2,1)} %get-tuple-element.120), channel_id=1, source_target_pairs={{0,2},{2,4},{4,6},{6,0},{1,3},{3,5},{5,7},{7,1},{8,10},{10,12},{12... | collective-permute-start | bytes 1572872 | tf_op jit(solution)/shard_map/ppermute | solution.py:479
  127.5 25.1 %collective-permute-start.2 = (bf16[2,8,128,128]{3,2,1,0:T(8,128)(2,1)}, bf16[2,8,128,128]{3,2,1,0:T(8,128)(2,1)S(1)}, u32[]{:S(2)}, u32[]{:S(2)}) collective-permute-start(bf16[2,8,128,128]{3,2,1,0:T(8,128)(2,1)} %get-tuple-element.121), channel_id=1, source_target_pairs={{0,4},{2,6},{4,0},{6,2},{1,5},{3,7},{5,1},{7,3},{8,12},{10,14},{12... | collective-permute-start | bytes 1572872 | tf_op jit(solution)/shard_map/ppermute | solution.py:479
  130.2 22.4 %collective-permute-start.3 = (bf16[2,8,128,128]{3,2,1,0:T(8,128)(2,1)}, bf16[2,8,128,128]{3,2,1,0:T(8,128)(2,1)S(1)}, u32[]{:S(2)}, u32[]{:S(2)}) collective-permute-start(bf16[2,8,128,128]{3,2,1,0:T(8,128)(2,1)} %get-tuple-element.122), channel_id=1, source_target_pairs={{0,6},{2,0},{4,2},{6,4},{1,7},{3,1},{5,3},{7,5},{8,14},{10,8},{12,... | collective-permute-start | bytes 1572872 | tf_op jit(solution)/shard_map/ppermute | solution.py:479
  149.6 15.7 %copy-start.5 = (bf16[2,8,128,128]{3,2,1,0:T(8,128)(2,1)}, bf16[2,8,128,128]{3,2,1,0:T(8,128)(2,1)S(1)}, u32[]{:S(2)}) copy-start(bf16[2,8,128,128]{3,2,1,0:T(8,128)(2,1)S(1)} %collective-permute-done.1.refs_1_) | copy-start | bytes 1572868
  152.6 12.7 %copy-start.6 = (bf16[2,8,128,128]{3,2,1,0:T(8,128)(2,1)}, bf16[2,8,128,128]{3,2,1,0:T(8,128)(2,1)S(1)}, u32[]{:S(2)}) copy-start(bf16[2,8,128,128]{3,2,1,0:T(8,128)(2,1)S(1)} %collective-permute-done.2.refs_2_) | copy-start | bytes 1572868
  152.6 12.7 %copy-start.7 = (bf16[2,8,128,128]{3,2,1,0:T(8,128)(2,1)}, bf16[2,8,128,128]{3,2,1,0:T(8,128)(2,1)S(1)}, u32[]{:S(2)}) copy-start(bf16[2,8,128,128]{3,2,1,0:T(8,128)(2,1)S(1)} %collective-permute-done.3.refs_3_) | copy-start | bytes 1572868
  152.6 10.1 %copy-start.4 = (bf16[4,8,128,128]{3,2,1,0:T(8,128)(2,1)}, bf16[4,8,128,128]{3,2,1,0:T(8,128)(2,1)S(1)}, u32[]{:S(2)}) copy-start(bf16[4,8,128,128]{3,2,1,0:T(8,128)(2,1)S(1)} %collective-permute-done.came) | copy-start | bytes 3145732
  156.0 24.8 %all-to-all-start.7 = ((bf16[4,640,128]{2,1,0:T(8,128)(2,1)}), bf16[4,640,128]{2,1,0:T(8,128)(2,1)S(1)}, u32[]{:S(2)}, u32[]{:S(2)}) async-start(bf16[4,640,128]{2,1,0:T(8,128)(2,1)} %pad_maximum_fusion), calls=%async_computation.8 | async-start | bytes 1310720 | tf_op jit(solution)/shard_map/all_to_all | solution.py:590
  165.3 24.1 %collective-permute-start.5 = (bf16[8,128,128]{2,1,0:T(8,128)(2,1)}, bf16[8,128,128]{2,1,0:T(8,128)(2,1)S(1)}, u32[]{:S(2)}, u32[]{:S(2)}) collective-permute-start(bf16[8,128,128]{2,1,0:T(8,128)(2,1)} %get-tuple-element.134), channel_id=1, source_target_pairs={{0,2},{2,4},{4,6},{6,0},{1,3},{3,5},{5,7},{7,1},{8,10},{10,12},{12... | collective-permute-start | bytes 786440 | tf_op jit(solution)/shard_map/ppermute | solution.py:479
  166.7 22.7 %collective-permute-start.6 = (bf16[8,128,128]{2,1,0:T(8,128)(2,1)}, bf16[8,128,128]{2,1,0:T(8,128)(2,1)S(1)}, u32[]{:S(2)}, u32[]{:S(2)}) collective-permute-start(bf16[8,128,128]{2,1,0:T(8,128)(2,1)} %get-tuple-element.135), channel_id=1, source_target_pairs={{0,4},{2,6},{4,0},{6,2},{1,5},{3,7},{5,1},{7,3},{8,12},{10,14},{12... | collective-permute-start | bytes 786440 | tf_op jit(solution)/shard_map/ppermute | solution.py:479
  170.7 18.7 %collective-permute-start.7 = (bf16[8,128,128]{2,1,0:T(8,128)(2,1)}, bf16[8,128,128]{2,1,0:T(8,128)(2,1)S(1)}, u32[]{:S(2)}, u32[]{:S(2)}) collective-permute-start(bf16[8,128,128]{2,1,0:T(8,128)(2,1)} %get-tuple-element.136), channel_id=1, source_target_pairs={{0,6},{2,0},{4,2},{6,4},{1,7},{3,1},{5,3},{7,5},{8,14},{10,8},{12,... | collective-permute-start | bytes 786440 | tf_op jit(solution)/shard_map/ppermute | solution.py:479
  174.2 12.5 %collective-permute-start.4 = (bf16[8,128,128]{2,1,0:T(8,128)(2,1)}, bf16[8,128,128]{2,1,0:T(8,128)(2,1)S(1)}, u32[]{:S(2)}, u32[]{:S(2)}) collective-permute-start(bf16[8,128,128]{2,1,0:T(8,128)(2,1)} %get-tuple-element.128), channel_id=1, source_target_pairs={{0,1},{1,0},{2,3},{3,2},{4,5},{5,4},{6,7},{7,6},{8,9},{9,8},{10,11... | collective-permute-start | bytes 786440 | tf_op jit(solution)/shard_map/ppermute | solution.py:595
  180.8 11.7 %copy-start.1 = (bf16[4,640,128]{2,1,0:T(8,128)(2,1)}, bf16[4,640,128]{2,1,0:T(8,128)(2,1)S(1)}, u32[]{:S(2)}) copy-start(bf16[4,640,128]{2,1,0:T(8,128)(2,1)S(1)} %all-to-all-done.7) | copy-start | bytes 1966084
  182.1 14.2 %all-to-all-start.8 = ((bf16[8,16,128]{2,1,0:T(8,128)(2,1)}), bf16[8,16,128]{2,1,0:T(8,128)(2,1)S(1)}, u32[]{:S(2)}, u32[]{:S(2)}) async-start(bf16[8,16,128]{2,1,0:T(8,128)(2,1)} %broadcast_in_dim.202), calls=%async_computation.9 | async-start | bytes 65536 | tf_op jit(solution)/shard_map/all_to_all | solution.py:465
  (13 other events, 41.4 us)
Sparse Core Ops, SparseCore 0:
  12.3 62.8 all-gather.1
  108.6 45.4 reduce-scatter.1

commit v4 on v3

--- a/solution.py
+++ b/solution.py
@@ -65,32 +65,35 @@
     return jax.ShapeDtypeStruct(dims, dtype)
 
 
-def pack_body(up_count, down_count, who, gate_w, up_w, down_w, mid, low, dlin, dlout, first, second):
+def put_live(out, weight, counts, mine, base):
+    at = jnp.int32(base)
+    for s in range(SLOTS):
+        count = counts[mine + s]
+        for k in range(DEPTH):
+            out[at] = weight[s, k]
+            at = at + (k < count).astype(I32)
+
+
+def pack_up_body(up_count, who, gate_w, up_w, mid, low, out):
     mine = who[0] * SLOTS
     for pad in (UP + 42, UP + 43):
-        first[pad] = jnp.zeros((4, BLK), BF16)
+        out[pad] = jnp.zeros((4, BLK), BF16)
+    put_live(out, gate_w, up_count, mine, GATE)
+    put_live(out, up_w, up_count, mine, UP)
+    for s in range(SLOTS):
+        out[MID + s] = mid[:, s * BLK : (s + 1) * BLK]
+    for e in range(32):
+        out[LOWIN + e] = low[e]
+
+
+def pack_down_body(down_count, who, down_w, dlin, dlout, out):
     for pad in (DOWN + 42, DOWN + 43):
-        second[pad] = jnp.zeros((4, BLK), BF16)
-
-    def put(out, weight, counts, base):
-        at = jnp.int32(base)
-        for s in range(SLOTS):
-            count = counts[mine + s]
-            for k in range(DEPTH):
-                out[at] = weight[s, k]
-                at = at + (k < count).astype(I32)
-
-    put(second, down_w, down_count, DOWN)
-    put(first, gate_w, up_count, GATE)
-    put(first, up_w, up_count, UP)
-    for s in range(SLOTS):
-        first[MID + s] = mid[s]
-    for e in range(32):
-        first[LOWIN + e] = low[e]
+        out[pad] = jnp.zeros((4, BLK), BF16)
+    put_live(out, down_w, down_count, who[0] * SLOTS, DOWN)
     for e in range(8):
-        second[DLIN + e] = dlin[e]
+        out[DLIN + e] = dlin[e]
     for e in range(4):
-        second[DLOUT + e] = dlout[e]
+        out[DLOUT + e] = dlout[e]
 
 
 def hidden_grad_body(meta, got, cot, perm, perm2, send, w_d, dlin, dlout, hgrad):
@@ -132,7 +135,22 @@
         send[peer, BACK_SUM:] = total
 
 
-def forward_body(meta, got, tok, perm, send, act, w_gu, mid, lat, low_share, hid):
+def forward_body(
+    meta, got_far, tok_far, perm, send, act, w_far, mid, lat, low_share, hid, got, tok, w_gu, sems
+):
+    loads = [
+        pltpu.make_async_copy(
+            got_far.at[:, : 4 * LOWIN, :], got.at[:, : 4 * LOWIN, :], sems.at[0]
+        ),
+        pltpu.make_async_copy(
+            got_far.at[:, 4 * LOWIN :, :], got.at[:, 4 * LOWIN :, :], sems.at[1]
+        ),
+        pltpu.make_async_copy(tok_far, tok, sems.at[2]),
+    ]
+    for load in loads:
+        load.start()
+    loads[0].wait()
+
     def rows(block):
         return got[:, 4 * block : 4 * block + 16, :].reshape(512, BLK)
 
@@ -154,6 +172,10 @@
         for half, i in enumerate((a, b)[: 1 + (a != b)]):
             for jj in range(4):
                 mid[i + jj] = both[jj * BLK : (jj + 1) * BLK, half * BLK : (half + 1) * BLK]
+    keep = pltpu.make_async_copy(w_gu, w_far, sems.at[3])
+    keep.start()
+    loads[1].wait()
+    loads[2].wait()
 
     acc0 = jnp.zeros((BLK, BLK), F32)
     acc1 = jnp.zeros((BLK, BLK), F32)
@@ -179,6 +201,7 @@
         act[s, :, BLK:] = active
     for lane in range(NMP * CAP):
         send[lane // CAP, lane % CAP] = hid[meta[SEND_A + lane]]
+    keep.wait()
 
 
 def up_grads_body(
@@ -231,8 +254,11 @@
 
 
 def down_grads_body(
-    meta, got, dlin, back_latent, cot, perm, perm2, start, grad, hd, part, hd_t, ding, full, sem
+    meta, got, dlin, back_latent, cot_far, perm, perm2, start, grad, hd, part, hd_t, ding, full,
+    cot, sem, cot_sem,
 ):
+    load = pltpu.make_async_copy(cot_far, cot, cot_sem)
+    load.start()
     back = back_latent[...]
     back_t = turned(jnp.concatenate([back, back], axis=1))[:RANK]
     down_sum = jnp.zeros((BLK, RANK), F32)
@@ -244,6 +270,7 @@
         down_sum = down_sum + dot_t(h, dlin[t])
         ding[t] = dot(back_t, h).astype(BF16)
     part[...] = down_sum
+    load.wait()
 
     def store(block, rows):
         full[:, 4 * block : 4 * block + 16, :] = rows.reshape(NDP, 16, BLK)
@@ -487,16 +514,19 @@
 ):
     mine = lax.axis_index(MP).astype(I32)
     who = mine.reshape(1)
-    mid_rows = low_mid.reshape(4, SLOTS, BLK).transpose(1, 0, 2)
+    low_rows = jnp.concatenate([low_in[:BLK], low_in[BLK:]], axis=1).reshape(32, 4, BLK)
+    first = call(
+        pack_up_body, shape(PACK_A, 4, BLK), (gate_weight, up_weight, low_mid, low_rows),
+        (up_count, who),
+    )
+    first, down_low_in, down_low_out = together((first, down_low_in, down_low_out))
     dlin_rows = jnp.pad(
         down_low_in.reshape(2, SLOTS, BLK).transpose(1, 0, 2).reshape(2 * SLOTS, BLK), ((0, 4), (0, 0))
     ).reshape(8, 4, BLK)
-    low_rows = jnp.concatenate([low_in[:BLK], low_in[BLK:]], axis=1).reshape(32, 4, BLK)
     dlout_rows = down_low_out.reshape(2, SHARE, BLK).transpose(1, 0, 2).reshape(4, 4, BLK)
-    first, second = call(
-        pack_body, (shape(PACK_A, 4, BLK), shape(PACK_B, 4, BLK)),
-        (gate_weight, up_weight, down_weight, mid_rows, low_rows, dlin_rows, dlout_rows),
-        (up_count, down_count, who),
+    second = call(
+        pack_down_body, shape(PACK_B, 4, BLK), (down_weight, dlin_rows, dlout_rows),
+        (down_count, who),
     )
     got_up = lax.all_gather(first.reshape(4 * PACK_A, BLK), DP)
     got_down = gather_step(second.reshape(1, 4 * PACK_B, BLK), "zh", 4)
@@ -524,19 +554,27 @@
     back_send, tok_t = together((back_send, tok_t))
     back_got = lax.all_to_all(back_send, MP, 0, 0, tiled=True)
 
-    send, act, w_gu, mid, lat, low_share = call(
-        forward_body,
-        (
-            parcel, shape(SLOTS, BLK, 2 * BLK, dtype=F32), shape(LIVE + 1, BLK, 2 * BLK), slots,
-            shape(BLK, RANK), shape(4, BLK, BLK),
-        ),
-        (got_up, tokens, take), (meta,), (slots_scratch,),
-    )
-    got = lax.all_to_all(send, MP, 0, 0, tiled=True)
-
     hbm = pl.BlockSpec(memory_space=pl.ANY)
     vmem = pl.BlockSpec(memory_space=pltpu.VMEM)
     smem = pl.BlockSpec(memory_space=pltpu.SMEM)
+    weights = (LIVE + 1, BLK, 2 * BLK)
+    send, act, w_gu, mid, lat, low_share = pl.pallas_call(
+        forward_body,
+        out_shape=(
+            parcel, shape(SLOTS, BLK, 2 * BLK, dtype=F32), shape(*weights), slots,
+            shape(BLK, RANK), shape(4, BLK, BLK),
+        ),
+        in_specs=[smem, hbm, hbm, vmem],
+        out_specs=(vmem, vmem, hbm, vmem, vmem, vmem),
+        scratch_shapes=[
+            slots_scratch, pltpu.VMEM((NDP, 4 * PACK_A, BLK), BF16),
+            pltpu.VMEM((BLK, COLS * BLK), BF16), pltpu.VMEM(weights, BF16),
+            pltpu.SemaphoreType.DMA((4,)),
+        ],
+        compiler_params=pltpu.CompilerParams(vmem_limit_bytes=VMEM_LIMIT),
+    )(meta, got_up, tokens, take)
+    got = lax.all_to_all(send, MP, 0, 0, tiled=True)
+
     grad_shape = shape(NDP, 4 * GRAD, BLK)
     grad, gu, part_up, back_latent = pl.pallas_call(
         up_grads_body,
@@ -553,11 +591,12 @@
     grad, hd, part_down = pl.pallas_call(
         down_grads_body,
         out_shape=(grad_shape, slots, shape(BLK, RANK, dtype=F32)),
-        in_specs=[smem] + [vmem] * 6 + [hbm],
+        in_specs=[smem] + [vmem] * 3 + [hbm] + [vmem] * 2 + [hbm],
         out_specs=(hbm, vmem, vmem),
         scratch_shapes=[
             slots_scratch, pltpu.VMEM((SLOTS, RANK, BLK), BF16),
-            pltpu.VMEM((NDP, 4 * (GRAD - GRAD_A), BLK), BF16), pltpu.SemaphoreType.DMA,
+            pltpu.VMEM((NDP, 4 * (GRAD - GRAD_A), BLK), BF16),
+            pltpu.VMEM((BLK, COLS * BLK), BF16), pltpu.SemaphoreType.DMA, pltpu.SemaphoreType.DMA,
         ],
         input_output_aliases={7: 0},
         compiler_params=pltpu.CompilerParams(vmem_limit_bytes=VMEM_LIMIT),
@@ -588,14 +627,15 @@
     small, grad, token_came, out_got = together((small, grad, token_came, out_got))
     grad = jnp.concatenate([grad.reshape(4, 4 * GRAD, BLK), small], axis=1)
     grad = lax.all_to_all(grad, "zh", 0, 0, tiled=True)
-    small = jnp.sum(grad[:, 4 * GRAD :].astype(F32), axis=0).astype(BF16)
     half = shape(SHARE, BLK, BLK)
     token_got = rotate(call(token_pair_body, (half,) * NY, (token_part[0], token_came), ()))
     out_keep, out_give = call(out_y_body, (half,) * 2, out_got, (meta,))
     out_came = lax.ppermute(out_give, "zl", swap)
-    low_g = spread(small[:16], MP, NMP)
     wide = shape(BLK, SHARE * BLK)
     token_grad = call(token_out_body, wide, (*token_got, latents, low_share), ())
+    grad, token_grad = together((grad, token_grad))
+    small = jnp.sum(grad[:, 4 * GRAD :].astype(F32), axis=0).astype(BF16)
+    low_g = spread(small[:16], MP, NMP)
     layer_out = call(layer_out_body, wide, (out_keep, out_came, latents, dlout), ())
     wide = shape(SLOTS, DEPTH, 4, BLK)
     gate_g, up_g, down_g, mid_g, tail = call(

time: 207 us -> 205 us (level)
  waiting for transfers between devices: 29.3 us -> 25.9 us
    pallas_call x0 -> x1, Pallas kernels: none -> 10 us  [local(): pl.pallas_call(forward_body, out_shape=(parcel, shape(SLOTS, BLK, 2 * BLK...]
    pallas_call x11, Pallas kernels: 43 us -> 34.2 us  [call(): pl.pallas_call(body, out_shape=out_shapes, in_specs=[smem] * len(scalars)...]
    all_to_all x1, waiting for transfers between devices: 5.85 us -> 0.01 us  [local(): grad = lax.all_to_all(grad, 'zh', 0, 0, tiled=True)]
    ppermute x6, waiting for transfers between devices: 3.01 us -> 7.21 us  [rotate(): lax.ppermute(parts[k], 'y', [(i, (i + k) % NY) for i in range(NY)])]
    all_gather x1, waiting for transfers between devices: 8.1 us -> 5.74 us  [local(): got_up = lax.all_gather(first.reshape(4 * PACK_A, BLK), DP)]
  transfers between devices with their start and end apart: 17 -> 17, of which waited for: 6 -> 8; matrix products, arithmetic and copies ran while one was open for 8% -> 9% of each run, Pallas kernels for 25% -> 27%
where the time goes in v4:
time: 205 us; the launch traced here: 201 us
  Pallas kernels  62.2 us (30%)
  starting transfers between devices  52.1 us (25%)
  waiting for transfers between devices  25.9 us (13%)
  blocking collectives  20.3 us (10%)
  local copies, waits for them, and re-layouts  18.6 us (9%)
  between operations  14.4 us (7%)
  other arithmetic  7.21 us (4%)
    pallas_call x11, Pallas kernels, call(): pl.pallas_call(body, out_shape=out_shapes, in_specs=[smem] * len(scalars)...  34.2 us
    all_to_all x4, starting transfers between devices, spread(): lax.all_to_all(jnp.broadcast_to(x[None], (n,) + x.shape), axis, 0, 0, til...  22 us
    all_to_all x1, blocking collectives, local(): lax.all_to_all(small.reshape(8, BLK, BLK), ('x', 'core'), 0, 0, tiled=True)  14.2 us
    ppermute x6, starting transfers between devices, rotate(): lax.ppermute(parts[k], 'y', [(i, (i + k) % NY) for i in range(NY)])  12 us
    pallas_call x1, Pallas kernels, local(): pl.pallas_call(up_grads_body, out_shape=(grad_shape, shape(SLOTS, BLK, 2...  10.9 us
    pallas_call x1, Pallas kernels, local(): pl.pallas_call(forward_body, out_shape=(parcel, shape(SLOTS, BLK, 2 * BLK...  10 us
    all_to_all x4, waiting for transfers between devices, spread(): lax.all_to_all(jnp.broadcast_to(x[None], (n,) + x.shape), axis, 0, 0, til...  9.86 us
    unnamed x43, local copies, waits for them, and re-layouts  8.55 us
  transfers between devices with their start and end apart: 17, of which 8 were waited for; matrix products, arithmetic and copies ran while one was open for 9% of the time, Pallas kernels for 27%

profile of v4, /device:TPU:64, one launch (start us, length us, event | category | flops | bytes accessed | tf_op | source)
XLA Modules:
  0.0 200.8 jit_solution(13431060033054082589)
XLA Ops:
  15.1 8.1 %all-to-all-start = ((bf16[4,1,224,128]{3,2,1,0:T(8,128)(2,1)}), bf16[4,1,224,128]{3,2,1,0:T(8,128)(2,1)S(1)}, u32[]{:S(2)}, u32[]{:S(2)}) async-start(bf16[4,1,224,128]{3,2,1,0:T(8,128)(2,1)} %broadcast_in_dim.181), calls=%async_computation | async-start | bytes 458752 | tf_op jit(solution)/shard_map/all_to_all | solution.py:492
  23.2 4.1 %copy.60 = bf16[128,8192]{0,1:T(8,128)(2,1)} copy(bf16[128,8192]{1,0:T(8,128)(2,1)} %tok_far.1) | data formatting | bytes 4194304 | tf_op args[0]
  33.1 5.0 %all-to-all-start.1 = ((bf16[4,4,224,128]{3,2,1,0:T(8,128)(2,1)}), bf16[4,4,224,128]{3,2,1,0:T(8,128)(2,1)S(1)}, u32[]{:S(2)}, u32[]{:S(2)}) async-start(bf16[4,4,224,128]{3,2,1,0:T(8,128)(2,1)} %broadcast_in_dim.182), calls=%async_computation.1 | async-start | bytes 1835008 | tf_op jit(solution)/shard_map/all_to_all | solution.py:492
  40.9 9.2 %all-to-all-done.1 = bf16[4,4,224,128]{3,2,1,0:T(8,128)(2,1)S(1)} async-done(((bf16[4,4,224,128]{3,2,1,0:T(8,128)(2,1)}), bf16[4,4,224,128]{3,2,1,0:T(8,128)(2,1)S(1)}, u32[]{:S(2)}, u32[]{:S(2)}) %all-to-all-start.1) | async-done | bytes 917536 | tf_op jit(solution)/shard_map/all_to_all | solution.py:492
  50.3 6.1 %all_to_all.45 = bf16[2,16,224,128]{3,2,1,0:T(8,128)(2,1)} all-to-all(bf16[2,16,224,128]{3,2,1,0:T(8,128)(2,1)S(1)} %broadcast_in_dim.200), channel_id=1, replica_groups=mesh['zh'=4,'x'=4,'core'=2,'y'=4,'zl'=2] {'core'}, dimensions={0} | all-to-all | bytes 3670016 | tf_op jit(solution)/shard_map/all_to_all | solution.py:492
  56.4 6.7 %shard_map.216 = (bf16[8,512,128]{2,1,0:T(8,128)(2,1)}, bf16[43,128,128]{2,1,0:T(8,128)(2,1)}, bf16[14,64,128]{2,1,0:T(8,128)(2,1)}, bf16[512,128]{1,0:T(8,128)(2,1)}) custom-call(s32[560]{0:T(1024)} %concatenate.21.meta, bf16[32,224,128]{2,1,0:T(8,128)(2,1)} %bitcast.40, bf16[128,8192]{1,0:T(8,128)(2,1)} %cot.3, bf16[512,512]{1,0:T(8,128)(2,1)} %get-tuple-element.214.perm, ...), custom_call_target="tpu_custom_call" | custom-call | tf_op jit(solution)/shard_map/pallas_call | solution.py:54
  63.1 5.0 %all-to-all-start.3 = ((bf16[8,512,128]{2,1,0:T(8,128)(2,1)}), bf16[8,512,128]{2,1,0:T(8,128)(2,1)S(1)}, u32[]{:S(2)}, u32[]{:S(2)}) async-start(bf16[8,512,128]{2,1,0:T(8,128)(2,1)} %get-tuple-element.94), calls=%async_computation.3 | async-start | bytes 2097152 | tf_op jit(solution)/shard_map/all_to_all | solution.py:555
  68.1 5.7 %all-gather.2.cloned.1.call-done.got_far = bf16[32,528,128]{2,1,0:T(8,128)(2,1)} async-done(((bf16[1,528,128]{2,1,0:T(8,128)(2,1)}), bf16[32,528,128]{2,1,0:T(8,128)(2,1)}) %all-gather.2.cloned.1.call-update) | async-done | bytes 4325392 | tf_op jit(solution)/shard_map/all_gather | solution.py:531
  73.9 10.0 %shard_map.217 = (bf16[8,2,128,128]{3,2,1,0:T(8,128)(2,1)}, f32[14,128,256]{2,1,0:T(8,128)}, bf16[43,128,256]{2,1,0:T(8,128)(2,1)}, bf16[14,128,128]{2,1,0:T(8,1...) custom-call(s32[560]{0:T(1024)} %concatenate.21.meta, ...), custom_call_target="tpu_custom_call" | custom-call | tf_op jit(solution)/shard_map/pallas_call | solution.py:561
  85.2 3.5 %all-to-all-start.4 = ((bf16[8,2,128,128]{3,2,1,0:T(8,128)(2,1)}), bf16[8,2,128,128]{3,2,1,0:T(8,128)(2,1)S(1)}, u32[]{:S(2)}, u32[]{:S(2)}) async-start(bf16[8,2,128,128]{3,2,1,0:T(8,128)(2,1)} %get-tuple-element.103), calls=%async_computation.4 | async-start | bytes 1048576 | tf_op jit(solution)/shard_map/all_to_all | solution.py:576
  88.9 10.9 %shard_map.218 = (bf16[32,608,128]{2,1,0:T(8,128)(2,1)}, bf16[14,128,256]{2,1,0:T(8,128)(2,1)}, f32[128,64]{1,0:T(8,128)}, bf16[128,64]{1,0:T(8,128)(2,1)}) custom-call(s32[560]{0:T(1024)} %concatenate.21.meta, bf16[8,512,128]{2,1,0:T(8,128)(2,1)} %copy-done, f32[14,128,256]{2,1,0:T(8,128)} %get-tuple-element.97.act, ...), custom_call_target="tpu_custom_call" | custom-call | tf_op jit(solution)/shard_map/pallas_call | solution.py:579
  100.7 7.1 %shard_map.219 = (bf16[32,608,128]{2,1,0:T(8,128)(2,1)}, bf16[14,128,128]{2,1,0:T(8,128)(2,1)}, f32[128,64]{1,0:T(8,128)}) custom-call(s32[560]{0:T(1024)} %concatenate.21.meta, bf16[8,2,128,128]{3,2,1,0:T(8,128)(2,1)} %copy-done.2, bf16[14,64,128]{2,1,0:T(8,128)(2,1)} %get-tuple-element.104.dlin, ...), custom_call_target="tpu_custom_call", output_to_operand_aliasing={{0}: (7, {})} | custom-call | tf_op jit(solution)/shard_map/pallas_call | solution.py:591
  109.5 5.4 %all-to-all-start.5 = ((bf16[8,128,128]{2,1,0:T(8,128)(2,1)}), bf16[8,128,128]{2,1,0:T(8,128)(2,1)S(1)}, u32[]{:S(2)}, u32[]{:S(2)}) async-start(bf16[8,128,128]{2,1,0:T(8,128)(2,1)} %broadcast_in_dim.201), calls=%async_computation.5 | async-start | bytes 524288 | tf_op jit(solution)/shard_map/all_to_all | solution.py:492
  114.9 4.6 %shard_map.220 = (bf16[4,8,128,128]{3,2,1,0:T(8,128)(2,1)}, bf16[4,8,128,128]{3,2,1,0:T(8,128)(2,1)}) custom-call(s32[560]{0:T(1024)} %concatenate.21.meta, bf16[14,128,256]{2,1,0:T(8,128)(2,1)} %get-tuple-element.109.gu, bf16[43,128,256]{2,1,0:T(8,128)(2,1)} %get-tuple-element.110.w_gu), custom_call_target="tpu_custom_call" | custom-call | tf_op jit(solution)/shard_map/pallas_call | solution.py:54
  119.5 3.9 %shard_map.221 = (bf16[2,8,128,128]{3,2,1,0:T(8,128)(2,1)}, bf16[2,8,128,128]{3,2,1,0:T(8,128)(2,1)}, bf16[2,8,128,128]{3,2,1,0:T(8,128)(2,1)}, bf16[2,8,128,128]{3,2,1,0:T(8,128)(2,1)}) custom-call(s32[560]{0:T(1024)} %concatenate.21.meta, bf16[14,128,128]{2,1,0:T(8,128)(2,1)} %get-tuple-element.113.hd, bf16[43,128,128]{2,1,0:T(8,128)(2,1)} %get-tuple-element.114.w_d), custom_call_target="tpu_custom_call" | custom-call | tf_op jit(solution)/shard_map/pallas_call | solution.py:54
  126.8 2.7 %collective-permute-start.2 = (bf16[2,8,128,128]{3,2,1,0:T(8,128)(2,1)}, bf16[2,8,128,128]{3,2,1,0:T(8,128)(2,1)S(1)}, u32[]{:S(2)}, u32[]{:S(2)}) collective-permute-start(bf16[2,8,128,128]{3,2,1,0:T(8,128)(2,1)} %get-tuple-element.125), channel_id=1, source_target_pairs={{0,4},{2,6},{4,0},{6,2},{1,5},{3,7},{5,1},{7,3},{8,12},{10,14},{12... | collective-permute-start | bytes 1572872 | tf_op jit(solution)/shard_map/ppermute | solution.py:506
  130.9 3.7 %shard_map.222 = (bf16[2,128,64]{2,1,0:T(8,128)(2,1)}, bf16[32,32,128]{2,1,0:T(8,128)(2,1)}) custom-call(s32[560]{0:T(1024)} %concatenate.21.meta, bf16[8,128,128]{2,1,0:T(8,128)(2,1)} %copy-done.3, bf16[64,128,128]{2,1,0:T(8,128)(2,1)} %bitcast.39, bf16[128,8192]{1,0:T(8,128)(2,1)} %cot.3, bf16[512,512]{1,0:T(8,128)(2,1)} %fusion.2.perm2), custom_call_target="tpu_custom_call" | custom-call | tf_op jit(solution)/shard_map/pallas_call | solution.py:54
  134.7 14.2 %all_to_all.46 = bf16[8,128,128]{2,1,0:T(8,128)(2,1)S(1)} all-to-all(bf16[8,128,128]{2,1,0:T(8,128)(2,1)} %bitcast.46), channel_id=1, replica_groups=mesh['zh'=4,'x'=4,'core'=2,'y'=4,'zl'=2] {'x','core'}, dimensions={0} | all-to-all | bytes 524288 | tf_op jit(solution)/shard_map/all_to_all | solution.py:625
  149.0 2.7 %collective-permute-done.2.refs_2_ = bf16[2,8,128,128]{3,2,1,0:T(8,128)(2,1)S(1)} collective-permute-done((bf16[2,8,128,128]{3,2,1,0:T(8,128)(2,1)}, bf16[2,8,128,128]{3,2,1,0:T(8,128)(2,1)S(1)}, u32[]{:S(2)}, u32[]{:S(2)}) %collective-permute-start.2) | collective-permute-done | bytes 524320 | tf_op jit(solution)/shard_map/ppermute | solution.py:506
  155.4 6.6 %all-to-all-start.7 = ((bf16[4,640,128]{2,1,0:T(8,128)(2,1)}), bf16[4,640,128]{2,1,0:T(8,128)(2,1)S(1)}, u32[]{:S(2)}, u32[]{:S(2)}) async-start(bf16[4,640,128]{2,1,0:T(8,128)(2,1)} %pad_maximum_fusion), calls=%async_computation.8 | async-start | bytes 1310720 | tf_op jit(solution)/shard_map/all_to_all | solution.py:629
  162.0 2.6 %shard_map.225 = (bf16[8,128,128]{2,1,0:T(8,128)(2,1)}, bf16[8,128,128]{2,1,0:T(8,128)(2,1)}, bf16[8,128,128]{2,1,0:T(8,128)(2,1)}, bf16[8,128,128]{2,1,0:T(8,128)(2,1)}) custom-call(bf16[4,8,128,128]{3,2,1,0:T(8,128)(2,1)} %get-tuple-element.137.keep, bf16[4,8,128,128]{3,2,1,0:T(8,128)(2,1)} %copy-done.4), custom_call_target="tpu_custom_call" | custom-call | tf_op jit(solution)/shard_map/pallas_call | solution.py:54
  166.0 4.1 %collective-permute-start.6 = (bf16[8,128,128]{2,1,0:T(8,128)(2,1)}, bf16[8,128,128]{2,1,0:T(8,128)(2,1)S(1)}, u32[]{:S(2)}, u32[]{:S(2)}) collective-permute-start(bf16[8,128,128]{2,1,0:T(8,128)(2,1)} %get-tuple-element.141), channel_id=1, source_target_pairs={{0,4},{2,6},{4,0},{6,2},{1,5},{3,7},{5,1},{7,3},{8,12},{10,14},{12... | collective-permute-start | bytes 786440 | tf_op jit(solution)/shard_map/ppermute | solution.py:506
  175.9 2.8 %collective-permute-done.6.refs_2_ = bf16[8,128,128]{2,1,0:T(8,128)(2,1)S(1)} collective-permute-done((bf16[8,128,128]{2,1,0:T(8,128)(2,1)}, bf16[8,128,128]{2,1,0:T(8,128)(2,1)S(1)}, u32[]{:S(2)}, u32[]{:S(2)}) %collective-permute-start.6) | collective-permute-done | bytes 262176 | tf_op jit(solution)/shard_map/ppermute | solution.py:506
  183.1 3.6 %all-to-all-start.8 = ((bf16[8,16,128]{2,1,0:T(8,128)(2,1)}), bf16[8,16,128]{2,1,0:T(8,128)(2,1)S(1)}, u32[]{:S(2)}, u32[]{:S(2)}) async-start(bf16[8,16,128]{2,1,0:T(8,128)(2,1)} %broadcast_in_dim.202), calls=%async_computation.9 | async-start | bytes 65536 | tf_op jit(solution)/shard_map/all_to_all | solution.py:492
  (143 shorter events, 48.1 us)
Async XLA Ops:
  7.2 66.7 %all-gather.2.cloned.1.call-start = ((), (), s32[]{:S(2)}) async-start(), calls=%async_computation.10 | async-start | bytes 4460544 | tf_op jit(solution)/shard_map/all_gather | solution.py:531
  15.1 16.4 %all-to-all-start = ((bf16[4,1,224,128]{3,2,1,0:T(8,128)(2,1)}), bf16[4,1,224,128]{3,2,1,0:T(8,128)(2,1)S(1)}, u32[]{:S(2)}, u32[]{:S(2)}) async-start(bf16[4,1,224,128]{3,2,1,0:T(8,128)(2,1)} %broadcast_in_dim.181), calls=%async_computation | async-start | bytes 458752 | tf_op jit(solution)/shard_map/all_to_all | solution.py:492
  29.5 8.7 %copy-start.16 = (s32[112]{0:T(128)S(1)}, s32[112]{0:T(128)}, u32[]{:S(2)}) copy-start(s32[112]{0:T(128)} %param.25) | copy-start | bytes 1348
  29.5 9.7 %copy-start.14 = (s32[112,5]{0,1:T(8,128)S(1)}, s32[112,5]{0,1:T(8,128)}, u32[]{:S(2)}) copy-start(s32[112,5]{0,1:T(8,128)} %param.27) | copy-start | bytes 6724
  29.5 9.7 %copy-start.15 = (s32[112,5]{0,1:T(8,128)S(1)}, s32[112,5]{0,1:T(8,128)}, u32[]{:S(2)}) copy-start(s32[112,5]{0,1:T(8,128)} %param.26) | copy-start | bytes 6724
  33.1 17.0 %all-to-all-start.1 = ((bf16[4,4,224,128]{3,2,1,0:T(8,128)(2,1)}), bf16[4,4,224,128]{3,2,1,0:T(8,128)(2,1)S(1)}, u32[]{:S(2)}, u32[]{:S(2)}) async-start(bf16[4,4,224,128]{3,2,1,0:T(8,128)(2,1)} %broadcast_in_dim.182), calls=%async_computation.1 | async-start | bytes 1835008 | tf_op jit(solution)/shard_map/all_to_all | solution.py:492
  63.1 22.1 %all-to-all-start.3 = ((bf16[8,512,128]{2,1,0:T(8,128)(2,1)}), bf16[8,512,128]{2,1,0:T(8,128)(2,1)S(1)}, u32[]{:S(2)}, u32[]{:S(2)}) async-start(bf16[8,512,128]{2,1,0:T(8,128)(2,1)} %get-tuple-element.94), calls=%async_computation.3 | async-start | bytes 2097152 | tf_op jit(solution)/shard_map/all_to_all | solution.py:555
  85.2 14.7 %all-to-all-start.4 = ((bf16[8,2,128,128]{3,2,1,0:T(8,128)(2,1)}), bf16[8,2,128,128]{3,2,1,0:T(8,128)(2,1)S(1)}, u32[]{:S(2)}, u32[]{:S(2)}) async-start(bf16[8,2,128,128]{3,2,1,0:T(8,128)(2,1)} %get-tuple-element.103), calls=%async_computation.4 | async-start | bytes 1048576 | tf_op jit(solution)/shard_map/all_to_all | solution.py:576
  88.7 64.7 %reduce-scatter.2.cloned.1.call-start = ((), (), s32[]{:S(2)}) async-start(), calls=%async_computation.11 | async-start | bytes 5603328 | tf_op jit(solution)/shard_map/reduce_scatter | solution.py:604
  109.5 13.8 %all-to-all-start.5 = ((bf16[8,128,128]{2,1,0:T(8,128)(2,1)}), bf16[8,128,128]{2,1,0:T(8,128)(2,1)S(1)}, u32[]{:S(2)}, u32[]{:S(2)}) async-start(bf16[8,128,128]{2,1,0:T(8,128)(2,1)} %broadcast_in_dim.201), calls=%async_computation.5 | async-start | bytes 524288 | tf_op jit(solution)/shard_map/all_to_all | solution.py:492
  123.3 28.3 %collective-permute-start = (bf16[4,8,128,128]{3,2,1,0:T(8,128)(2,1)}, bf16[4,8,128,128]{3,2,1,0:T(8,128)(2,1)S(1)}, u32[]{:S(2)}, u32[]{:S(2)}) collective-permute-start(bf16[4,8,128,128]{3,2,1,0:T(8,128)(2,1)} %get-tuple-element.122), channel_id=1, source_target_pairs={{0,1},{1,0},{2,3},{3,2},{4,5},{5,4},{6,7},{7,6},{8,9},{9,8},{10,11... | collective-permute-start | bytes 3145736 | tf_op jit(solution)/shard_map/ppermute | solution.py:623
  125.3 23.6 %collective-permute-start.1 = (bf16[2,8,128,128]{3,2,1,0:T(8,128)(2,1)}, bf16[2,8,128,128]{3,2,1,0:T(8,128)(2,1)S(1)}, u32[]{:S(2)}, u32[]{:S(2)}) collective-permute-start(bf16[2,8,128,128]{3,2,1,0:T(8,128)(2,1)} %get-tuple-element.124), channel_id=1, source_target_pairs={{0,2},{2,4},{4,6},{6,0},{1,3},{3,5},{5,7},{7,1},{8,10},{10,12},{12... | collective-permute-start | bytes 1572872 | tf_op jit(solution)/shard_map/ppermute | solution.py:506
  126.8 24.9 %collective-permute-start.2 = (bf16[2,8,128,128]{3,2,1,0:T(8,128)(2,1)}, bf16[2,8,128,128]{3,2,1,0:T(8,128)(2,1)S(1)}, u32[]{:S(2)}, u32[]{:S(2)}) collective-permute-start(bf16[2,8,128,128]{3,2,1,0:T(8,128)(2,1)} %get-tuple-element.125), channel_id=1, source_target_pairs={{0,4},{2,6},{4,0},{6,2},{1,5},{3,7},{5,1},{7,3},{8,12},{10,14},{12... | collective-permute-start | bytes 1572872 | tf_op jit(solution)/shard_map/ppermute | solution.py:506
  129.5 22.2 %collective-permute-start.3 = (bf16[2,8,128,128]{3,2,1,0:T(8,128)(2,1)}, bf16[2,8,128,128]{3,2,1,0:T(8,128)(2,1)S(1)}, u32[]{:S(2)}, u32[]{:S(2)}) collective-permute-start(bf16[2,8,128,128]{3,2,1,0:T(8,128)(2,1)} %get-tuple-element.126), channel_id=1, source_target_pairs={{0,6},{2,0},{4,2},{6,4},{1,7},{3,1},{5,3},{7,5},{8,14},{10,8},{12,... | collective-permute-start | bytes 1572872 | tf_op jit(solution)/shard_map/ppermute | solution.py:506
  148.9 15.7 %copy-start.5 = (bf16[2,8,128,128]{3,2,1,0:T(8,128)(2,1)}, bf16[2,8,128,128]{3,2,1,0:T(8,128)(2,1)S(1)}, u32[]{:S(2)}) copy-start(bf16[2,8,128,128]{3,2,1,0:T(8,128)(2,1)S(1)} %collective-permute-done.1.refs_1_) | copy-start | bytes 1572868
  151.7 12.9 %copy-start.6 = (bf16[2,8,128,128]{3,2,1,0:T(8,128)(2,1)}, bf16[2,8,128,128]{3,2,1,0:T(8,128)(2,1)S(1)}, u32[]{:S(2)}) copy-start(bf16[2,8,128,128]{3,2,1,0:T(8,128)(2,1)S(1)} %collective-permute-done.2.refs_2_) | copy-start | bytes 1572868
  151.7 12.9 %copy-start.7 = (bf16[2,8,128,128]{3,2,1,0:T(8,128)(2,1)}, bf16[2,8,128,128]{3,2,1,0:T(8,128)(2,1)S(1)}, u32[]{:S(2)}) copy-start(bf16[2,8,128,128]{3,2,1,0:T(8,128)(2,1)S(1)} %collective-permute-done.3.refs_3_) | copy-start | bytes 1572868
  151.7 10.4 %copy-start.4 = (bf16[4,8,128,128]{3,2,1,0:T(8,128)(2,1)}, bf16[4,8,128,128]{3,2,1,0:T(8,128)(2,1)S(1)}, u32[]{:S(2)}) copy-start(bf16[4,8,128,128]{3,2,1,0:T(8,128)(2,1)S(1)} %collective-permute-done.came) | copy-start | bytes 3145732
  155.4 26.4 %all-to-all-start.7 = ((bf16[4,640,128]{2,1,0:T(8,128)(2,1)}), bf16[4,640,128]{2,1,0:T(8,128)(2,1)S(1)}, u32[]{:S(2)}, u32[]{:S(2)}) async-start(bf16[4,640,128]{2,1,0:T(8,128)(2,1)} %pad_maximum_fusion), calls=%async_computation.8 | async-start | bytes 1310720 | tf_op jit(solution)/shard_map/all_to_all | solution.py:629
  164.6 11.3 %collective-permute-start.5 = (bf16[8,128,128]{2,1,0:T(8,128)(2,1)}, bf16[8,128,128]{2,1,0:T(8,128)(2,1)S(1)}, u32[]{:S(2)}, u32[]{:S(2)}) collective-permute-start(bf16[8,128,128]{2,1,0:T(8,128)(2,1)} %get-tuple-element.140), channel_id=1, source_target_pairs={{0,2},{2,4},{4,6},{6,0},{1,3},{3,5},{5,7},{7,1},{8,10},{10,12},{12... | collective-permute-start | bytes 786440 | tf_op jit(solution)/shard_map/ppermute | solution.py:506
  166.0 12.7 %collective-permute-start.6 = (bf16[8,128,128]{2,1,0:T(8,128)(2,1)}, bf16[8,128,128]{2,1,0:T(8,128)(2,1)S(1)}, u32[]{:S(2)}, u32[]{:S(2)}) collective-permute-start(bf16[8,128,128]{2,1,0:T(8,128)(2,1)} %get-tuple-element.141), channel_id=1, source_target_pairs={{0,4},{2,6},{4,0},{6,2},{1,5},{3,7},{5,1},{7,3},{8,12},{10,14},{12... | collective-permute-start | bytes 786440 | tf_op jit(solution)/shard_map/ppermute | solution.py:506
  170.1 8.7 %collective-permute-start.7 = (bf16[8,128,128]{2,1,0:T(8,128)(2,1)}, bf16[8,128,128]{2,1,0:T(8,128)(2,1)S(1)}, u32[]{:S(2)}, u32[]{:S(2)}) collective-permute-start(bf16[8,128,128]{2,1,0:T(8,128)(2,1)} %get-tuple-element.142), channel_id=1, source_target_pairs={{0,6},{2,0},{4,2},{6,4},{1,7},{3,1},{5,3},{7,5},{8,14},{10,8},{12,... | collective-permute-start | bytes 786440 | tf_op jit(solution)/shard_map/ppermute | solution.py:506
  173.5 13.2 %collective-permute-start.4 = (bf16[8,128,128]{2,1,0:T(8,128)(2,1)}, bf16[8,128,128]{2,1,0:T(8,128)(2,1)S(1)}, u32[]{:S(2)}, u32[]{:S(2)}) collective-permute-start(bf16[8,128,128]{2,1,0:T(8,128)(2,1)} %get-tuple-element.132), channel_id=1, source_target_pairs={{0,1},{1,0},{2,3},{3,2},{4,5},{5,4},{6,7},{7,6},{8,9},{9,8},{10,11... | collective-permute-start | bytes 786440 | tf_op jit(solution)/shard_map/ppermute | solution.py:633
  183.1 10.0 %all-to-all-start.8 = ((bf16[8,16,128]{2,1,0:T(8,128)(2,1)}), bf16[8,16,128]{2,1,0:T(8,128)(2,1)S(1)}, u32[]{:S(2)}, u32[]{:S(2)}) async-start(bf16[8,16,128]{2,1,0:T(8,128)(2,1)} %broadcast_in_dim.202), calls=%async_computation.9 | async-start | bytes 65536 | tf_op jit(solution)/shard_map/all_to_all | solution.py:492
  (13 other events, 39.2 us)
Sparse Core Ops, SparseCore 0:
  11.2 62.6 all-gather.1
  108.0 45.4 reduce-scatter.1

commit v5 on v4

--- a/solution.py
+++ b/solution.py
@@ -254,11 +254,8 @@
 
 
 def down_grads_body(
-    meta, got, dlin, back_latent, cot_far, perm, perm2, start, grad, hd, part, hd_t, ding, full,
-    cot, sem, cot_sem,
+    meta, got, dlin, back_latent, cot, perm, perm2, start, grad, hd, part, hd_t, ding, full, sem
 ):
-    load = pltpu.make_async_copy(cot_far, cot, cot_sem)
-    load.start()
     back = back_latent[...]
     back_t = turned(jnp.concatenate([back, back], axis=1))[:RANK]
     down_sum = jnp.zeros((BLK, RANK), F32)
@@ -270,7 +267,6 @@
         down_sum = down_sum + dot_t(h, dlin[t])
         ding[t] = dot(back_t, h).astype(BF16)
     part[...] = down_sum
-    load.wait()
 
     def store(block, rows):
         full[:, 4 * block : 4 * block + 16, :] = rows.reshape(NDP, 16, BLK)
@@ -591,12 +587,11 @@
     grad, hd, part_down = pl.pallas_call(
         down_grads_body,
         out_shape=(grad_shape, slots, shape(BLK, RANK, dtype=F32)),
-        in_specs=[smem] + [vmem] * 3 + [hbm] + [vmem] * 2 + [hbm],
+        in_specs=[smem] + [vmem] * 6 + [hbm],
         out_specs=(hbm, vmem, vmem),
         scratch_shapes=[
             slots_scratch, pltpu.VMEM((SLOTS, RANK, BLK), BF16),
-            pltpu.VMEM((NDP, 4 * (GRAD - GRAD_A), BLK), BF16),
-            pltpu.VMEM((BLK, COLS * BLK), BF16), pltpu.SemaphoreType.DMA, pltpu.SemaphoreType.DMA,
+            pltpu.VMEM((NDP, 4 * (GRAD - GRAD_A), BLK), BF16), pltpu.SemaphoreType.DMA,
         ],
         input_output_aliases={7: 0},
         compiler_params=pltpu.CompilerParams(vmem_limit_bytes=VMEM_LIMIT),
@@ -628,15 +623,16 @@
     grad = jnp.concatenate([grad.reshape(4, 4 * GRAD, BLK), small], axis=1)
     grad = lax.all_to_all(grad, "zh", 0, 0, tiled=True)
     half = shape(SHARE, BLK, BLK)
+    out_keep, out_give = call(out_y_body, (half,) * 2, out_got, (meta,))
+    token_came, out_give = together((token_came, out_give))
+    out_came = lax.ppermute(out_give, "zl", swap)
     token_got = rotate(call(token_pair_body, (half,) * NY, (token_part[0], token_came), ()))
-    out_keep, out_give = call(out_y_body, (half,) * 2, out_got, (meta,))
-    out_came = lax.ppermute(out_give, "zl", swap)
     wide = shape(BLK, SHARE * BLK)
     token_grad = call(token_out_body, wide, (*token_got, latents, low_share), ())
-    grad, token_grad = together((grad, token_grad))
+    layer_out = call(layer_out_body, wide, (out_keep, out_came, latents, dlout), ())
+    grad, token_grad, layer_out = together((grad, token_grad, layer_out))
     small = jnp.sum(grad[:, 4 * GRAD :].astype(F32), axis=0).astype(BF16)
     low_g = spread(small[:16], MP, NMP)
-    layer_out = call(layer_out_body, wide, (out_keep, out_came, latents, dlout), ())
     wide = shape(SLOTS, DEPTH, 4, BLK)
     gate_g, up_g, down_g, mid_g, tail = call(
         final_body, (wide, wide, wide, shape(4, SLOTS * BLK), shape(8, 4, BLK)),

time: 205 us -> 209 us (1.020)
  waiting for transfers between devices: 25.9 us -> 30.6 us
    ppermute x1, waiting for transfers between devices: 0.01 us -> 6.71 us  [local(): out_came = lax.ppermute(out_give, 'zl', swap)]
    ppermute x6, waiting for transfers between devices: 7.21 us -> 2.7 us  [rotate(): lax.ppermute(parts[k], 'y', [(i, (i + k) % NY) for i in range(NY)])]
    all_to_all x4, waiting for transfers between devices: 9.86 us -> 12.4 us  [spread(): lax.all_to_all(jnp.broadcast_to(x[None], (n,) + x.shape), axis, 0, 0, til...]
  transfers between devices with their start and end apart: 17 -> 17, of which waited for: 8 -> 8; matrix products, arithmetic and copies ran while one was open for 9% -> 8% of each run, Pallas kernels for 27% -> 26%
where the time goes in v5:
time: 209 us; the launch traced here: 205 us
  Pallas kernels  61.6 us (29%)
  starting transfers between devices  52.6 us (25%)
  waiting for transfers between devices  30.6 us (15%)
  blocking collectives  20.3 us (10%)
  local copies, waits for them, and re-layouts  18.7 us (9%)
  between operations  14.4 us (7%)
  other arithmetic  7.21 us (3%)
    pallas_call x11, Pallas kernels, call(): pl.pallas_call(body, out_shape=out_shapes, in_specs=[smem] * len(scalars)...  34.2 us
    all_to_all x4, starting transfers between devices, spread(): lax.all_to_all(jnp.broadcast_to(x[None], (n,) + x.shape), axis, 0, 0, til...  22.8 us
    all_to_all x1, blocking collectives, local(): lax.all_to_all(small.reshape(8, BLK, BLK), ('x', 'core'), 0, 0, tiled=True)  14.2 us
    all_to_all x4, waiting for transfers between devices, spread(): lax.all_to_all(jnp.broadcast_to(x[None], (n,) + x.shape), axis, 0, 0, til...  12.4 us
    ppermute x6, starting transfers between devices, rotate(): lax.ppermute(parts[k], 'y', [(i, (i + k) % NY) for i in range(NY)])  11.7 us
    pallas_call x1, Pallas kernels, local(): pl.pallas_call(up_grads_body, out_shape=(grad_shape, shape(SLOTS, BLK, 2...  10.9 us
    pallas_call x1, Pallas kernels, local(): pl.pallas_call(forward_body, out_shape=(parcel, shape(SLOTS, BLK, 2 * BLK...  10 us
    unnamed x43, local copies, waits for them, and re-layouts  8.61 us
  transfers between devices with their start and end apart: 17, of which 8 were waited for; matrix products, arithmetic and copies ran while one was open for 8% of the time, Pallas kernels for 26%

profile of v5, /device:TPU:64, one launch (start us, length us, event | category | flops | bytes accessed | tf_op | source)
XLA Modules:
  0.0 205.3 jit_solution(6483432620722029689)
XLA Ops:
  15.1 8.1 %all-to-all-start = ((bf16[4,1,224,128]{3,2,1,0:T(8,128)(2,1)}), bf16[4,1,224,128]{3,2,1,0:T(8,128)(2,1)S(1)}, u32[]{:S(2)}, u32[]{:S(2)}) async-start(bf16[4,1,224,128]{3,2,1,0:T(8,128)(2,1)} %broadcast_in_dim.181), calls=%async_computation | async-start | bytes 458752 | tf_op jit(solution)/shard_map/all_to_all | solution.py:488
  23.2 4.1 %copy.60 = bf16[128,8192]{0,1:T(8,128)(2,1)} copy(bf16[128,8192]{1,0:T(8,128)(2,1)} %tok_far.1) | data formatting | bytes 4194304 | tf_op args[0]
  33.1 5.0 %all-to-all-start.1 = ((bf16[4,4,224,128]{3,2,1,0:T(8,128)(2,1)}), bf16[4,4,224,128]{3,2,1,0:T(8,128)(2,1)S(1)}, u32[]{:S(2)}, u32[]{:S(2)}) async-start(bf16[4,4,224,128]{3,2,1,0:T(8,128)(2,1)} %broadcast_in_dim.182), calls=%async_computation.1 | async-start | bytes 1835008 | tf_op jit(solution)/shard_map/all_to_all | solution.py:488
  40.9 9.2 %all-to-all-done.1 = bf16[4,4,224,128]{3,2,1,0:T(8,128)(2,1)S(1)} async-done(((bf16[4,4,224,128]{3,2,1,0:T(8,128)(2,1)}), bf16[4,4,224,128]{3,2,1,0:T(8,128)(2,1)S(1)}, u32[]{:S(2)}, u32[]{:S(2)}) %all-to-all-start.1) | async-done | bytes 917536 | tf_op jit(solution)/shard_map/all_to_all | solution.py:488
  50.3 6.1 %all_to_all.45 = bf16[2,16,224,128]{3,2,1,0:T(8,128)(2,1)} all-to-all(bf16[2,16,224,128]{3,2,1,0:T(8,128)(2,1)S(1)} %broadcast_in_dim.200), channel_id=1, replica_groups=mesh['zh'=4,'x'=4,'core'=2,'y'=4,'zl'=2] {'core'}, dimensions={0} | all-to-all | bytes 3670016 | tf_op jit(solution)/shard_map/all_to_all | solution.py:488
  56.4 6.7 %shard_map.216 = (bf16[8,512,128]{2,1,0:T(8,128)(2,1)}, bf16[43,128,128]{2,1,0:T(8,128)(2,1)}, bf16[14,64,128]{2,1,0:T(8,128)(2,1)}, bf16[512,128]{1,0:T(8,128)(2,1)}) custom-call(s32[560]{0:T(1024)} %concatenate.21.meta, bf16[32,224,128]{2,1,0:T(8,128)(2,1)} %bitcast.40, bf16[128,8192]{1,0:T(8,128)(2,1)} %cot.5, bf16[512,512]{1,0:T(8,128)(2,1)} %get-tuple-element.220.perm, ...), custom_call_target="tpu_custom_call" | custom-call | tf_op jit(solution)/shard_map/pallas_call | solution.py:54
  63.1 5.0 %all-to-all-start.3 = ((bf16[8,512,128]{2,1,0:T(8,128)(2,1)}), bf16[8,512,128]{2,1,0:T(8,128)(2,1)S(1)}, u32[]{:S(2)}, u32[]{:S(2)}) async-start(bf16[8,512,128]{2,1,0:T(8,128)(2,1)} %get-tuple-element.97), calls=%async_computation.3 | async-start | bytes 2097152 | tf_op jit(solution)/shard_map/all_to_all | solution.py:551
  68.1 5.7 %all-gather.2.cloned.1.call-done.got_far = bf16[32,528,128]{2,1,0:T(8,128)(2,1)} async-done(((bf16[1,528,128]{2,1,0:T(8,128)(2,1)}), bf16[32,528,128]{2,1,0:T(8,128)(2,1)}) %all-gather.2.cloned.1.call-update) | async-done | bytes 4325392 | tf_op jit(solution)/shard_map/all_gather | solution.py:527
  73.8 10.0 %shard_map.217 = (bf16[8,2,128,128]{3,2,1,0:T(8,128)(2,1)}, f32[14,128,256]{2,1,0:T(8,128)}, bf16[43,128,256]{2,1,0:T(8,128)(2,1)}, bf16[14,128,128]{2,1,0:T(8,1...) custom-call(s32[560]{0:T(1024)} %concatenate.21.meta, ...), custom_call_target="tpu_custom_call" | custom-call | tf_op jit(solution)/shard_map/pallas_call | solution.py:557
  85.2 3.5 %all-to-all-start.4 = ((bf16[8,2,128,128]{3,2,1,0:T(8,128)(2,1)}), bf16[8,2,128,128]{3,2,1,0:T(8,128)(2,1)S(1)}, u32[]{:S(2)}, u32[]{:S(2)}) async-start(bf16[8,2,128,128]{3,2,1,0:T(8,128)(2,1)} %get-tuple-element.106), calls=%async_computation.4 | async-start | bytes 1048576 | tf_op jit(solution)/shard_map/all_to_all | solution.py:572
  89.0 10.9 %shard_map.218 = (bf16[32,608,128]{2,1,0:T(8,128)(2,1)}, bf16[14,128,256]{2,1,0:T(8,128)(2,1)}, f32[128,64]{1,0:T(8,128)}, bf16[128,64]{1,0:T(8,128)(2,1)}) custom-call(s32[560]{0:T(1024)} %concatenate.21.meta, bf16[8,512,128]{2,1,0:T(8,128)(2,1)} %copy-done, f32[14,128,256]{2,1,0:T(8,128)} %get-tuple-element.100.act, ...), custom_call_target="tpu_custom_call" | custom-call | tf_op jit(solution)/shard_map/pallas_call | solution.py:575
  100.7 6.4 %shard_map.219 = (bf16[32,608,128]{2,1,0:T(8,128)(2,1)}, bf16[14,128,128]{2,1,0:T(8,128)(2,1)}, f32[128,64]{1,0:T(8,128)}) custom-call(s32[560]{0:T(1024)} %concatenate.21.meta, bf16[8,2,128,128]{3,2,1,0:T(8,128)(2,1)} %copy-done.2, bf16[14,64,128]{2,1,0:T(8,128)(2,1)} %get-tuple-element.107.dlin, ...), custom_call_target="tpu_custom_call", output_to_operand_aliasing={{0}: (7, {})} | custom-call | tf_op jit(solution)/shard_map/pallas_call | solution.py:587
  108.8 5.4 %all-to-all-start.5 = ((bf16[8,128,128]{2,1,0:T(8,128)(2,1)}), bf16[8,128,128]{2,1,0:T(8,128)(2,1)S(1)}, u32[]{:S(2)}, u32[]{:S(2)}) async-start(bf16[8,128,128]{2,1,0:T(8,128)(2,1)} %broadcast_in_dim.201), calls=%async_computation.5 | async-start | bytes 524288 | tf_op jit(solution)/shard_map/all_to_all | solution.py:488
  114.2 4.6 %shard_map.220 = (bf16[4,8,128,128]{3,2,1,0:T(8,128)(2,1)}, bf16[4,8,128,128]{3,2,1,0:T(8,128)(2,1)}) custom-call(s32[560]{0:T(1024)} %concatenate.21.meta, bf16[14,128,256]{2,1,0:T(8,128)(2,1)} %get-tuple-element.112.gu, bf16[43,128,256]{2,1,0:T(8,128)(2,1)} %get-tuple-element.113.w_gu), custom_call_target="tpu_custom_call" | custom-call | tf_op jit(solution)/shard_map/pallas_call | solution.py:54
  118.8 3.8 %shard_map.221 = (bf16[2,8,128,128]{3,2,1,0:T(8,128)(2,1)}, bf16[2,8,128,128]{3,2,1,0:T(8,128)(2,1)}, bf16[2,8,128,128]{3,2,1,0:T(8,128)(2,1)}, bf16[2,8,128,128]{3,2,1,0:T(8,128)(2,1)}) custom-call(s32[560]{0:T(1024)} %concatenate.21.meta, bf16[14,128,128]{2,1,0:T(8,128)(2,1)} %get-tuple-element.116.hd, bf16[43,128,128]{2,1,0:T(8,128)(2,1)} %get-tuple-element.117.w_d), custom_call_target="tpu_custom_call" | custom-call | tf_op jit(solution)/shard_map/pallas_call | solution.py:54
  126.1 2.7 %collective-permute-start.2 = (bf16[2,8,128,128]{3,2,1,0:T(8,128)(2,1)}, bf16[2,8,128,128]{3,2,1,0:T(8,128)(2,1)S(1)}, u32[]{:S(2)}, u32[]{:S(2)}) collective-permute-start(bf16[2,8,128,128]{3,2,1,0:T(8,128)(2,1)} %get-tuple-element.128), channel_id=1, source_target_pairs={{0,4},{2,6},{4,0},{6,2},{1,5},{3,7},{5,1},{7,3},{8,12},{10,14},{12... | collective-permute-start | bytes 1572872 | tf_op jit(solution)/shard_map/ppermute | solution.py:502
  130.2 3.7 %shard_map.222 = (bf16[2,128,64]{2,1,0:T(8,128)(2,1)}, bf16[32,32,128]{2,1,0:T(8,128)(2,1)}) custom-call(s32[560]{0:T(1024)} %concatenate.21.meta, bf16[8,128,128]{2,1,0:T(8,128)(2,1)} %copy-done.3, bf16[64,128,128]{2,1,0:T(8,128)(2,1)} %bitcast.39, bf16[128,8192]{1,0:T(8,128)(2,1)} %cot.5, bf16[512,512]{1,0:T(8,128)(2,1)} %fusion.2.perm2), custom_call_target="tpu_custom_call" | custom-call | tf_op jit(solution)/shard_map/pallas_call | solution.py:54
  134.0 14.2 %all_to_all.46 = bf16[8,128,128]{2,1,0:T(8,128)(2,1)S(1)} all-to-all(bf16[8,128,128]{2,1,0:T(8,128)(2,1)} %bitcast.46), channel_id=1, replica_groups=mesh['zh'=4,'x'=4,'core'=2,'y'=4,'zl'=2] {'x','core'}, dimensions={0} | all-to-all | bytes 524288 | tf_op jit(solution)/shard_map/all_to_all | solution.py:620
  148.3 2.7 %collective-permute-done.2.refs_2_ = bf16[2,8,128,128]{3,2,1,0:T(8,128)(2,1)S(1)} collective-permute-done((bf16[2,8,128,128]{3,2,1,0:T(8,128)(2,1)}, bf16[2,8,128,128]{3,2,1,0:T(8,128)(2,1)S(1)}, u32[]{:S(2)}, u32[]{:S(2)}) %collective-permute-start.2) | collective-permute-done | bytes 524320 | tf_op jit(solution)/shard_map/ppermute | solution.py:502
  154.7 6.7 %all-to-all-start.7 = ((bf16[4,640,128]{2,1,0:T(8,128)(2,1)}), bf16[4,640,128]{2,1,0:T(8,128)(2,1)S(1)}, u32[]{:S(2)}, u32[]{:S(2)}) async-start(bf16[4,640,128]{2,1,0:T(8,128)(2,1)} %pad_maximum_fusion), calls=%async_computation.8 | async-start | bytes 1310720 | tf_op jit(solution)/shard_map/all_to_all | solution.py:624
  164.5 2.6 %shard_map.224 = (bf16[8,128,128]{2,1,0:T(8,128)(2,1)}, bf16[8,128,128]{2,1,0:T(8,128)(2,1)}, bf16[8,128,128]{2,1,0:T(8,128)(2,1)}, bf16[8,128,128]{2,1,0:T(8,128)(2,1)}) custom-call(bf16[4,8,128,128]{3,2,1,0:T(8,128)(2,1)} %get-tuple-element.132.keep, bf16[4,8,128,128]{3,2,1,0:T(8,128)(2,1)} %copy-done.4), custom_call_target="tpu_custom_call" | custom-call | tf_op jit(solution)/shard_map/pallas_call | solution.py:54
  168.2 3.9 %collective-permute-start.5 = (bf16[8,128,128]{2,1,0:T(8,128)(2,1)}, bf16[8,128,128]{2,1,0:T(8,128)(2,1)S(1)}, u32[]{:S(2)}, u32[]{:S(2)}) collective-permute-start(bf16[8,128,128]{2,1,0:T(8,128)(2,1)} %get-tuple-element.142), channel_id=1, source_target_pairs={{0,4},{2,6},{4,0},{6,2},{1,5},{3,7},{5,1},{7,3},{8,12},{10,14},{12... | collective-permute-start | bytes 786440 | tf_op jit(solution)/shard_map/ppermute | solution.py:502
  173.2 6.7 %collective-permute-done.7.came = bf16[8,128,128]{2,1,0:T(8,128)(2,1)S(1)} collective-permute-done((bf16[8,128,128]{2,1,0:T(8,128)(2,1)}, bf16[8,128,128]{2,1,0:T(8,128)(2,1)S(1)}, u32[]{:S(2)}, u32[]{:S(2)}) %collective-permute-start.7) | collective-permute-done | bytes 262176 | tf_op jit(solution)/shard_map/ppermute | solution.py:628
  187.1 4.3 %all-to-all-start.8 = ((bf16[8,16,128]{2,1,0:T(8,128)(2,1)}), bf16[8,16,128]{2,1,0:T(8,128)(2,1)S(1)}, u32[]{:S(2)}, u32[]{:S(2)}) async-start(bf16[8,16,128]{2,1,0:T(8,128)(2,1)} %broadcast_in_dim.202), calls=%async_computation.9 | async-start | bytes 65536 | tf_op jit(solution)/shard_map/all_to_all | solution.py:488
  (143 shorter events, 48.9 us)
Async XLA Ops:
  7.2 66.7 %all-gather.2.cloned.1.call-start = ((), (), s32[]{:S(2)}) async-start(), calls=%async_computation.10 | async-start | bytes 4460544 | tf_op jit(solution)/shard_map/all_gather | solution.py:527
  15.1 16.4 %all-to-all-start = ((bf16[4,1,224,128]{3,2,1,0:T(8,128)(2,1)}), bf16[4,1,224,128]{3,2,1,0:T(8,128)(2,1)S(1)}, u32[]{:S(2)}, u32[]{:S(2)}) async-start(bf16[4,1,224,128]{3,2,1,0:T(8,128)(2,1)} %broadcast_in_dim.181), calls=%async_computation | async-start | bytes 458752 | tf_op jit(solution)/shard_map/all_to_all | solution.py:488
  29.5 8.7 %copy-start.16 = (s32[112]{0:T(128)S(1)}, s32[112]{0:T(128)}, u32[]{:S(2)}) copy-start(s32[112]{0:T(128)} %param.25) | copy-start | bytes 1348
  29.5 9.7 %copy-start.14 = (s32[112,5]{0,1:T(8,128)S(1)}, s32[112,5]{0,1:T(8,128)}, u32[]{:S(2)}) copy-start(s32[112,5]{0,1:T(8,128)} %param.27) | copy-start | bytes 6724
  29.5 9.7 %copy-start.15 = (s32[112,5]{0,1:T(8,128)S(1)}, s32[112,5]{0,1:T(8,128)}, u32[]{:S(2)}) copy-start(s32[112,5]{0,1:T(8,128)} %param.26) | copy-start | bytes 6724
  33.1 17.0 %all-to-all-start.1 = ((bf16[4,4,224,128]{3,2,1,0:T(8,128)(2,1)}), bf16[4,4,224,128]{3,2,1,0:T(8,128)(2,1)S(1)}, u32[]{:S(2)}, u32[]{:S(2)}) async-start(bf16[4,4,224,128]{3,2,1,0:T(8,128)(2,1)} %broadcast_in_dim.182), calls=%async_computation.1 | async-start | bytes 1835008 | tf_op jit(solution)/shard_map/all_to_all | solution.py:488
  63.1 22.1 %all-to-all-start.3 = ((bf16[8,512,128]{2,1,0:T(8,128)(2,1)}), bf16[8,512,128]{2,1,0:T(8,128)(2,1)S(1)}, u32[]{:S(2)}, u32[]{:S(2)}) async-start(bf16[8,512,128]{2,1,0:T(8,128)(2,1)} %get-tuple-element.97), calls=%async_computation.3 | async-start | bytes 2097152 | tf_op jit(solution)/shard_map/all_to_all | solution.py:551
  85.2 14.7 %all-to-all-start.4 = ((bf16[8,2,128,128]{3,2,1,0:T(8,128)(2,1)}), bf16[8,2,128,128]{3,2,1,0:T(8,128)(2,1)S(1)}, u32[]{:S(2)}, u32[]{:S(2)}) async-start(bf16[8,2,128,128]{3,2,1,0:T(8,128)(2,1)} %get-tuple-element.106), calls=%async_computation.4 | async-start | bytes 1048576 | tf_op jit(solution)/shard_map/all_to_all | solution.py:572
  88.7 64.0 %reduce-scatter.2.cloned.1.call-start = ((), (), s32[]{:S(2)}) async-start(), calls=%async_computation.11 | async-start | bytes 5603328 | tf_op jit(solution)/shard_map/reduce_scatter | solution.py:599
  108.8 13.8 %all-to-all-start.5 = ((bf16[8,128,128]{2,1,0:T(8,128)(2,1)}), bf16[8,128,128]{2,1,0:T(8,128)(2,1)S(1)}, u32[]{:S(2)}, u32[]{:S(2)}) async-start(bf16[8,128,128]{2,1,0:T(8,128)(2,1)} %broadcast_in_dim.201), calls=%async_computation.5 | async-start | bytes 524288 | tf_op jit(solution)/shard_map/all_to_all | solution.py:488
  122.6 28.3 %collective-permute-start = (bf16[4,8,128,128]{3,2,1,0:T(8,128)(2,1)}, bf16[4,8,128,128]{3,2,1,0:T(8,128)(2,1)S(1)}, u32[]{:S(2)}, u32[]{:S(2)}) collective-permute-start(bf16[4,8,128,128]{3,2,1,0:T(8,128)(2,1)} %get-tuple-element.125), channel_id=1, source_target_pairs={{0,1},{1,0},{2,3},{3,2},{4,5},{5,4},{6,7},{7,6},{8,9},{9,8},{10,11... | collective-permute-start | bytes 3145736 | tf_op jit(solution)/shard_map/ppermute | solution.py:618
  124.6 23.6 %collective-permute-start.1 = (bf16[2,8,128,128]{3,2,1,0:T(8,128)(2,1)}, bf16[2,8,128,128]{3,2,1,0:T(8,128)(2,1)S(1)}, u32[]{:S(2)}, u32[]{:S(2)}) collective-permute-start(bf16[2,8,128,128]{3,2,1,0:T(8,128)(2,1)} %get-tuple-element.127), channel_id=1, source_target_pairs={{0,2},{2,4},{4,6},{6,0},{1,3},{3,5},{5,7},{7,1},{8,10},{10,12},{12... | collective-permute-start | bytes 1572872 | tf_op jit(solution)/shard_map/ppermute | solution.py:502
  126.1 24.9 %collective-permute-start.2 = (bf16[2,8,128,128]{3,2,1,0:T(8,128)(2,1)}, bf16[2,8,128,128]{3,2,1,0:T(8,128)(2,1)S(1)}, u32[]{:S(2)}, u32[]{:S(2)}) collective-permute-start(bf16[2,8,128,128]{3,2,1,0:T(8,128)(2,1)} %get-tuple-element.128), channel_id=1, source_target_pairs={{0,4},{2,6},{4,0},{6,2},{1,5},{3,7},{5,1},{7,3},{8,12},{10,14},{12... | collective-permute-start | bytes 1572872 | tf_op jit(solution)/shard_map/ppermute | solution.py:502
  128.8 22.2 %collective-permute-start.3 = (bf16[2,8,128,128]{3,2,1,0:T(8,128)(2,1)}, bf16[2,8,128,128]{3,2,1,0:T(8,128)(2,1)S(1)}, u32[]{:S(2)}, u32[]{:S(2)}) collective-permute-start(bf16[2,8,128,128]{3,2,1,0:T(8,128)(2,1)} %get-tuple-element.129), channel_id=1, source_target_pairs={{0,6},{2,0},{4,2},{6,4},{1,7},{3,1},{5,3},{7,5},{8,14},{10,8},{12,... | collective-permute-start | bytes 1572872 | tf_op jit(solution)/shard_map/ppermute | solution.py:502
  148.3 13.1 %copy-start.5 = (bf16[2,8,128,128]{3,2,1,0:T(8,128)(2,1)}, bf16[2,8,128,128]{3,2,1,0:T(8,128)(2,1)S(1)}, u32[]{:S(2)}) copy-start(bf16[2,8,128,128]{3,2,1,0:T(8,128)(2,1)S(1)} %collective-permute-done.1.refs_1_) | copy-start | bytes 1572868
  150.9 10.4 %copy-start.6 = (bf16[2,8,128,128]{3,2,1,0:T(8,128)(2,1)}, bf16[2,8,128,128]{3,2,1,0:T(8,128)(2,1)S(1)}, u32[]{:S(2)}) copy-start(bf16[2,8,128,128]{3,2,1,0:T(8,128)(2,1)S(1)} %collective-permute-done.2.refs_2_) | copy-start | bytes 1572868
  151.0 10.4 %copy-start.7 = (bf16[2,8,128,128]{3,2,1,0:T(8,128)(2,1)}, bf16[2,8,128,128]{3,2,1,0:T(8,128)(2,1)S(1)}, u32[]{:S(2)}) copy-start(bf16[2,8,128,128]{3,2,1,0:T(8,128)(2,1)S(1)} %collective-permute-done.3.refs_3_) | copy-start | bytes 1572868
  151.0 12.9 %copy-start.4 = (bf16[4,8,128,128]{3,2,1,0:T(8,128)(2,1)}, bf16[4,8,128,128]{3,2,1,0:T(8,128)(2,1)S(1)}, u32[]{:S(2)}) copy-start(bf16[4,8,128,128]{3,2,1,0:T(8,128)(2,1)S(1)} %collective-permute-done.came) | copy-start | bytes 3145732
  154.7 31.2 %all-to-all-start.7 = ((bf16[4,640,128]{2,1,0:T(8,128)(2,1)}), bf16[4,640,128]{2,1,0:T(8,128)(2,1)S(1)}, u32[]{:S(2)}, u32[]{:S(2)}) async-start(bf16[4,640,128]{2,1,0:T(8,128)(2,1)} %pad_maximum_fusion), calls=%async_computation.8 | async-start | bytes 1310720 | tf_op jit(solution)/shard_map/all_to_all | solution.py:624
  163.8 16.1 %collective-permute-start.7 = (bf16[8,128,128]{2,1,0:T(8,128)(2,1)}, bf16[8,128,128]{2,1,0:T(8,128)(2,1)S(1)}, u32[]{:S(2)}, u32[]{:S(2)}) collective-permute-start(bf16[8,128,128]{2,1,0:T(8,128)(2,1)} %get-tuple-element.147), channel_id=1, source_target_pairs={{0,1},{1,0},{2,3},{3,2},{4,5},{5,4},{6,7},{7,6},{8,9},{9,8},{10,11... | collective-permute-start | bytes 786440 | tf_op jit(solution)/shard_map/ppermute | solution.py:628
  167.1 15.5 %collective-permute-start.4 = (bf16[8,128,128]{2,1,0:T(8,128)(2,1)}, bf16[8,128,128]{2,1,0:T(8,128)(2,1)S(1)}, u32[]{:S(2)}, u32[]{:S(2)}) collective-permute-start(bf16[8,128,128]{2,1,0:T(8,128)(2,1)} %get-tuple-element.141), channel_id=1, source_target_pairs={{0,2},{2,4},{4,6},{6,0},{1,3},{3,5},{5,7},{7,1},{8,10},{10,12},{12... | collective-permute-start | bytes 786440 | tf_op jit(solution)/shard_map/ppermute | solution.py:502
  168.2 14.5 %collective-permute-start.5 = (bf16[8,128,128]{2,1,0:T(8,128)(2,1)}, bf16[8,128,128]{2,1,0:T(8,128)(2,1)S(1)}, u32[]{:S(2)}, u32[]{:S(2)}) collective-permute-start(bf16[8,128,128]{2,1,0:T(8,128)(2,1)} %get-tuple-element.142), channel_id=1, source_target_pairs={{0,4},{2,6},{4,0},{6,2},{1,5},{3,7},{5,1},{7,3},{8,12},{10,14},{12... | collective-permute-start | bytes 786440 | tf_op jit(solution)/shard_map/ppermute | solution.py:502
  172.1 10.6 %collective-permute-start.6 = (bf16[8,128,128]{2,1,0:T(8,128)(2,1)}, bf16[8,128,128]{2,1,0:T(8,128)(2,1)S(1)}, u32[]{:S(2)}, u32[]{:S(2)}) collective-permute-start(bf16[8,128,128]{2,1,0:T(8,128)(2,1)} %get-tuple-element.143), channel_id=1, source_target_pairs={{0,6},{2,0},{4,2},{6,4},{1,7},{3,1},{5,3},{7,5},{8,14},{10,8},{12,... | collective-permute-start | bytes 786440 | tf_op jit(solution)/shard_map/ppermute | solution.py:502
  187.1 10.6 %all-to-all-start.8 = ((bf16[8,16,128]{2,1,0:T(8,128)(2,1)}), bf16[8,16,128]{2,1,0:T(8,128)(2,1)S(1)}, u32[]{:S(2)}, u32[]{:S(2)}) async-start(bf16[8,16,128]{2,1,0:T(8,128)(2,1)} %broadcast_in_dim.202), calls=%async_computation.9 | async-start | bytes 65536 | tf_op jit(solution)/shard_map/all_to_all | solution.py:488
  (13 other events, 35.3 us)
Sparse Core Ops, SparseCore 0:
  11.2 62.6 all-gather.1
  107.2 45.4 reduce-scatter.1

commit v6 on v5

--- a/solution.py
+++ b/solution.py
@@ -623,16 +623,15 @@
     grad = jnp.concatenate([grad.reshape(4, 4 * GRAD, BLK), small], axis=1)
     grad = lax.all_to_all(grad, "zh", 0, 0, tiled=True)
     half = shape(SHARE, BLK, BLK)
+    token_got = rotate(call(token_pair_body, (half,) * NY, (token_part[0], token_came), ()))
     out_keep, out_give = call(out_y_body, (half,) * 2, out_got, (meta,))
-    token_came, out_give = together((token_came, out_give))
     out_came = lax.ppermute(out_give, "zl", swap)
-    token_got = rotate(call(token_pair_body, (half,) * NY, (token_part[0], token_came), ()))
     wide = shape(BLK, SHARE * BLK)
     token_grad = call(token_out_body, wide, (*token_got, latents, low_share), ())
-    layer_out = call(layer_out_body, wide, (out_keep, out_came, latents, dlout), ())
-    grad, token_grad, layer_out = together((grad, token_grad, layer_out))
+    grad, token_grad = together((grad, token_grad))
     small = jnp.sum(grad[:, 4 * GRAD :].astype(F32), axis=0).astype(BF16)
     low_g = spread(small[:16], MP, NMP)
+    layer_out = call(layer_out_body, wide, (out_keep, out_came, latents, dlout), ())
     wide = shape(SLOTS, DEPTH, 4, BLK)
     gate_g, up_g, down_g, mid_g, tail = call(
         final_body, (wide, wide, wide, shape(4, SLOTS * BLK), shape(8, 4, BLK)),

time: 209 us -> 204 us (0.976)
  waiting for transfers between devices: 30.6 us -> 25.8 us
    ppermute x1, waiting for transfers between devices: 6.71 us -> 0.01 us  [local(): out_came = lax.ppermute(out_give, 'zl', swap)]
    ppermute x6, waiting for transfers between devices: 2.7 us -> 7.2 us  [rotate(): lax.ppermute(parts[k], 'y', [(i, (i + k) % NY) for i in range(NY)])]
    all_to_all x4, waiting for transfers between devices: 12.4 us -> 9.86 us  [spread(): lax.all_to_all(jnp.broadcast_to(x[None], (n,) + x.shape), axis, 0, 0, til...]
  transfers between devices with their start and end apart: 17 -> 17, of which waited for: 8 -> 8; matrix products, arithmetic and copies ran while one was open for 8% -> 9% of each run, Pallas kernels for 26% -> 27%
where the time goes in v6:
time: 204 us; the launch traced here: 200 us
  Pallas kernels  61.5 us (30%)
  starting transfers between devices  52.3 us (26%)
  waiting for transfers between devices  25.8 us (13%)
  blocking collectives  20.3 us (10%)
  local copies, waits for them, and re-layouts  18.6 us (9%)
  between operations  14.4 us (7%)
  other arithmetic  7.21 us (4%)
    pallas_call x11, Pallas kernels, call(): pl.pallas_call(body, out_shape=out_shapes, in_specs=[smem] * len(scalars)...  34.2 us
    all_to_all x4, starting transfers between devices, spread(): lax.all_to_all(jnp.broadcast_to(x[None], (n,) + x.shape), axis, 0, 0, til...  22.1 us
    all_to_all x1, blocking collectives, local(): lax.all_to_all(small.reshape(8, BLK, BLK), ('x', 'core'), 0, 0, tiled=True)  14.2 us
    ppermute x6, starting transfers between devices, rotate(): lax.ppermute(parts[k], 'y', [(i, (i + k) % NY) for i in range(NY)])  12 us
    pallas_call x1, Pallas kernels, local(): pl.pallas_call(up_grads_body, out_shape=(grad_shape, shape(SLOTS, BLK, 2...  10.9 us
    pallas_call x1, Pallas kernels, local(): pl.pallas_call(forward_body, out_shape=(parcel, shape(SLOTS, BLK, 2 * BLK...  10 us
    all_to_all x4, waiting for transfers between devices, spread(): lax.all_to_all(jnp.broadcast_to(x[None], (n,) + x.shape), axis, 0, 0, til...  9.86 us
    unnamed x43, local copies, waits for them, and re-layouts  8.55 us
  transfers between devices with their start and end apart: 17, of which 8 were waited for; matrix products, arithmetic and copies ran while one was open for 9% of the time, Pallas kernels for 27%

profile of v6, /device:TPU:64, one launch (start us, length us, event | category | flops | bytes accessed | tf_op | source)
XLA Modules:
  0.0 200.0 jit_solution(822142504897102956)
XLA Ops:
  15.1 8.1 %all-to-all-start = ((bf16[4,1,224,128]{3,2,1,0:T(8,128)(2,1)}), bf16[4,1,224,128]{3,2,1,0:T(8,128)(2,1)S(1)}, u32[]{:S(2)}, u32[]{:S(2)}) async-start(bf16[4,1,224,128]{3,2,1,0:T(8,128)(2,1)} %broadcast_in_dim.181), calls=%async_computation | async-start | bytes 458752 | tf_op jit(solution)/shard_map/all_to_all | solution.py:488
  23.2 4.1 %copy.60 = bf16[128,8192]{0,1:T(8,128)(2,1)} copy(bf16[128,8192]{1,0:T(8,128)(2,1)} %tok_far.1) | data formatting | bytes 4194304 | tf_op args[0]
  33.1 5.0 %all-to-all-start.1 = ((bf16[4,4,224,128]{3,2,1,0:T(8,128)(2,1)}), bf16[4,4,224,128]{3,2,1,0:T(8,128)(2,1)S(1)}, u32[]{:S(2)}, u32[]{:S(2)}) async-start(bf16[4,4,224,128]{3,2,1,0:T(8,128)(2,1)} %broadcast_in_dim.182), calls=%async_computation.1 | async-start | bytes 1835008 | tf_op jit(solution)/shard_map/all_to_all | solution.py:488
  40.9 9.2 %all-to-all-done.1 = bf16[4,4,224,128]{3,2,1,0:T(8,128)(2,1)S(1)} async-done(((bf16[4,4,224,128]{3,2,1,0:T(8,128)(2,1)}), bf16[4,4,224,128]{3,2,1,0:T(8,128)(2,1)S(1)}, u32[]{:S(2)}, u32[]{:S(2)}) %all-to-all-start.1) | async-done | bytes 917536 | tf_op jit(solution)/shard_map/all_to_all | solution.py:488
  50.3 6.1 %all_to_all.45 = bf16[2,16,224,128]{3,2,1,0:T(8,128)(2,1)} all-to-all(bf16[2,16,224,128]{3,2,1,0:T(8,128)(2,1)S(1)} %broadcast_in_dim.200), channel_id=1, replica_groups=mesh['zh'=4,'x'=4,'core'=2,'y'=4,'zl'=2] {'core'}, dimensions={0} | all-to-all | bytes 3670016 | tf_op jit(solution)/shard_map/all_to_all | solution.py:488
  56.4 6.7 %shard_map.216 = (bf16[8,512,128]{2,1,0:T(8,128)(2,1)}, bf16[43,128,128]{2,1,0:T(8,128)(2,1)}, bf16[14,64,128]{2,1,0:T(8,128)(2,1)}, bf16[512,128]{1,0:T(8,128)(2,1)}) custom-call(s32[560]{0:T(1024)} %concatenate.21.meta, bf16[32,224,128]{2,1,0:T(8,128)(2,1)} %bitcast.40, bf16[128,8192]{1,0:T(8,128)(2,1)} %cot.5, bf16[512,512]{1,0:T(8,128)(2,1)} %get-tuple-element.214.perm, ...), custom_call_target="tpu_custom_call" | custom-call | tf_op jit(solution)/shard_map/pallas_call | solution.py:54
  63.1 5.0 %all-to-all-start.3 = ((bf16[8,512,128]{2,1,0:T(8,128)(2,1)}), bf16[8,512,128]{2,1,0:T(8,128)(2,1)S(1)}, u32[]{:S(2)}, u32[]{:S(2)}) async-start(bf16[8,512,128]{2,1,0:T(8,128)(2,1)} %get-tuple-element.94), calls=%async_computation.3 | async-start | bytes 2097152 | tf_op jit(solution)/shard_map/all_to_all | solution.py:551
  68.1 5.7 %all-gather.2.cloned.1.call-done.got_far = bf16[32,528,128]{2,1,0:T(8,128)(2,1)} async-done(((bf16[1,528,128]{2,1,0:T(8,128)(2,1)}), bf16[32,528,128]{2,1,0:T(8,128)(2,1)}) %all-gather.2.cloned.1.call-update) | async-done | bytes 4325392 | tf_op jit(solution)/shard_map/all_gather | solution.py:527
  73.8 10.0 %shard_map.217 = (bf16[8,2,128,128]{3,2,1,0:T(8,128)(2,1)}, f32[14,128,256]{2,1,0:T(8,128)}, bf16[43,128,256]{2,1,0:T(8,128)(2,1)}, bf16[14,128,128]{2,1,0:T(8,1...) custom-call(s32[560]{0:T(1024)} %concatenate.21.meta, ...), custom_call_target="tpu_custom_call" | custom-call | tf_op jit(solution)/shard_map/pallas_call | solution.py:557
  85.2 3.5 %all-to-all-start.4 = ((bf16[8,2,128,128]{3,2,1,0:T(8,128)(2,1)}), bf16[8,2,128,128]{3,2,1,0:T(8,128)(2,1)S(1)}, u32[]{:S(2)}, u32[]{:S(2)}) async-start(bf16[8,2,128,128]{3,2,1,0:T(8,128)(2,1)} %get-tuple-element.103), calls=%async_computation.4 | async-start | bytes 1048576 | tf_op jit(solution)/shard_map/all_to_all | solution.py:572
  88.9 10.9 %shard_map.218 = (bf16[32,608,128]{2,1,0:T(8,128)(2,1)}, bf16[14,128,256]{2,1,0:T(8,128)(2,1)}, f32[128,64]{1,0:T(8,128)}, bf16[128,64]{1,0:T(8,128)(2,1)}) custom-call(s32[560]{0:T(1024)} %concatenate.21.meta, bf16[8,512,128]{2,1,0:T(8,128)(2,1)} %copy-done, f32[14,128,256]{2,1,0:T(8,128)} %get-tuple-element.97.act, ...), custom_call_target="tpu_custom_call" | custom-call | tf_op jit(solution)/shard_map/pallas_call | solution.py:575
  100.7 6.4 %shard_map.219 = (bf16[32,608,128]{2,1,0:T(8,128)(2,1)}, bf16[14,128,128]{2,1,0:T(8,128)(2,1)}, f32[128,64]{1,0:T(8,128)}) custom-call(s32[560]{0:T(1024)} %concatenate.21.meta, bf16[8,2,128,128]{3,2,1,0:T(8,128)(2,1)} %copy-done.2, bf16[14,64,128]{2,1,0:T(8,128)(2,1)} %get-tuple-element.104.dlin, ...), custom_call_target="tpu_custom_call", output_to_operand_aliasing={{0}: (7, {})} | custom-call | tf_op jit(solution)/shard_map/pallas_call | solution.py:587
  108.8 5.4 %all-to-all-start.5 = ((bf16[8,128,128]{2,1,0:T(8,128)(2,1)}), bf16[8,128,128]{2,1,0:T(8,128)(2,1)S(1)}, u32[]{:S(2)}, u32[]{:S(2)}) async-start(bf16[8,128,128]{2,1,0:T(8,128)(2,1)} %broadcast_in_dim.201), calls=%async_computation.5 | async-start | bytes 524288 | tf_op jit(solution)/shard_map/all_to_all | solution.py:488
  114.2 4.6 %shard_map.220 = (bf16[4,8,128,128]{3,2,1,0:T(8,128)(2,1)}, bf16[4,8,128,128]{3,2,1,0:T(8,128)(2,1)}) custom-call(s32[560]{0:T(1024)} %concatenate.21.meta, bf16[14,128,256]{2,1,0:T(8,128)(2,1)} %get-tuple-element.109.gu, bf16[43,128,256]{2,1,0:T(8,128)(2,1)} %get-tuple-element.110.w_gu), custom_call_target="tpu_custom_call" | custom-call | tf_op jit(solution)/shard_map/pallas_call | solution.py:54
  118.8 3.8 %shard_map.221 = (bf16[2,8,128,128]{3,2,1,0:T(8,128)(2,1)}, bf16[2,8,128,128]{3,2,1,0:T(8,128)(2,1)}, bf16[2,8,128,128]{3,2,1,0:T(8,128)(2,1)}, bf16[2,8,128,128]{3,2,1,0:T(8,128)(2,1)}) custom-call(s32[560]{0:T(1024)} %concatenate.21.meta, bf16[14,128,128]{2,1,0:T(8,128)(2,1)} %get-tuple-element.113.hd, bf16[43,128,128]{2,1,0:T(8,128)(2,1)} %get-tuple-element.114.w_d), custom_call_target="tpu_custom_call" | custom-call | tf_op jit(solution)/shard_map/pallas_call | solution.py:54
  126.1 2.7 %collective-permute-start.2 = (bf16[2,8,128,128]{3,2,1,0:T(8,128)(2,1)}, bf16[2,8,128,128]{3,2,1,0:T(8,128)(2,1)S(1)}, u32[]{:S(2)}, u32[]{:S(2)}) collective-permute-start(bf16[2,8,128,128]{3,2,1,0:T(8,128)(2,1)} %get-tuple-element.125), channel_id=1, source_target_pairs={{0,4},{2,6},{4,0},{6,2},{1,5},{3,7},{5,1},{7,3},{8,12},{10,14},{12... | collective-permute-start | bytes 1572872 | tf_op jit(solution)/shard_map/ppermute | solution.py:502
  130.2 3.7 %shard_map.222 = (bf16[2,128,64]{2,1,0:T(8,128)(2,1)}, bf16[32,32,128]{2,1,0:T(8,128)(2,1)}) custom-call(s32[560]{0:T(1024)} %concatenate.21.meta, bf16[8,128,128]{2,1,0:T(8,128)(2,1)} %copy-done.3, bf16[64,128,128]{2,1,0:T(8,128)(2,1)} %bitcast.39, bf16[128,8192]{1,0:T(8,128)(2,1)} %cot.5, bf16[512,512]{1,0:T(8,128)(2,1)} %fusion.2.perm2), custom_call_target="tpu_custom_call" | custom-call | tf_op jit(solution)/shard_map/pallas_call | solution.py:54
  134.0 14.2 %all_to_all.46 = bf16[8,128,128]{2,1,0:T(8,128)(2,1)S(1)} all-to-all(bf16[8,128,128]{2,1,0:T(8,128)(2,1)} %bitcast.46), channel_id=1, replica_groups=mesh['zh'=4,'x'=4,'core'=2,'y'=4,'zl'=2] {'x','core'}, dimensions={0} | all-to-all | bytes 524288 | tf_op jit(solution)/shard_map/all_to_all | solution.py:620
  148.2 2.7 %collective-permute-done.2.refs_2_ = bf16[2,8,128,128]{3,2,1,0:T(8,128)(2,1)S(1)} collective-permute-done((bf16[2,8,128,128]{3,2,1,0:T(8,128)(2,1)}, bf16[2,8,128,128]{3,2,1,0:T(8,128)(2,1)S(1)}, u32[]{:S(2)}, u32[]{:S(2)}) %collective-permute-start.2) | collective-permute-done | bytes 524320 | tf_op jit(solution)/shard_map/ppermute | solution.py:502
  154.6 6.8 %all-to-all-start.7 = ((bf16[4,640,128]{2,1,0:T(8,128)(2,1)}), bf16[4,640,128]{2,1,0:T(8,128)(2,1)S(1)}, u32[]{:S(2)}, u32[]{:S(2)}) async-start(bf16[4,640,128]{2,1,0:T(8,128)(2,1)} %pad_maximum_fusion), calls=%async_computation.8 | async-start | bytes 1310720 | tf_op jit(solution)/shard_map/all_to_all | solution.py:624
  161.3 2.6 %shard_map.225 = (bf16[8,128,128]{2,1,0:T(8,128)(2,1)}, bf16[8,128,128]{2,1,0:T(8,128)(2,1)}, bf16[8,128,128]{2,1,0:T(8,128)(2,1)}, bf16[8,128,128]{2,1,0:T(8,128)(2,1)}) custom-call(bf16[4,8,128,128]{3,2,1,0:T(8,128)(2,1)} %get-tuple-element.137.keep, bf16[4,8,128,128]{3,2,1,0:T(8,128)(2,1)} %copy-done.4), custom_call_target="tpu_custom_call" | custom-call | tf_op jit(solution)/shard_map/pallas_call | solution.py:54
  165.3 4.1 %collective-permute-start.6 = (bf16[8,128,128]{2,1,0:T(8,128)(2,1)}, bf16[8,128,128]{2,1,0:T(8,128)(2,1)S(1)}, u32[]{:S(2)}, u32[]{:S(2)}) collective-permute-start(bf16[8,128,128]{2,1,0:T(8,128)(2,1)} %get-tuple-element.141), channel_id=1, source_target_pairs={{0,4},{2,6},{4,0},{6,2},{1,5},{3,7},{5,1},{7,3},{8,12},{10,14},{12... | collective-permute-start | bytes 786440 | tf_op jit(solution)/shard_map/ppermute | solution.py:502
  175.1 2.8 %collective-permute-done.6.refs_2_ = bf16[8,128,128]{2,1,0:T(8,128)(2,1)S(1)} collective-permute-done((bf16[8,128,128]{2,1,0:T(8,128)(2,1)}, bf16[8,128,128]{2,1,0:T(8,128)(2,1)S(1)}, u32[]{:S(2)}, u32[]{:S(2)}) %collective-permute-start.6) | collective-permute-done | bytes 262176 | tf_op jit(solution)/shard_map/ppermute | solution.py:502
  182.3 3.6 %all-to-all-start.8 = ((bf16[8,16,128]{2,1,0:T(8,128)(2,1)}), bf16[8,16,128]{2,1,0:T(8,128)(2,1)S(1)}, u32[]{:S(2)}, u32[]{:S(2)}) async-start(bf16[8,16,128]{2,1,0:T(8,128)(2,1)} %broadcast_in_dim.202), calls=%async_computation.9 | async-start | bytes 65536 | tf_op jit(solution)/shard_map/all_to_all | solution.py:488
  (143 shorter events, 48.0 us)
Async XLA Ops:
  7.2 66.7 %all-gather.2.cloned.1.call-start = ((), (), s32[]{:S(2)}) async-start(), calls=%async_computation.10 | async-start | bytes 4460544 | tf_op jit(solution)/shard_map/all_gather | solution.py:527
  15.1 16.4 %all-to-all-start = ((bf16[4,1,224,128]{3,2,1,0:T(8,128)(2,1)}), bf16[4,1,224,128]{3,2,1,0:T(8,128)(2,1)S(1)}, u32[]{:S(2)}, u32[]{:S(2)}) async-start(bf16[4,1,224,128]{3,2,1,0:T(8,128)(2,1)} %broadcast_in_dim.181), calls=%async_computation | async-start | bytes 458752 | tf_op jit(solution)/shard_map/all_to_all | solution.py:488
  29.5 8.7 %copy-start.16 = (s32[112]{0:T(128)S(1)}, s32[112]{0:T(128)}, u32[]{:S(2)}) copy-start(s32[112]{0:T(128)} %param.25) | copy-start | bytes 1348
  29.5 9.7 %copy-start.14 = (s32[112,5]{0,1:T(8,128)S(1)}, s32[112,5]{0,1:T(8,128)}, u32[]{:S(2)}) copy-start(s32[112,5]{0,1:T(8,128)} %param.27) | copy-start | bytes 6724
  29.5 9.7 %copy-start.15 = (s32[112,5]{0,1:T(8,128)S(1)}, s32[112,5]{0,1:T(8,128)}, u32[]{:S(2)}) copy-start(s32[112,5]{0,1:T(8,128)} %param.26) | copy-start | bytes 6724
  33.1 17.0 %all-to-all-start.1 = ((bf16[4,4,224,128]{3,2,1,0:T(8,128)(2,1)}), bf16[4,4,224,128]{3,2,1,0:T(8,128)(2,1)S(1)}, u32[]{:S(2)}, u32[]{:S(2)}) async-start(bf16[4,4,224,128]{3,2,1,0:T(8,128)(2,1)} %broadcast_in_dim.182), calls=%async_computation.1 | async-start | bytes 1835008 | tf_op jit(solution)/shard_map/all_to_all | solution.py:488
  63.1 22.1 %all-to-all-start.3 = ((bf16[8,512,128]{2,1,0:T(8,128)(2,1)}), bf16[8,512,128]{2,1,0:T(8,128)(2,1)S(1)}, u32[]{:S(2)}, u32[]{:S(2)}) async-start(bf16[8,512,128]{2,1,0:T(8,128)(2,1)} %get-tuple-element.94), calls=%async_computation.3 | async-start | bytes 2097152 | tf_op jit(solution)/shard_map/all_to_all | solution.py:551
  85.2 14.7 %all-to-all-start.4 = ((bf16[8,2,128,128]{3,2,1,0:T(8,128)(2,1)}), bf16[8,2,128,128]{3,2,1,0:T(8,128)(2,1)S(1)}, u32[]{:S(2)}, u32[]{:S(2)}) async-start(bf16[8,2,128,128]{3,2,1,0:T(8,128)(2,1)} %get-tuple-element.103), calls=%async_computation.4 | async-start | bytes 1048576 | tf_op jit(solution)/shard_map/all_to_all | solution.py:572
  88.7 63.9 %reduce-scatter.2.cloned.1.call-start = ((), (), s32[]{:S(2)}) async-start(), calls=%async_computation.11 | async-start | bytes 5603328 | tf_op jit(solution)/shard_map/reduce_scatter | solution.py:599
  108.8 13.8 %all-to-all-start.5 = ((bf16[8,128,128]{2,1,0:T(8,128)(2,1)}), bf16[8,128,128]{2,1,0:T(8,128)(2,1)S(1)}, u32[]{:S(2)}, u32[]{:S(2)}) async-start(bf16[8,128,128]{2,1,0:T(8,128)(2,1)} %broadcast_in_dim.201), calls=%async_computation.5 | async-start | bytes 524288 | tf_op jit(solution)/shard_map/all_to_all | solution.py:488
  122.6 28.3 %collective-permute-start = (bf16[4,8,128,128]{3,2,1,0:T(8,128)(2,1)}, bf16[4,8,128,128]{3,2,1,0:T(8,128)(2,1)S(1)}, u32[]{:S(2)}, u32[]{:S(2)}) collective-permute-start(bf16[4,8,128,128]{3,2,1,0:T(8,128)(2,1)} %get-tuple-element.122), channel_id=1, source_target_pairs={{0,1},{1,0},{2,3},{3,2},{4,5},{5,4},{6,7},{7,6},{8,9},{9,8},{10,11... | collective-permute-start | bytes 3145736 | tf_op jit(solution)/shard_map/ppermute | solution.py:618
  124.6 23.6 %collective-permute-start.1 = (bf16[2,8,128,128]{3,2,1,0:T(8,128)(2,1)}, bf16[2,8,128,128]{3,2,1,0:T(8,128)(2,1)S(1)}, u32[]{:S(2)}, u32[]{:S(2)}) collective-permute-start(bf16[2,8,128,128]{3,2,1,0:T(8,128)(2,1)} %get-tuple-element.124), channel_id=1, source_target_pairs={{0,2},{2,4},{4,6},{6,0},{1,3},{3,5},{5,7},{7,1},{8,10},{10,12},{12... | collective-permute-start | bytes 1572872 | tf_op jit(solution)/shard_map/ppermute | solution.py:502
  126.1 24.9 %collective-permute-start.2 = (bf16[2,8,128,128]{3,2,1,0:T(8,128)(2,1)}, bf16[2,8,128,128]{3,2,1,0:T(8,128)(2,1)S(1)}, u32[]{:S(2)}, u32[]{:S(2)}) collective-permute-start(bf16[2,8,128,128]{3,2,1,0:T(8,128)(2,1)} %get-tuple-element.125), channel_id=1, source_target_pairs={{0,4},{2,6},{4,0},{6,2},{1,5},{3,7},{5,1},{7,3},{8,12},{10,14},{12... | collective-permute-start | bytes 1572872 | tf_op jit(solution)/shard_map/ppermute | solution.py:502
  128.8 22.2 %collective-permute-start.3 = (bf16[2,8,128,128]{3,2,1,0:T(8,128)(2,1)}, bf16[2,8,128,128]{3,2,1,0:T(8,128)(2,1)S(1)}, u32[]{:S(2)}, u32[]{:S(2)}) collective-permute-start(bf16[2,8,128,128]{3,2,1,0:T(8,128)(2,1)} %get-tuple-element.126), channel_id=1, source_target_pairs={{0,6},{2,0},{4,2},{6,4},{1,7},{3,1},{5,3},{7,5},{8,14},{10,8},{12,... | collective-permute-start | bytes 1572872 | tf_op jit(solution)/shard_map/ppermute | solution.py:502
  148.2 15.7 %copy-start.5 = (bf16[2,8,128,128]{3,2,1,0:T(8,128)(2,1)}, bf16[2,8,128,128]{3,2,1,0:T(8,128)(2,1)S(1)}, u32[]{:S(2)}) copy-start(bf16[2,8,128,128]{3,2,1,0:T(8,128)(2,1)S(1)} %collective-permute-done.1.refs_1_) | copy-start | bytes 1572868
  150.9 12.9 %copy-start.6 = (bf16[2,8,128,128]{3,2,1,0:T(8,128)(2,1)}, bf16[2,8,128,128]{3,2,1,0:T(8,128)(2,1)S(1)}, u32[]{:S(2)}) copy-start(bf16[2,8,128,128]{3,2,1,0:T(8,128)(2,1)S(1)} %collective-permute-done.2.refs_2_) | copy-start | bytes 1572868
  150.9 12.9 %copy-start.7 = (bf16[2,8,128,128]{3,2,1,0:T(8,128)(2,1)}, bf16[2,8,128,128]{3,2,1,0:T(8,128)(2,1)S(1)}, u32[]{:S(2)}) copy-start(bf16[2,8,128,128]{3,2,1,0:T(8,128)(2,1)S(1)} %collective-permute-done.3.refs_3_) | copy-start | bytes 1572868
  151.0 10.4 %copy-start.4 = (bf16[4,8,128,128]{3,2,1,0:T(8,128)(2,1)}, bf16[4,8,128,128]{3,2,1,0:T(8,128)(2,1)S(1)}, u32[]{:S(2)}) copy-start(bf16[4,8,128,128]{3,2,1,0:T(8,128)(2,1)S(1)} %collective-permute-done.came) | copy-start | bytes 3145732
  154.6 26.5 %all-to-all-start.7 = ((bf16[4,640,128]{2,1,0:T(8,128)(2,1)}), bf16[4,640,128]{2,1,0:T(8,128)(2,1)S(1)}, u32[]{:S(2)}, u32[]{:S(2)}) async-start(bf16[4,640,128]{2,1,0:T(8,128)(2,1)} %pad_maximum_fusion), calls=%async_computation.8 | async-start | bytes 1310720 | tf_op jit(solution)/shard_map/all_to_all | solution.py:624
  163.9 11.3 %collective-permute-start.5 = (bf16[8,128,128]{2,1,0:T(8,128)(2,1)}, bf16[8,128,128]{2,1,0:T(8,128)(2,1)S(1)}, u32[]{:S(2)}, u32[]{:S(2)}) collective-permute-start(bf16[8,128,128]{2,1,0:T(8,128)(2,1)} %get-tuple-element.140), channel_id=1, source_target_pairs={{0,2},{2,4},{4,6},{6,0},{1,3},{3,5},{5,7},{7,1},{8,10},{10,12},{12... | collective-permute-start | bytes 786440 | tf_op jit(solution)/shard_map/ppermute | solution.py:502
  165.3 12.7 %collective-permute-start.6 = (bf16[8,128,128]{2,1,0:T(8,128)(2,1)}, bf16[8,128,128]{2,1,0:T(8,128)(2,1)S(1)}, u32[]{:S(2)}, u32[]{:S(2)}) collective-permute-start(bf16[8,128,128]{2,1,0:T(8,128)(2,1)} %get-tuple-element.141), channel_id=1, source_target_pairs={{0,4},{2,6},{4,0},{6,2},{1,5},{3,7},{5,1},{7,3},{8,12},{10,14},{12... | collective-permute-start | bytes 786440 | tf_op jit(solution)/shard_map/ppermute | solution.py:502
  169.3 8.6 %collective-permute-start.7 = (bf16[8,128,128]{2,1,0:T(8,128)(2,1)}, bf16[8,128,128]{2,1,0:T(8,128)(2,1)S(1)}, u32[]{:S(2)}, u32[]{:S(2)}) collective-permute-start(bf16[8,128,128]{2,1,0:T(8,128)(2,1)} %get-tuple-element.142), channel_id=1, source_target_pairs={{0,6},{2,0},{4,2},{6,4},{1,7},{3,1},{5,3},{7,5},{8,14},{10,8},{12,... | collective-permute-start | bytes 786440 | tf_op jit(solution)/shard_map/ppermute | solution.py:502
  172.8 13.2 %collective-permute-start.4 = (bf16[8,128,128]{2,1,0:T(8,128)(2,1)}, bf16[8,128,128]{2,1,0:T(8,128)(2,1)S(1)}, u32[]{:S(2)}, u32[]{:S(2)}) collective-permute-start(bf16[8,128,128]{2,1,0:T(8,128)(2,1)} %get-tuple-element.132), channel_id=1, source_target_pairs={{0,1},{1,0},{2,3},{3,2},{4,5},{5,4},{6,7},{7,6},{8,9},{9,8},{10,11... | collective-permute-start | bytes 786440 | tf_op jit(solution)/shard_map/ppermute | solution.py:628
  182.3 10.1 %all-to-all-start.8 = ((bf16[8,16,128]{2,1,0:T(8,128)(2,1)}), bf16[8,16,128]{2,1,0:T(8,128)(2,1)S(1)}, u32[]{:S(2)}, u32[]{:S(2)}) async-start(bf16[8,16,128]{2,1,0:T(8,128)(2,1)} %broadcast_in_dim.202), calls=%async_computation.9 | async-start | bytes 65536 | tf_op jit(solution)/shard_map/all_to_all | solution.py:488
  (13 other events, 39.3 us)
Sparse Core Ops, SparseCore 0:
  11.2 62.6 all-gather.1
  107.2 45.3 reduce-scatter.1
